TPU v7x, 256 devices: a whole 4x4x8 slice. The times are simulated.
256 devices in a mesh: lag: 16 (over z, x_hi), col: 16 (over y, x_lo, core).
Axes of the slice: x: 4 (x_hi: 2, x_lo: 2; x = x_hi * 2 + x_lo), y: 4, z: 8, core: 2. Of those that a mesh axis runs over, the one named last changes fastest.
Arguments:
- blocks: bfloat16 [16, 512, 8, 128, 128], P('lag', 'col'), may hold values from -0.046875 to 0.046875
- offsets: int32 [16, 512, 8], P('lag', 'col'), may hold values from -24 to 24
- history: bfloat16 [16, 512, 16, 128], P('lag', 'col'), may hold values from -6 to 6
- instant_inverse: float32 [512, 128, 128], P('col'), may hold values from -0.5 to 0.5
- incident: float32 [2, 512, 16, 256], P(None, 'col', 'lag'), may hold values from -6 to 6
- element_map: int32 [512, 256], P('col'), may hold values from 0 to 127
Outputs:
- currents: bfloat16 [2, 512, 16, 128], P(None, 'col', 'lag')
- history_out: bfloat16 [16, 512, 16, 128], P('lag', 'col')
All inputs are finite; a program needn't handle non-finite values.
Results may differ from a plain program's by a relative error of at most 0.015.
Values may be sent and summed in bfloat16 or wider, within the bound.
No kernel may reach another device: no remote copies, remote signals or barrier semaphores. Data moves between devices by JAX's collectives and lax.ppermute only.
A program may use at most 64 MiB of HBM per device.

v0:
```python
import jax
import jax.numpy as jnp
from jax import lax
from jax.sharding import PartitionSpec as P

STEPS = 2


def passed_along(block, axis, distance):
    devices = range(lax.axis_size(axis))
    route = [(i - distance, i) for i in devices if i - distance in devices]
    return lax.ppermute(block, axis, route)


def body(blocks, offsets, history, instant_inverse, incident, element_map):
    col_count = lax.axis_size("col")
    col_index = lax.axis_index("col")
    lag_index = lax.axis_index("lag")
    block_cols = blocks.shape[1]
    block_size = blocks.shape[3]
    pulses = history.shape[2]
    total_blocks = block_cols * col_count
    first = col_index * block_cols
    columns = first + jnp.arange(block_cols, dtype=jnp.int32)
    rows = jnp.clip(columns[None, :, None] + offsets, 0, total_blocks - 1)
    local_rows = rows.reshape(-1) - (first - block_cols)
    load = (
        element_map[:, :, None] == jnp.arange(block_size, dtype=jnp.int32)[None, None, :]
    ).astype(jnp.float32)
    outs = []
    for step in range(STEPS):
        aged = passed_along(history[-1], "lag", 1)
        prod = jnp.einsum("sckij,scpj->sckpi", blocks, history, preferred_element_type=jnp.float32)
        terms = prod.reshape(-1, pulses, block_size)
        window = (
            jnp.zeros((3 * block_cols, pulses, block_size), jnp.float32).at[local_rows].add(terms)
        )
        from_below = passed_along(window[2 * block_cols :].astype(jnp.bfloat16), "col", 1).astype(
            jnp.float32
        )
        from_above = passed_along(window[:block_cols].astype(jnp.bfloat16), "col", -1).astype(
            jnp.float32
        )
        mine = window[block_cols : 2 * block_cols] + from_below + from_above
        owned = lax.psum_scatter(
            mine.astype(jnp.bfloat16), "lag", scatter_dimension=1, tiled=True
        ).astype(jnp.float32)
        source = jnp.einsum("bpe,bei->bpi", incident[step], load, precision=lax.Precision.HIGHEST)
        current = jnp.einsum(
            "bij,bpj->bpi", instant_inverse, source - owned, precision=lax.Precision.HIGHEST
        ).astype(jnp.bfloat16)
        outs.append(current)
        newest = lax.all_gather(current, "lag", axis=1, tiled=True)
        head = jnp.where(lag_index == 0, newest, aged)
        history = jnp.concatenate([head[None], history[:-1]], axis=0)
    return (jnp.stack(outs), history)


def solution(mesh):
    placed = (
        P("lag", "col", None, None, None),
        P("lag", "col", None),
        P("lag", "col", None, None),
        P("col", None, None),
        P(None, "col", "lag", None),
        P("col", None),
    )
    return jax.shard_map(
        body,
        mesh=mesh,
        in_specs=placed,
        out_specs=(P(None, "col", "lag", None), P("lag", "col", None, None)),
        check_vma=False,
    )
```

profile of v0, /device:TPU:4, one launch (start us, length us, event | category | flops | bytes accessed | tf_op | source)
XLA Modules:
  0.0 578.3 jit_solution(12101879359398112784)
XLA Ops:
  7.2 0.8 clamp_subtract_fusion
  8.1 0.1 copy.9
  8.2 0.1 sub.28
  8.3 7.1 %fusion.2 = f32[32,16,8,128]{3,1,2,0:T(8,128)} fusion(bf16[1,32,8,128,128]{4,3,2,1,0:T(8,128)(2,1)} %param.6, bf16[1,32,16,128]{3,2,1,0:T(8,128)(2,1)} %param.8), kind=kOutput, calls=%fused_computation.4 | convolution fusion | flops 134217728 | bytes 10616832 | tf_op jit(solution)/shard_map/sckij,scpj->sckpi/dot_general | solution.py:33
  15.4 20.4 %scatter_fusion = f32[96,16,128]{2,1,0:T(8,128)S(1)} fusion(f32[96,16,128]{2,1,0:T(8,128)S(1)} %broadcast.38.clone, s32[256]{0:T(256)S(1)} %bitcast.80, f32[256,16,128]{2,1,0:T(8,128)} %bitcast.67), kind=kCustom, calls=%fused_computation | custom fusion | flops 524288 | bytes 6292480 | tf_op jit(solution)/shard_map/scatter-add | solution.py:36
  35.9 0.1 convert.8
  35.9 1.7 collective-permute-start
  37.6 1.3 collective-permute-start.1
  38.9 2.9 collective-permute-done.1
  41.8 0.1 fusion.11
  41.9 0.7 copy.10
  42.6 4.1 collective-permute-start.2
  46.8 2.4 fusion.5
  49.1 199.3 %reduce-scatter.3.cloned.1.call-done = bf16[32,1,128]{2,0,1:T(8,128)(2,1)} async-done(((bf16[32,16,128]{2,0,1:T(8,128)(2,1)}), bf16[32,1,128]{2,0,1:T(8,128)(2,1)}) %reduce-scatter.3.cloned.1.call-update) | async-done | bytes 8208 | tf_op jit(solution)/shard_map/reduce_scatter | solution.py:45
  248.4 0.7 convert_subtract_fusion.1
  249.1 3.3 fusion.20
  252.5 38.0 %all-gather = bf16[32,2048]{1,0:T(8,128)(2,1)S(1)} all-gather(bf16[32,128]{1,0:T(8,128)(2,1)S(1)} %convert_element_type.45), channel_id=2, replica_groups=mesh['lag'=16,'col'=16] {'lag'}, dimensions={1}, use_global_device_ids=true | all-gather | bytes 139264 | tf_op jit(solution)/shard_map/all_gather | solution.py:53
  290.5 7.0 %fusion = f32[32,16,8,128]{3,1,2,0:T(8,128)} fusion(bf16[1,32,8,128,128]{4,3,2,1,0:T(8,128)(2,1)} %param.6, bf16[32,16,128]{2,1,0:T(8,128)(2,1)S(1)} %bitcast_select_fusion.1), kind=kOutput, calls=%fused_computation.2 | convolution fusion | flops 134217728 | bytes 10616832 | tf_op jit(solution)/shard_map/sckij,scpj->sckpi/dot_general | solution.py:33
  297.6 20.4 %scatter_fusion.1 = f32[96,16,128]{2,1,0:T(8,128)S(1)} fusion(f32[96,16,128]{2,1,0:T(8,128)S(1)} %broadcast.38, s32[256]{0:T(256)S(1)} %bitcast.81, f32[256,16,128]{2,1,0:T(8,128)} %bitcast.66), kind=kCustom, calls=%fused_computation.1 | custom fusion | flops 524288 | bytes 6292480 | tf_op jit(solution)/shard_map/scatter-add | solution.py:36
  318.0 0.1 convert.9
  318.1 1.3 collective-permute-start.3
  319.4 1.3 collective-permute-start.4
  320.7 3.2 collective-permute-done.4
  324.0 0.7 copy.11
  324.7 2.4 fusion.4
  327.1 2.8 collective-permute-start.5
  329.9 198.2 %reduce-scatter.5.cloned.1.call-done = bf16[32,1,128]{2,0,1:T(8,128)(2,1)} async-done(((bf16[32,16,128]{2,0,1:T(8,128)(2,1)}), bf16[32,1,128]{2,0,1:T(8,128)(2,1)}) %reduce-scatter.5.cloned.1.call-update) | async-done | bytes 8208 | tf_op jit(solution)/shard_map/reduce_scatter | solution.py:45
  528.1 0.7 convert_subtract_fusion
  528.8 3.3 fusion.21
  532.2 38.0 %all-gather.1 = bf16[32,2048]{1,0:T(8,128)(2,1)S(1)} all-gather(bf16[32,128]{1,0:T(8,128)(2,1)S(1)} %convert_element_type.51), channel_id=3, replica_groups=mesh['lag'=16,'col'=16] {'lag'}, dimensions={1}, use_global_device_ids=true | all-gather | bytes 139264 | tf_op jit(solution)/shard_map/all_gather | solution.py:53
  570.2 0.6 pad_maximum_fusion
  570.8 0.7 bitcast_select_fusion
  (30 shorter events, 0.4 us)
Async XLA Ops:
  7.2 242.0 %copy-start = (f32[32,128,128]{2,1,0:T(8,128)S(1)}, f32[32,128,128]{2,1,0:T(8,128)}, u32[]{:S(2)}) copy-start(f32[32,128,128]{2,1,0:T(8,128)} %param.9) | copy-start | bytes 6291460
  7.2 241.3 %reduce-scatter.3.cloned.1.call-start = ((), (), s32[]{:S(2)}) async-start(), calls=%async_computation.2 | async-start | bytes 139264 | tf_op jit(solution)/shard_map/reduce_scatter | solution.py:45
  35.8 6.8 %copy-start.1 = (bf16[1,32,16,128]{3,2,1,0:T(8,128)(2,1)S(1)}, bf16[1,32,16,128]{3,2,1,0:T(8,128)(2,1)}, u32[]{:S(2)}) copy-start(bf16[1,32,16,128]{3,2,1,0:T(8,128)(2,1)} %param.8) | copy-start | bytes 393220
  35.8 10.9 %copy-start.2 = (f32[2,32,1,256]{3,2,1,0:T(1,128)S(1)}, f32[2,32,1,256]{3,2,1,0:T(1,128)}, u32[]{:S(2)}) copy-start(f32[2,32,1,256]{3,2,1,0:T(1,128)} %param.10) | copy-start | bytes 196612
  35.8 10.9 %copy-start.3 = (s32[32,256]{1,0:T(8,128)S(1)}, s32[32,256]{1,0:T(8,128)}, u32[]{:S(2)}) copy-start(s32[32,256]{1,0:T(8,128)} %param.11) | copy-start | bytes 98308
  35.9 3.0 collective-permute-start
  37.6 4.2 collective-permute-start.1
  42.6 485.5 %reduce-scatter.5.cloned.1.call-start = ((), (), s32[]{:S(2)}) async-start(), calls=%async_computation.3 | async-start | bytes 139264 | tf_op jit(solution)/shard_map/reduce_scatter | solution.py:45
  42.6 247.9 %collective-permute-start.2 = (bf16[32,16,128]{2,1,0:T(8,128)(2,1)S(1)}, bf16[32,16,128]{2,1,0:T(8,128)(2,1)S(1)}, u32[]{:S(2)}, u32[]{:S(2)}) collective-permute-start(bf16[32,16,128]{2,1,0:T(8,128)(2,1)S(1)} %bitcast.75), channel_id=1, source_target_pairs={{0,16},{16,32},{32,48},{48,64},{64,80},{80,96},{96,112},{112,128},... | collective-permute-start | bytes 393224 | tf_op jit(solution)/shard_map/ppermute | solution.py:12
  318.1 2.6 collective-permute-start.3
  319.4 4.5 collective-permute-start.4
  327.1 243.7 %collective-permute-start.5 = (bf16[32,16,128]{2,1,0:T(8,128)(2,1)S(1)}, bf16[32,16,128]{2,1,0:T(8,128)(2,1)S(1)}, u32[]{:S(2)}, u32[]{:S(2)}) collective-permute-start(bf16[32,16,128]{2,1,0:T(8,128)(2,1)S(1)} %bitcast_select_fusion.1), channel_id=1, source_target_pairs={{0,16},{16,32},{32,48},{48,64},{64,80},{80,96},{96,112},{112,128},... | collective-permute-start | bytes 393224 | tf_op jit(solution)/shard_map/ppermute | solution.py:12
Sparse Core Ops, SparseCore 0:
  42.7 205.6 reduce-scatter.2
  324.8 203.2 reduce-scatter.4
where the time goes:
time: 581 us; the launch traced here: 578 us
  waiting for transfers between devices  404 us (70%)
  blocking collectives  75.9 us (13%)
  other arithmetic  44.6 us (8%)
  matrix products  25.6 us (4%)
  between operations  14.3 us (2%)
  starting transfers between devices  12.5 us (2%)
    reduce_scatter x2, waiting for transfers between devices, body(): lax.psum_scatter(mine.astype(jnp.bfloat16), 'lag', scatter_dimension=1, t...  397 us
    all_gather x2, blocking collectives, body(): newest = lax.all_gather(current, 'lag', axis=1, tiled=True)  75.9 us
    scatter-add x2, other arithmetic, body(): jnp.zeros((3 * block_cols, pulses, block_size), jnp.float32).at[local_rows]  40.8 us
    dot_general x2, matrix products, body(): jnp.einsum('sckij,scpj->sckpi', blocks, history, preferred_element_type=j...  14.1 us
    ppermute x6, starting transfers between devices, passed_along(): return lax.ppermute(block, axis, route)  12.4 us
  transfers between devices with their start and end apart: 8, of which 4 were waited for; matrix products, arithmetic and copies ran while one was open for 2% of the time, Pallas kernels for 0%

commit v1 on v0

v1 whole, which is shorter than its diff:
```python
import functools

import jax
import jax.numpy as jnp
from jax import lax
from jax.experimental import pallas as pl
from jax.experimental.pallas import tpu as pltpu
from jax.sharding import PartitionSpec as P

F32 = jnp.float32
BF16 = jnp.bfloat16
HALF = 24
NT = (((1,), (1,)), ((), ()))
VMEM = pl.BlockSpec(memory_space=pltpu.VMEM)
SMEM = pl.BlockSpec(memory_space=pltpu.SMEM)


def split(x):
    high = x.astype(BF16)
    return high, (x - high.astype(F32)).astype(BF16)


def banded(place_ref, offsets_ref, hist, blocks, window, total_blocks):
    block_cols, width, size, _ = blocks.shape
    first = place_ref[0]
    window[...] = jnp.zeros_like(window)

    def columns(i, carry):
        for j in range(4):
            c = i * 4 + j
            column = blocks[c].reshape(width * size, size)
            prod = lax.dot_general(hist[c], column, NT, preferred_element_type=F32)
            for k in range(width):
                row = jnp.clip(first + c + offsets_ref[k, c], 0, total_blocks - 1) - first + HALF
                window[row] += prod[:, size * k : size * (k + 1)]
        return carry

    lax.fori_loop(0, block_cols // 4, columns, 0)


def hand_out(window, main, up, down):
    n = main.shape[0]
    main[...] = window[HALF : HALF + n]
    up[...] = window[HALF + n :].astype(BF16)
    down[...] = window[:HALF].astype(BF16)


def partial_kernel(total_blocks, place_ref, offsets_ref, hist, blocks, main, up, down, window):
    banded(place_ref, offsets_ref, hist, blocks, window, total_blocks)
    hand_out(window, main, up, down)


def prepare_kernel(incident, element_map, inverse, source, inverse_parts):
    n, size, _ = inverse.shape
    samples = element_map.shape[1]
    unknown = lax.broadcasted_iota(jnp.int32, (size, samples), 0)
    line = lax.broadcasted_iota(jnp.int32, (8, samples), 0)
    for b in range(n):
        load = (unknown == element_map[b : b + 1, :]).astype(F32).astype(BF16)
        rows = jnp.zeros((8, samples), F32)
        for t in range(2):
            sample = jnp.broadcast_to(incident[t, b], (8, samples))
            high = sample.astype(BF16).astype(F32)
            rows = jnp.where(line == 2 * t, high, jnp.where(line == 2 * t + 1, sample - high, rows))
        out = lax.dot_general(rows.astype(BF16), load, NT, preferred_element_type=F32)
        for t in range(2):
            source[t, b : b + 1, :] = out[2 * t : 2 * t + 1] + out[2 * t + 1 : 2 * t + 2]
        high, low = split(inverse[b])
        inverse_parts[b, :, :size] = high
        inverse_parts[b, :, size:] = low


def combine_kernel(place_ref, main, from_below, from_above, source, out):
    n, pulses, size = main.shape
    mine = lax.broadcasted_iota(jnp.int32, (1, pulses, size), 1) == place_ref[1]
    for b in range(n):
        value = main[b]
        if b < HALF:
            value = value + from_below[b].astype(F32)
        if b >= n - HALF:
            value = value + from_above[b - (n - HALF)].astype(F32)
        value = value - jnp.where(mine[0], source[b : b + 1, :], 0.0)
        out[b] = value.astype(BF16)


def solve(rest, inverse_part):
    pulses, size = rest.shape
    high, low = split(-rest)
    lhs = jnp.concatenate(
        [jnp.concatenate([high, high], 1), jnp.concatenate([low, jnp.zeros_like(low)], 1)], 0
    )
    out = lax.dot_general(lhs, inverse_part, NT, preferred_element_type=F32)
    return out[:pulses] + out[pulses:]


def first_step_kernel(
    total_blocks, place_ref, offsets_ref, own, far1, far2, far3, inverse_parts, blocks,
    current, own_pulse, main, up, down, window,
):
    n, pulses, size = own.shape
    mine = lax.broadcasted_iota(jnp.int32, (pulses, size), 0) == place_ref[1]
    for b in range(n):
        rest = sum(part[b].astype(F32) for part in (far1, far2, far3)) + own[b].astype(F32)
        new = solve(rest, inverse_parts[b])
        current[b] = new.astype(BF16)
        own_pulse[b : b + 1, :] = jnp.sum(jnp.where(mine, new, 0.0), axis=0, keepdims=True)
    banded(place_ref, offsets_ref, current, blocks, window, total_blocks)
    hand_out(window, main, up, down)


def second_step_kernel(
    own, far1, far2, far3, main, from_below, from_above, inverse_parts,
    current, by_pulse, scratch,
):
    n, pulses, size = own.shape
    for b in range(n):
        rest = sum(part[b].astype(F32) for part in (far1, far2, far3)) + own[b].astype(F32)
        rest = rest + main[b]
        if b < HALF:
            rest = rest + from_below[b].astype(F32)
        if b >= n - HALF:
            rest = rest + from_above[b - (n - HALF)].astype(F32)
        new = solve(rest, inverse_parts[b])
        current[b] = new.astype(BF16)
        scratch[b * pulses : (b + 1) * pulses, :] = new
    for p in range(pulses):
        by_pulse[p] = scratch[pl.ds(p, n, stride=pulses), :].astype(BF16)


def call(kernel, name, out_shape, in_specs, scratch_shapes=()):
    return pl.pallas_call(
        kernel,
        name=name,
        out_shape=out_shape,
        in_specs=in_specs,
        out_specs=[VMEM] * len(out_shape),
        scratch_shapes=scratch_shapes,
        compiler_params=pltpu.CompilerParams(vmem_limit_bytes=16 * 2**20),
    )


def exchange(block, distance):
    return lax.ppermute(block, "lag", [(i, i ^ distance) for i in range(16)])


def halo(up, down):
    n = lax.axis_size("col")
    from_below = lax.ppermute(up, "col", [(i, i + 1) for i in range(n - 1)])
    from_above = lax.ppermute(down, "col", [(i + 1, i) for i in range(n - 1)])
    return from_below, from_above


def near_sum(block):
    total = block.astype(F32)
    for distance in (1, 2, 3):
        total = total + exchange(block, distance).astype(F32)
    return total.astype(BF16)


def body(blocks, offsets, history, instant_inverse, incident, element_map):
    lag_index = lax.axis_index("lag")
    lags = lax.axis_size("lag")
    n, pulses, size = history.shape[1:]
    width = blocks.shape[2]
    total_blocks = n * lax.axis_size("col")
    place = jnp.stack([lax.axis_index("col") * n, lag_index]).astype(jnp.int32)
    blocks = blocks[0]
    band_rows = offsets[0].T
    shells = history[0]

    def shape(*dims, dtype=F32):
        return jax.ShapeDtypeStruct(dims, dtype)

    window = pltpu.VMEM((n + 2 * HALF, pulses, size), F32)
    partial_out = (
        shape(n, pulses, size),
        shape(HALF, pulses, size, dtype=BF16),
        shape(HALF, pulses, size, dtype=BF16),
    )

    partial = call(
        functools.partial(partial_kernel, total_blocks), "partial",
        partial_out, [SMEM, SMEM, VMEM, VMEM], [window],
    )
    prepare = call(
        prepare_kernel, "prepare",
        (shape(2, n, size), shape(n, size, 2 * size, dtype=BF16)), [VMEM] * 3,
    )
    combine = call(
        combine_kernel, "combine", (shape(n, pulses, size, dtype=BF16),), [SMEM] + [VMEM] * 4,
    )
    first_step = call(
        functools.partial(first_step_kernel, total_blocks), "first_step",
        (shape(n, pulses, size, dtype=BF16), shape(n, size)) + partial_out,
        [SMEM, SMEM] + [VMEM] * 6, [window],
    )
    second_step = call(
        second_step_kernel, "second_step",
        (shape(n, pulses, size, dtype=BF16), shape(pulses, n, size, dtype=BF16)),
        [VMEM] * 8, [pltpu.VMEM((n * pulses, size), F32)],
    )

    with jax.named_scope("shells_step0"):
        main0, up0, down0 = partial(place, band_rows, shells, blocks)
    older = lax.ppermute(shells, "lag", [(i, i + 1) for i in range(lags - 1)])
    oldest = lax.ppermute(shells, "lag", [(i, i + 2) for i in range(lags - 2)])
    with jax.named_scope("halo0"):
        below0, above0 = halo(up0, down0)
    source, inverse_parts = prepare(incident, element_map, instant_inverse)
    (rest0,) = combine(place, main0, below0, above0, source[0])
    with jax.named_scope("near0"):
        near0 = near_sum(rest0)
    with jax.named_scope("shells_step1"):
        main1, up1, down1 = partial(place, band_rows, older, blocks)
    with jax.named_scope("halo1"):
        below1, above1 = halo(up1, down1)
    (rest1,) = combine(place, main1, below1, above1, source[1])
    with jax.named_scope("far0"):
        far0 = [exchange(near0, distance) for distance in (4, 8, 12)]
    with jax.named_scope("near1"):
        near1 = near_sum(rest1)
    with jax.named_scope("far1"):
        far1 = [exchange(near1, distance) for distance in (4, 8, 12)]
    current0, own0, extra, up, down = first_step(
        place, band_rows, near0, *far0, inverse_parts, blocks
    )
    with jax.named_scope("halo_extra"):
        below, above = halo(up, down)
    current1, by_pulse = second_step(near1, *far1, extra, below, above, inverse_parts)
    with jax.named_scope("spread"):
        group = pulses // 4
        parts = [
            lax.ppermute(by_pulse[group * g : group * (g + 1)], "lag", [(0, 4 * g)])
            for g in (1, 2, 3)
        ]
        leader = jnp.where(lag_index == 0, by_pulse[:group], parts[0] + parts[1] + parts[2])
        parts = [
            lax.ppermute(leader[d], "lag", [(4 * g, 4 * g + d) for g in range(4)])
            for d in (1, 2, 3)
        ]
        own1 = jnp.where(lag_index % 4 == 0, leader[0], parts[0] + parts[1] + parts[2])
    currents = jnp.stack([own0.astype(BF16), own1])[:, :, None, :]
    aged = jnp.where(lag_index == 0, current1, jnp.where(lag_index == 1, current0, oldest))
    return currents, aged[None]


def solution(mesh):
    placed = (
        P("lag", "col", None, None, None),
        P("lag", "col", None),
        P("lag", "col", None, None),
        P("col", None, None),
        P(None, "col", "lag", None),
        P("col", None),
    )
    return jax.shard_map(
        body,
        mesh=mesh,
        in_specs=placed,
        out_specs=(P(None, "col", "lag", None), P("lag", "col", None, None)),
        check_vma=False,
    )
```

time: 581 us -> 109 us (0.19)
  the two profiles are of different devices: /device:TPU:4 before, /device:TPU:47 now
where the time goes in v1:
time: 109 us; the launch traced here: 108 us
  starting transfers between devices  64.9 us (60%)
  waiting for transfers between devices  19.3 us (18%)
  Pallas kernels  15.2 us (14%)
  local copies, waits for them, and re-layouts  6.6 us (6%)
  other arithmetic  1.54 us (1%)
    ppermute x12, starting transfers between devices, exchange(): return lax.ppermute(block, 'lag', [(i, i ^ distance) for i in range(16)])  24.3 us
    ppermute x3, starting transfers between devices, halo(): from_below = lax.ppermute(up, 'col', [(i, i + 1) for i in range(n - 1)])  24 us
    ppermute x3, waiting for transfers between devices, body(): lax.ppermute(leader[d], 'lag', [(4 * g, 4 * g + d) for g in range(4)])  11.4 us
    unnamed x18, local copies, waits for them, and re-layouts  6.58 us
    ppermute x3, starting transfers between devices, halo(): from_above = lax.ppermute(down, 'col', [(i + 1, i) for i in range(n - 1)])  5.76 us
    ppermute x3, waiting for transfers between devices, halo(): from_above = lax.ppermute(down, 'col', [(i + 1, i) for i in range(n - 1)])  5.71 us
    pallas_call x1, Pallas kernels, body(): first_step(place, band_rows, near0, *far0, inverse_parts, blocks)  4.6 us
    ppermute x1, starting transfers between devices, body(): older = lax.ppermute(shells, 'lag', [(i, i + 1) for i in range(lags - 1)])  4.39 us
  transfers between devices with their start and end apart: 26, of which 6 were waited for; matrix products, arithmetic and copies ran while one was open for 1% of the time, Pallas kernels for 14%

profile of v1, /device:TPU:47, one launch (start us, length us, event | category | flops | bytes accessed | tf_op | source)
XLA Modules:
  0.0 108.5 jit_solution(13849754289443969675)
XLA Ops:
  0.6 4.4 %collective-permute-start.8 = (bf16[32,16,128]{2,1,0:T(8,128)(2,1)}, bf16[32,16,128]{2,1,0:T(8,128)(2,1)S(1)}, u32[]{:S(2)}, u32[]{:S(2)}) collective-permute-start(bf16[32,16,128]{2,1,0:T(8,128)(2,1)} %bitcast.36), channel_id=1, source_target_pairs={{0,16},{16,32},{32,48},{48,64},{64,80},{80,96},{96,112},{112,128},... | collective-permute-start | bytes 393224 | tf_op jit(solution)/shard_map/ppermute | solution.py:205
  5.1 3.4 %copy-done = bf16[1,32,8,128,128]{4,3,2,1,0:T(8,128)(2,1)S(1)} copy-done((bf16[1,32,8,128,128]{4,3,2,1,0:T(8,128)(2,1)S(1)}, bf16[1,32,8,128,128]{4,3,2,1,0:T(8,128)(2,1)}, u32[]{:S(2)}) %copy-start) | copy-done | bytes 8388632
  8.5 0.9 copy-done.3
  9.4 0.7 copy-done.6
  10.1 3.9 %partial.2 = (f32[32,16,128]{2,1,0:T(8,128)S(1)}, bf16[24,16,128]{2,1,0:T(8,128)(2,1)S(1)}, bf16[24,16,128]{2,1,0:T(8,128)(2,1)S(1)}) custom-call(s32[2]{0:T(128)S(1)} %pad_add_fusion.place_ref, s32[8,32]{1,0:T(8,128)S(1)} %bitcast.39, bf16[32,16,128]{2,1,0:T(8,128)(2,1)S(1)} %bitcast.37, bf16[32,8,128,128]{3,2,1,0:T(8,128)(2,1)S(1)} %bitcast.33), custom_call_target="tpu_custom_call" | custom-call | tf_op jit(solution)/shard_map/shells_step0/partial/pallas_call | solution.py:204
  14.0 3.4 %collective-permute-start = (bf16[24,16,128]{2,1,0:T(8,128)(2,1)S(1)}, bf16[24,16,128]{2,1,0:T(8,128)(2,1)S(1)}, u32[]{:S(2)}, u32[]{:S(2)}) collective-permute-start(bf16[24,16,128]{2,1,0:T(8,128)(2,1)S(1)} %get-tuple-element.18), channel_id=1, source_target_pairs={{0,1},{1,2},{2,3},{3,4},{4,5},{5,6},{6,7},{7,8},{8,9},{9,10},{10,1... | collective-permute-start | bytes 294920 | tf_op jit(solution)/shard_map/halo0/ppermute | solution.py:148
  17.4 1.9 %collective-permute-start.1 = (bf16[24,16,128]{2,1,0:T(8,128)(2,1)S(1)}, bf16[24,16,128]{2,1,0:T(8,128)(2,1)S(1)}, u32[]{:S(2)}, u32[]{:S(2)}) collective-permute-start(bf16[24,16,128]{2,1,0:T(8,128)(2,1)S(1)} %get-tuple-element.19), channel_id=1, source_target_pairs={{1,0},{2,1},{3,2},{4,3},{5,4},{6,5},{7,6},{8,7},{9,8},{10,9},{11,1... | collective-permute-start | bytes 294920 | tf_op jit(solution)/shard_map/halo0/ppermute | solution.py:149
  19.3 1.6 %copy-done.2 = f32[32,128,128]{2,1,0:T(8,128)S(1)} copy-done((f32[32,128,128]{2,1,0:T(8,128)S(1)}, f32[32,128,128]{2,1,0:T(8,128)}, u32[]{:S(2)}) %copy-start.2) | copy-done | bytes 2097176
  20.9 0.9 prepare.1
  21.8 2.4 %collective-permute-done.1.from_above = bf16[24,16,128]{2,1,0:T(8,128)(2,1)S(1)} collective-permute-done((bf16[24,16,128]{2,1,0:T(8,128)(2,1)S(1)}, bf16[24,16,128]{2,1,0:T(8,128)(2,1)S(1)}, u32[]{:S(2)}, u32[]{:S(2)}) %collective-permute-start.1) | collective-permute-done | bytes 98336 | tf_op jit(solution)/shard_map/halo0/ppermute | solution.py:149
  24.8 2.1 %collective-permute-start.2 = (bf16[32,16,128]{2,1,0:T(8,128)(2,1)S(1)}, bf16[32,16,128]{2,1,0:T(8,128)(2,1)S(1)}, u32[]{:S(2)}, u32[]{:S(2)}) collective-permute-start(bf16[32,16,128]{2,1,0:T(8,128)(2,1)S(1)} %combine.2), channel_id=1, source_target_pairs={{0,16},{16,0},{32,48},{48,32},{64,80},{80,64},{96,112},{112,96},{1... | collective-permute-start | bytes 393224 | tf_op jit(solution)/shard_map/near0/ppermute | solution.py:143
  26.9 2.2 %collective-permute-start.4 = (bf16[32,16,128]{2,1,0:T(8,128)(2,1)S(1)}, bf16[32,16,128]{2,1,0:T(8,128)(2,1)S(1)}, u32[]{:S(2)}, u32[]{:S(2)}) collective-permute-start(bf16[32,16,128]{2,1,0:T(8,128)(2,1)S(1)} %combine.2), channel_id=1, source_target_pairs={{0,48},{16,32},{32,16},{48,0},{64,112},{80,96},{96,80},{112,64},{1... | collective-permute-start | bytes 393224 | tf_op jit(solution)/shard_map/near0/ppermute | solution.py:143
  29.1 3.9 %partial.3 = (f32[32,16,128]{2,1,0:T(8,128)S(1)}, bf16[24,16,128]{2,1,0:T(8,128)(2,1)S(1)}, bf16[24,16,128]{2,1,0:T(8,128)(2,1)S(1)}) custom-call(s32[2]{0:T(128)S(1)} %pad_add_fusion.place_ref, s32[8,32]{1,0:T(8,128)S(1)} %bitcast.40, bf16[32,16,128]{2,1,0:T(8,128)(2,1)S(1)} %collective-permute-done.8.hist, bf16[32,8,128,128]{3,2,1,0:T(8,128)(2,1)S(1)} %bitcast.34), custom_call_target="tpu_custom_call" | custom-call | tf_op jit(solution)/shard_map/shells_step1/partial/pallas_call | solution.py:214
  32.9 1.9 %collective-permute-start.10 = (bf16[24,16,128]{2,1,0:T(8,128)(2,1)S(1)}, bf16[24,16,128]{2,1,0:T(8,128)(2,1)S(1)}, u32[]{:S(2)}, u32[]{:S(2)}) collective-permute-start(bf16[24,16,128]{2,1,0:T(8,128)(2,1)S(1)} %get-tuple-element.25), channel_id=1, source_target_pairs={{1,0},{2,1},{3,2},{4,3},{5,4},{6,5},{7,6},{8,7},{9,8},{10,9},{11,1... | collective-permute-start | bytes 294920 | tf_op jit(solution)/shard_map/halo1/ppermute | solution.py:149
  34.8 4.5 %collective-permute-start.9 = (bf16[24,16,128]{2,1,0:T(8,128)(2,1)S(1)}, bf16[24,16,128]{2,1,0:T(8,128)(2,1)S(1)}, u32[]{:S(2)}, u32[]{:S(2)}) collective-permute-start(bf16[24,16,128]{2,1,0:T(8,128)(2,1)S(1)} %get-tuple-element.24), channel_id=1, source_target_pairs={{0,1},{1,2},{2,3},{3,4},{4,5},{5,6},{6,7},{7,8},{8,9},{9,10},{10,1... | collective-permute-start | bytes 294920 | tf_op jit(solution)/shard_map/halo1/ppermute | solution.py:148
  39.8 1.3 %collective-permute-done.9.from_below = bf16[24,16,128]{2,1,0:T(8,128)(2,1)S(1)} collective-permute-done((bf16[24,16,128]{2,1,0:T(8,128)(2,1)S(1)}, bf16[24,16,128]{2,1,0:T(8,128)(2,1)S(1)}, u32[]{:S(2)}, u32[]{:S(2)}) %collective-permute-start.9) | collective-permute-done | bytes 98336 | tf_op jit(solution)/shard_map/halo1/ppermute | solution.py:148
  41.6 2.1 %collective-permute-start.11 = (bf16[32,16,128]{2,1,0:T(8,128)(2,1)S(1)}, bf16[32,16,128]{2,1,0:T(8,128)(2,1)S(1)}, u32[]{:S(2)}, u32[]{:S(2)}) collective-permute-start(bf16[32,16,128]{2,1,0:T(8,128)(2,1)S(1)} %combine.3), channel_id=1, source_target_pairs={{0,16},{16,0},{32,48},{48,32},{64,80},{80,64},{96,112},{112,96},{1... | collective-permute-start | bytes 393224 | tf_op jit(solution)/shard_map/near1/ppermute | solution.py:143
  43.7 2.1 %collective-permute-start.13 = (bf16[32,16,128]{2,1,0:T(8,128)(2,1)S(1)}, bf16[32,16,128]{2,1,0:T(8,128)(2,1)S(1)}, u32[]{:S(2)}, u32[]{:S(2)}) collective-permute-start(bf16[32,16,128]{2,1,0:T(8,128)(2,1)S(1)} %combine.3), channel_id=1, source_target_pairs={{0,48},{16,32},{32,16},{48,0},{64,112},{80,96},{96,80},{112,64},{1... | collective-permute-start | bytes 393224 | tf_op jit(solution)/shard_map/near1/ppermute | solution.py:143
  46.0 4.3 %collective-permute-start.5 = (bf16[32,16,128]{2,1,0:T(8,128)(2,1)S(1)}, bf16[32,16,128]{2,1,0:T(8,128)(2,1)S(1)}, u32[]{:S(2)}, u32[]{:S(2)}) collective-permute-start(bf16[32,16,128]{2,1,0:T(8,128)(2,1)S(1)} %add_convert_fusion.1.own), channel_id=1, source_target_pairs={{0,64},{16,80},{32,96},{48,112},{64,0},{80,16},{96,32},{112,48},{1... | collective-permute-start | bytes 393224 | tf_op jit(solution)/shard_map/far0/ppermute | solution.py:143
  50.2 2.1 %collective-permute-start.6 = (bf16[32,16,128]{2,1,0:T(8,128)(2,1)S(1)}, bf16[32,16,128]{2,1,0:T(8,128)(2,1)S(1)}, u32[]{:S(2)}, u32[]{:S(2)}) collective-permute-start(bf16[32,16,128]{2,1,0:T(8,128)(2,1)S(1)} %add_convert_fusion.1.own), channel_id=1, source_target_pairs={{0,128},{16,144},{32,160},{48,176},{64,192},{80,208},{96,224},{112... | collective-permute-start | bytes 393224 | tf_op jit(solution)/shard_map/far0/ppermute | solution.py:143
  52.4 1.3 %collective-permute-start.7 = (bf16[32,16,128]{2,1,0:T(8,128)(2,1)S(1)}, bf16[32,16,128]{2,1,0:T(8,128)(2,1)S(1)}, u32[]{:S(2)}, u32[]{:S(2)}) collective-permute-start(bf16[32,16,128]{2,1,0:T(8,128)(2,1)S(1)} %add_convert_fusion.1.own), channel_id=1, source_target_pairs={{0,192},{16,208},{32,224},{48,240},{64,128},{80,144},{96,160},{112... | collective-permute-start | bytes 393224 | tf_op jit(solution)/shard_map/far0/ppermute | solution.py:143
  53.7 3.2 %collective-permute-start.14 = (bf16[32,16,128]{2,1,0:T(8,128)(2,1)S(1)}, bf16[32,16,128]{2,1,0:T(8,128)(2,1)S(1)}, u32[]{:S(2)}, u32[]{:S(2)}) collective-permute-start(bf16[32,16,128]{2,1,0:T(8,128)(2,1)S(1)} %add_convert_fusion.own), channel_id=1, source_target_pairs={{0,64},{16,80},{32,96},{48,112},{64,0},{80,16},{96,32},{112,48},{1... | collective-permute-start | bytes 393224 | tf_op jit(solution)/shard_map/far1/ppermute | solution.py:143
  56.9 4.3 %collective-permute-start.15 = (bf16[32,16,128]{2,1,0:T(8,128)(2,1)S(1)}, bf16[32,16,128]{2,1,0:T(8,128)(2,1)S(1)}, u32[]{:S(2)}, u32[]{:S(2)}) collective-permute-start(bf16[32,16,128]{2,1,0:T(8,128)(2,1)S(1)} %add_convert_fusion.own), channel_id=1, source_target_pairs={{0,128},{16,144},{32,160},{48,176},{64,192},{80,208},{96,224},{112... | collective-permute-start | bytes 393224 | tf_op jit(solution)/shard_map/far1/ppermute | solution.py:143
  61.8 0.9 collective-permute-done.6.far2
  62.7 4.6 %first_step.1 = (bf16[32,16,128]{2,1,0:T(8,128)(2,1)S(1)}, f32[32,128]{1,0:T(8,128)S(1)}, f32[32,16,128]{2,1,0:T(8,128)S(1)}, bf16[24,16,128]{2,1,0:T(8,128)(2,1)S(1)}, bf16[24,16,128]{2,1,0:T(8,128)(2,1)S(1)}) custom-call(s32[2]{0:T(128)S(1)} %pad_add_fusion.place_ref, s32[8,32]{1,0:T(8,128)S(1)} %bitcast.41, ...), custom_call_target="tpu_custom_call" | custom-call | tf_op jit(solution)/shard_map/first_step/pallas_call | solution.py:224
  67.3 16.0 %collective-permute-start.17 = (bf16[24,16,128]{2,1,0:T(8,128)(2,1)S(1)}, bf16[24,16,128]{2,1,0:T(8,128)(2,1)S(1)}, u32[]{:S(2)}, u32[]{:S(2)}) collective-permute-start(bf16[24,16,128]{2,1,0:T(8,128)(2,1)S(1)} %get-tuple-element.27), channel_id=1, source_target_pairs={{0,1},{1,2},{2,3},{3,4},{4,5},{5,6},{6,7},{7,8},{8,9},{9,10},{10,1... | collective-permute-start | bytes 294920 | tf_op jit(solution)/shard_map/halo_extra/ppermute | solution.py:148
  83.4 1.9 %collective-permute-start.18 = (bf16[24,16,128]{2,1,0:T(8,128)(2,1)S(1)}, bf16[24,16,128]{2,1,0:T(8,128)(2,1)S(1)}, u32[]{:S(2)}, u32[]{:S(2)}) collective-permute-start(bf16[24,16,128]{2,1,0:T(8,128)(2,1)S(1)} %get-tuple-element.28), channel_id=1, source_target_pairs={{1,0},{2,1},{3,2},{4,3},{5,4},{6,5},{7,6},{8,7},{9,8},{10,9},{11,1... | collective-permute-start | bytes 294920 | tf_op jit(solution)/shard_map/halo_extra/ppermute | solution.py:149
  85.3 1.9 %collective-permute-start.25 = (bf16[32,16,128]{2,1,0:T(8,128)(2,1)S(1)}, bf16[32,16,128]{2,1,0:T(8,128)(2,1)S(1)}, u32[]{:S(2)}, u32[]{:S(2)}) collective-permute-start(bf16[32,16,128]{2,1,0:T(8,128)(2,1)S(1)} %bitcast.38), channel_id=1, source_target_pairs={{0,32},{16,48},{32,64},{48,80},{64,96},{80,112},{96,128},{112,144}... | collective-permute-start | bytes 393224 | tf_op jit(solution)/shard_map/ppermute | solution.py:206
  87.3 2.9 %collective-permute-done.18.from_above = bf16[24,16,128]{2,1,0:T(8,128)(2,1)S(1)} collective-permute-done((bf16[24,16,128]{2,1,0:T(8,128)(2,1)S(1)}, bf16[24,16,128]{2,1,0:T(8,128)(2,1)S(1)}, u32[]{:S(2)}, u32[]{:S(2)}) %collective-permute-start.18) | collective-permute-done | bytes 98336 | tf_op jit(solution)/shard_map/halo_extra/ppermute | solution.py:149
  90.2 0.8 second_step.1
  94.5 1.3 %collective-permute-start.24 = (bf16[32,128]{1,0:T(8,128)(2,1)S(1)}, bf16[32,128]{1,0:T(8,128)(2,1)S(1)}, u32[]{:S(2)}, u32[]{:S(2)}) collective-permute-start(bf16[32,128]{1,0:T(8,128)(2,1)S(1)} %get-tuple-element.38), channel_id=1, source_target_pairs={{0,48},{64,112},{128,176},{192,240},{1,49},{65,113},{129,177},{193... | collective-permute-start | bytes 24584 | tf_op jit(solution)/shard_map/spread/ppermute | solution.py:238
  96.5 11.4 %collective-permute-done.24 = bf16[32,128]{1,0:T(8,128)(2,1)S(1)} collective-permute-done((bf16[32,128]{1,0:T(8,128)(2,1)S(1)}, bf16[32,128]{1,0:T(8,128)(2,1)S(1)}, u32[]{:S(2)}, u32[]{:S(2)}) %collective-permute-start.24) | collective-permute-done | bytes 8224 | tf_op jit(solution)/shard_map/spread/ppermute | solution.py:238
  (56 shorter events, 7.1 us)
Async XLA Ops:
  0.6 28.4 %collective-permute-start.8 = (bf16[32,16,128]{2,1,0:T(8,128)(2,1)}, bf16[32,16,128]{2,1,0:T(8,128)(2,1)S(1)}, u32[]{:S(2)}, u32[]{:S(2)}) collective-permute-start(bf16[32,16,128]{2,1,0:T(8,128)(2,1)} %bitcast.36), channel_id=1, source_target_pairs={{0,16},{16,32},{32,48},{48,64},{64,80},{80,96},{96,112},{112,128},... | collective-permute-start | bytes 393224 | tf_op jit(solution)/shard_map/ppermute | solution.py:205
  5.1 3.4 %copy-start = (bf16[1,32,8,128,128]{4,3,2,1,0:T(8,128)(2,1)S(1)}, bf16[1,32,8,128,128]{4,3,2,1,0:T(8,128)(2,1)}, u32[]{:S(2)}) copy-start(bf16[1,32,8,128,128]{4,3,2,1,0:T(8,128)(2,1)} %param.6) | copy-start | bytes 25165828
  10.1 9.2 %copy-start.5 = (f32[2,32,1,256]{3,2,1,0:T(1,128)S(1)}, f32[2,32,1,256]{3,2,1,0:T(1,128)}, u32[]{:S(2)}) copy-start(f32[2,32,1,256]{3,2,1,0:T(1,128)} %incident.1) | copy-start | bytes 196612
  10.1 9.2 %copy-start.8 = (s32[32,256]{1,0:T(8,128)S(1)}, s32[32,256]{1,0:T(8,128)}, u32[]{:S(2)}) copy-start(s32[32,256]{1,0:T(8,128)} %element_map.1) | copy-start | bytes 98308
  10.1 19.0 %copy-start.1 = (bf16[1,32,8,128,128]{4,3,2,1,0:T(8,128)(2,1)S(1)}, bf16[1,32,8,128,128]{4,3,2,1,0:T(8,128)(2,1)}, u32[]{:S(2)}) copy-start(bf16[1,32,8,128,128]{4,3,2,1,0:T(8,128)(2,1)} %param.6) | copy-start | bytes 25165828
  10.1 19.0 %copy-start.7 = (s32[1,32,8]{1,2,0:T(8,128)S(1)}, s32[1,32,8]{1,2,0:T(8,128)}, u32[]{:S(2)}) copy-start(s32[1,32,8]{1,2,0:T(8,128)} %param.7) | copy-start | bytes 3076
  14.0 7.8 %collective-permute-start = (bf16[24,16,128]{2,1,0:T(8,128)(2,1)S(1)}, bf16[24,16,128]{2,1,0:T(8,128)(2,1)S(1)}, u32[]{:S(2)}, u32[]{:S(2)}) collective-permute-start(bf16[24,16,128]{2,1,0:T(8,128)(2,1)S(1)} %get-tuple-element.18), channel_id=1, source_target_pairs={{0,1},{1,2},{2,3},{3,4},{4,5},{5,6},{6,7},{7,8},{8,9},{9,10},{10,1... | collective-permute-start | bytes 294920 | tf_op jit(solution)/shard_map/halo0/ppermute | solution.py:148
  17.4 6.8 %collective-permute-start.1 = (bf16[24,16,128]{2,1,0:T(8,128)(2,1)S(1)}, bf16[24,16,128]{2,1,0:T(8,128)(2,1)S(1)}, u32[]{:S(2)}, u32[]{:S(2)}) collective-permute-start(bf16[24,16,128]{2,1,0:T(8,128)(2,1)S(1)} %get-tuple-element.19), channel_id=1, source_target_pairs={{1,0},{2,1},{3,2},{4,3},{5,4},{6,5},{7,6},{8,7},{9,8},{10,9},{11,1... | collective-permute-start | bytes 294920 | tf_op jit(solution)/shard_map/halo0/ppermute | solution.py:149
  24.8 18.9 %collective-permute-start.2 = (bf16[32,16,128]{2,1,0:T(8,128)(2,1)S(1)}, bf16[32,16,128]{2,1,0:T(8,128)(2,1)S(1)}, u32[]{:S(2)}, u32[]{:S(2)}) collective-permute-start(bf16[32,16,128]{2,1,0:T(8,128)(2,1)S(1)} %combine.2), channel_id=1, source_target_pairs={{0,16},{16,0},{32,48},{48,32},{64,80},{80,64},{96,112},{112,96},{1... | collective-permute-start | bytes 393224 | tf_op jit(solution)/shard_map/near0/ppermute | solution.py:143
  26.9 19.0 %collective-permute-start.3 = (bf16[32,16,128]{2,1,0:T(8,128)(2,1)S(1)}, bf16[32,16,128]{2,1,0:T(8,128)(2,1)S(1)}, u32[]{:S(2)}, u32[]{:S(2)}) collective-permute-start(bf16[32,16,128]{2,1,0:T(8,128)(2,1)S(1)} %combine.2), channel_id=1, source_target_pairs={{0,32},{16,48},{32,0},{48,16},{64,96},{80,112},{96,64},{112,80},{1... | collective-permute-start | bytes 393224 | tf_op jit(solution)/shard_map/near0/ppermute | solution.py:143
  26.9 19.0 %collective-permute-start.4 = (bf16[32,16,128]{2,1,0:T(8,128)(2,1)S(1)}, bf16[32,16,128]{2,1,0:T(8,128)(2,1)S(1)}, u32[]{:S(2)}, u32[]{:S(2)}) collective-permute-start(bf16[32,16,128]{2,1,0:T(8,128)(2,1)S(1)} %combine.2), channel_id=1, source_target_pairs={{0,48},{16,32},{32,16},{48,0},{64,112},{80,96},{96,80},{112,64},{1... | collective-permute-start | bytes 393224 | tf_op jit(solution)/shard_map/near0/ppermute | solution.py:143
  32.9 6.8 %collective-permute-start.10 = (bf16[24,16,128]{2,1,0:T(8,128)(2,1)S(1)}, bf16[24,16,128]{2,1,0:T(8,128)(2,1)S(1)}, u32[]{:S(2)}, u32[]{:S(2)}) collective-permute-start(bf16[24,16,128]{2,1,0:T(8,128)(2,1)S(1)} %get-tuple-element.25), channel_id=1, source_target_pairs={{1,0},{2,1},{3,2},{4,3},{5,4},{6,5},{7,6},{8,7},{9,8},{10,9},{11,1... | collective-permute-start | bytes 294920 | tf_op jit(solution)/shard_map/halo1/ppermute | solution.py:149
  34.8 6.2 %collective-permute-start.9 = (bf16[24,16,128]{2,1,0:T(8,128)(2,1)S(1)}, bf16[24,16,128]{2,1,0:T(8,128)(2,1)S(1)}, u32[]{:S(2)}, u32[]{:S(2)}) collective-permute-start(bf16[24,16,128]{2,1,0:T(8,128)(2,1)S(1)} %get-tuple-element.24), channel_id=1, source_target_pairs={{0,1},{1,2},{2,3},{3,4},{4,5},{5,6},{6,7},{7,8},{8,9},{9,10},{10,1... | collective-permute-start | bytes 294920 | tf_op jit(solution)/shard_map/halo1/ppermute | solution.py:148
  41.6 10.7 %collective-permute-start.11 = (bf16[32,16,128]{2,1,0:T(8,128)(2,1)S(1)}, bf16[32,16,128]{2,1,0:T(8,128)(2,1)S(1)}, u32[]{:S(2)}, u32[]{:S(2)}) collective-permute-start(bf16[32,16,128]{2,1,0:T(8,128)(2,1)S(1)} %combine.3), channel_id=1, source_target_pairs={{0,16},{16,0},{32,48},{48,32},{64,80},{80,64},{96,112},{112,96},{1... | collective-permute-start | bytes 393224 | tf_op jit(solution)/shard_map/near1/ppermute | solution.py:143
  43.7 9.9 %collective-permute-start.12 = (bf16[32,16,128]{2,1,0:T(8,128)(2,1)S(1)}, bf16[32,16,128]{2,1,0:T(8,128)(2,1)S(1)}, u32[]{:S(2)}, u32[]{:S(2)}) collective-permute-start(bf16[32,16,128]{2,1,0:T(8,128)(2,1)S(1)} %combine.3), channel_id=1, source_target_pairs={{0,32},{16,48},{32,0},{48,16},{64,96},{80,112},{96,64},{112,80},{1... | collective-permute-start | bytes 393224 | tf_op jit(solution)/shard_map/near1/ppermute | solution.py:143
  43.7 9.9 %collective-permute-start.13 = (bf16[32,16,128]{2,1,0:T(8,128)(2,1)S(1)}, bf16[32,16,128]{2,1,0:T(8,128)(2,1)S(1)}, u32[]{:S(2)}, u32[]{:S(2)}) collective-permute-start(bf16[32,16,128]{2,1,0:T(8,128)(2,1)S(1)} %combine.3), channel_id=1, source_target_pairs={{0,48},{16,32},{32,16},{48,0},{64,112},{80,96},{96,80},{112,64},{1... | collective-permute-start | bytes 393224 | tf_op jit(solution)/shard_map/near1/ppermute | solution.py:143
  46.0 15.3 %collective-permute-start.5 = (bf16[32,16,128]{2,1,0:T(8,128)(2,1)S(1)}, bf16[32,16,128]{2,1,0:T(8,128)(2,1)S(1)}, u32[]{:S(2)}, u32[]{:S(2)}) collective-permute-start(bf16[32,16,128]{2,1,0:T(8,128)(2,1)S(1)} %add_convert_fusion.1.own), channel_id=1, source_target_pairs={{0,64},{16,80},{32,96},{48,112},{64,0},{80,16},{96,32},{112,48},{1... | collective-permute-start | bytes 393224 | tf_op jit(solution)/shard_map/far0/ppermute | solution.py:143
  50.2 12.5 %collective-permute-start.6 = (bf16[32,16,128]{2,1,0:T(8,128)(2,1)S(1)}, bf16[32,16,128]{2,1,0:T(8,128)(2,1)S(1)}, u32[]{:S(2)}, u32[]{:S(2)}) collective-permute-start(bf16[32,16,128]{2,1,0:T(8,128)(2,1)S(1)} %add_convert_fusion.1.own), channel_id=1, source_target_pairs={{0,128},{16,144},{32,160},{48,176},{64,192},{80,208},{96,224},{112... | collective-permute-start | bytes 393224 | tf_op jit(solution)/shard_map/far0/ppermute | solution.py:143
  52.4 10.4 %collective-permute-start.7 = (bf16[32,16,128]{2,1,0:T(8,128)(2,1)S(1)}, bf16[32,16,128]{2,1,0:T(8,128)(2,1)S(1)}, u32[]{:S(2)}, u32[]{:S(2)}) collective-permute-start(bf16[32,16,128]{2,1,0:T(8,128)(2,1)S(1)} %add_convert_fusion.1.own), channel_id=1, source_target_pairs={{0,192},{16,208},{32,224},{48,240},{64,128},{80,144},{96,160},{112... | collective-permute-start | bytes 393224 | tf_op jit(solution)/shard_map/far0/ppermute | solution.py:143
  53.7 36.5 %collective-permute-start.14 = (bf16[32,16,128]{2,1,0:T(8,128)(2,1)S(1)}, bf16[32,16,128]{2,1,0:T(8,128)(2,1)S(1)}, u32[]{:S(2)}, u32[]{:S(2)}) collective-permute-start(bf16[32,16,128]{2,1,0:T(8,128)(2,1)S(1)} %add_convert_fusion.own), channel_id=1, source_target_pairs={{0,64},{16,80},{32,96},{48,112},{64,0},{80,16},{96,32},{112,48},{1... | collective-permute-start | bytes 393224 | tf_op jit(solution)/shard_map/far1/ppermute | solution.py:143
  56.9 33.3 %collective-permute-start.15 = (bf16[32,16,128]{2,1,0:T(8,128)(2,1)S(1)}, bf16[32,16,128]{2,1,0:T(8,128)(2,1)S(1)}, u32[]{:S(2)}, u32[]{:S(2)}) collective-permute-start(bf16[32,16,128]{2,1,0:T(8,128)(2,1)S(1)} %add_convert_fusion.own), channel_id=1, source_target_pairs={{0,128},{16,144},{32,160},{48,176},{64,192},{80,208},{96,224},{112... | collective-permute-start | bytes 393224 | tf_op jit(solution)/shard_map/far1/ppermute | solution.py:143
  61.3 29.0 %collective-permute-start.16 = (bf16[32,16,128]{2,1,0:T(8,128)(2,1)S(1)}, bf16[32,16,128]{2,1,0:T(8,128)(2,1)S(1)}, u32[]{:S(2)}, u32[]{:S(2)}) collective-permute-start(bf16[32,16,128]{2,1,0:T(8,128)(2,1)S(1)} %add_convert_fusion.own), channel_id=1, source_target_pairs={{0,192},{16,208},{32,224},{48,240},{64,128},{80,144},{96,160},{112... | collective-permute-start | bytes 393224 | tf_op jit(solution)/shard_map/far1/ppermute | solution.py:143
  62.7 22.6 %copy-start.4 = (bf16[1,32,16,128]{3,2,1,0:T(8,128)(2,1)S(1)}, bf16[1,32,16,128]{3,2,1,0:T(8,128)(2,1)}, u32[]{:S(2)}) copy-start(bf16[1,32,16,128]{3,2,1,0:T(8,128)(2,1)} %param.8) | copy-start | bytes 393220
  67.3 18.0 %collective-permute-start.17 = (bf16[24,16,128]{2,1,0:T(8,128)(2,1)S(1)}, bf16[24,16,128]{2,1,0:T(8,128)(2,1)S(1)}, u32[]{:S(2)}, u32[]{:S(2)}) collective-permute-start(bf16[24,16,128]{2,1,0:T(8,128)(2,1)S(1)} %get-tuple-element.27), channel_id=1, source_target_pairs={{0,1},{1,2},{2,3},{3,4},{4,5},{5,6},{6,7},{7,8},{8,9},{9,10},{10,1... | collective-permute-start | bytes 294920 | tf_op jit(solution)/shard_map/halo_extra/ppermute | solution.py:148
  83.4 6.8 %collective-permute-start.18 = (bf16[24,16,128]{2,1,0:T(8,128)(2,1)S(1)}, bf16[24,16,128]{2,1,0:T(8,128)(2,1)S(1)}, u32[]{:S(2)}, u32[]{:S(2)}) collective-permute-start(bf16[24,16,128]{2,1,0:T(8,128)(2,1)S(1)} %get-tuple-element.28), channel_id=1, source_target_pairs={{1,0},{2,1},{3,2},{4,3},{5,4},{6,5},{7,6},{8,7},{9,8},{10,9},{11,1... | collective-permute-start | bytes 294920 | tf_op jit(solution)/shard_map/halo_extra/ppermute | solution.py:149
  85.3 10.4 %collective-permute-start.25 = (bf16[32,16,128]{2,1,0:T(8,128)(2,1)S(1)}, bf16[32,16,128]{2,1,0:T(8,128)(2,1)S(1)}, u32[]{:S(2)}, u32[]{:S(2)}) collective-permute-start(bf16[32,16,128]{2,1,0:T(8,128)(2,1)S(1)} %bitcast.38), channel_id=1, source_target_pairs={{0,32},{16,48},{32,64},{48,80},{64,96},{80,112},{96,128},{112,144}... | collective-permute-start | bytes 393224 | tf_op jit(solution)/shard_map/ppermute | solution.py:206
  91.0 2.0 %collective-permute-start.19 = (bf16[4,32,128]{2,1,0:T(8,128)(2,1)S(1)}, bf16[4,32,128]{2,1,0:T(8,128)(2,1)S(1)}, u32[]{:S(2)}, u32[]{:S(2)}) collective-permute-start(bf16[4,32,128]{2,1,0:T(8,128)(2,1)S(1)} %get-tuple-element.36), channel_id=1, source_target_pairs={{0,64},{1,65},{2,66},{3,67},{4,68},{5,69},{6,70},{7,71},{8,72},{9,... | collective-permute-start | bytes 98312 | tf_op jit(solution)/shard_map/spread/ppermute | solution.py:233
  91.7 1.4 %collective-permute-start.20 = (bf16[4,32,128]{2,1,0:T(8,128)(2,1)S(1)}, bf16[4,32,128]{2,1,0:T(8,128)(2,1)S(1)}, u32[]{:S(2)}, u32[]{:S(2)}) collective-permute-start(bf16[4,32,128]{2,1,0:T(8,128)(2,1)S(1)} %get-tuple-element.34), channel_id=1, source_target_pairs={{0,128},{1,129},{2,130},{3,131},{4,132},{5,133},{6,134},{7,135},{8... | collective-permute-start | bytes 98312 | tf_op jit(solution)/shard_map/spread/ppermute | solution.py:233
  92.4 0.7 collective-permute-start.21
  93.1 3.3 %collective-permute-start.22 = (bf16[32,128]{1,0:T(8,128)(2,1)S(1)}, bf16[32,128]{1,0:T(8,128)(2,1)S(1)}, u32[]{:S(2)}, u32[]{:S(2)}) collective-permute-start(bf16[32,128]{1,0:T(8,128)(2,1)S(1)} %get-tuple-element.39), channel_id=1, source_target_pairs={{0,16},{64,80},{128,144},{192,208},{1,17},{65,81},{129,145},{193,2... | collective-permute-start | bytes 24584 | tf_op jit(solution)/shard_map/spread/ppermute | solution.py:238
  93.8 2.7 %collective-permute-start.23 = (bf16[32,128]{1,0:T(8,128)(2,1)S(1)}, bf16[32,128]{1,0:T(8,128)(2,1)S(1)}, u32[]{:S(2)}, u32[]{:S(2)}) collective-permute-start(bf16[32,128]{1,0:T(8,128)(2,1)S(1)} %get-tuple-element.37), channel_id=1, source_target_pairs={{0,32},{64,96},{128,160},{192,224},{1,33},{65,97},{129,161},{193,2... | collective-permute-start | bytes 24584 | tf_op jit(solution)/shard_map/spread/ppermute | solution.py:238
  94.5 13.4 %collective-permute-start.24 = (bf16[32,128]{1,0:T(8,128)(2,1)S(1)}, bf16[32,128]{1,0:T(8,128)(2,1)S(1)}, u32[]{:S(2)}, u32[]{:S(2)}) collective-permute-start(bf16[32,128]{1,0:T(8,128)(2,1)S(1)} %get-tuple-element.38), channel_id=1, source_target_pairs={{0,48},{64,112},{128,176},{192,240},{1,49},{65,113},{129,177},{193... | collective-permute-start | bytes 24584 | tf_op jit(solution)/shard_map/spread/ppermute | solution.py:238
  (3 other events, 3.2 us)

commit v2 on v1

v2 whole, which is shorter than its diff:
```python
import functools

import jax
import jax.numpy as jnp
from jax import lax
from jax.experimental import pallas as pl
from jax.experimental.pallas import tpu as pltpu
from jax.sharding import PartitionSpec as P

F32 = jnp.float32
BF16 = jnp.bfloat16
HALF = 24
NT = (((1,), (1,)), ((), ()))
VMEM = pl.BlockSpec(memory_space=pltpu.VMEM)
HBM = pl.BlockSpec(memory_space=pltpu.HBM)
SMEM = pl.BlockSpec(memory_space=pltpu.SMEM)


def split(x):
    high = x.astype(BF16)
    return high, (x - high.astype(F32)).astype(BF16)


def banded(place_ref, offsets_ref, rows_of, blocks, window, total_blocks, chunks, arrived=None):
    block_cols, width, size, _ = blocks.shape
    first = place_ref[0]
    window[...] = jnp.zeros_like(window)

    def columns(i, carry):
        if arrived is not None:
            arrived(i)
        for j in range(block_cols // chunks):
            c = i * (block_cols // chunks) + j
            column = blocks[c].reshape(width * size, size)
            prod = lax.dot_general(rows_of(c), column, NT, preferred_element_type=F32)
            for k in range(width):
                row = jnp.clip(first + c + offsets_ref[k, c], 0, total_blocks - 1) - first + HALF
                window[row] += prod[:, size * k : size * (k + 1)]
        return carry

    lax.fori_loop(0, chunks, columns, 0)


def hand_out(place_ref, windows, main, first_out, second_out):
    n = main.shape[0]
    even = 1 - place_ref[2]
    for t, window in enumerate(windows):
        rows = slice(t * window.shape[1], (t + 1) * window.shape[1])
        main[:, rows] = window[HALF : HALF + n]
        first_out[:, rows] = window[pl.ds(even * (HALF + n), HALF)].astype(BF16)
        second_out[:, rows] = window[pl.ds((1 - even) * (HALF + n), HALF)].astype(BF16)


def take_in(place_ref, main, first_in, second_in):
    n = main.shape[0]
    even = 1 - place_ref[2]
    main[pl.ds(even * (n - HALF), HALF)] += first_in[...].astype(F32)
    main[pl.ds((1 - even) * (n - HALF), HALF)] += second_in[...].astype(F32)


def first_shells_kernel(
    total_blocks, place_ref, offsets_hbm, shells_hbm, blocks_hbm, window, blocks, shells, offsets_ref, sems
):
    chunks = sems.shape[0] - 2
    some = blocks.shape[0] // chunks

    def copy(i):
        part = pl.ds(i * some, some)
        return pltpu.make_async_copy(blocks_hbm.at[part], blocks.at[part], sems.at[i])

    small = [
        pltpu.make_async_copy(offsets_hbm, offsets_ref, sems.at[chunks]),
        pltpu.make_async_copy(shells_hbm, shells, sems.at[chunks + 1]),
    ]
    for each in small:
        each.start()
    for i in range(chunks):
        copy(i).start()
    for each in small:
        each.wait()
    banded(
        place_ref, offsets_ref, lambda c: shells[c], blocks, window, total_blocks, chunks,
        lambda i: copy(i).wait(),
    )


def second_shells_kernel(
    total_blocks, place_ref, offsets_ref, older, first_window, blocks,
    main, first_out, second_out, kept, window,
):
    banded(place_ref, offsets_ref, lambda c: older[c], blocks, window, total_blocks, 2)
    hand_out(place_ref, (first_window, window), main, first_out, second_out)


def prepare_kernel(incident, element_map, inverse, source, inverse_parts):
    n, size, _ = inverse.shape
    samples = element_map.shape[1]
    unknown = lax.broadcasted_iota(jnp.int32, (size, samples), 0)
    line = lax.broadcasted_iota(jnp.int32, (8, samples), 0)
    for b in range(n):
        load = (unknown == element_map[b : b + 1, :]).astype(F32).astype(BF16)
        rows = jnp.zeros((8, samples), F32)
        for t in range(2):
            sample = jnp.broadcast_to(incident[t, b], (8, samples))
            high = sample.astype(BF16).astype(F32)
            rows = jnp.where(line == 2 * t, high, jnp.where(line == 2 * t + 1, sample - high, rows))
        out = lax.dot_general(rows.astype(BF16), load, NT, preferred_element_type=F32)
        for t in range(2):
            source[t, b : b + 1, :] = out[2 * t : 2 * t + 1] + out[2 * t + 1 : 2 * t + 2]
        high, low = split(inverse[b])
        inverse_parts[b, :, :size] = high
        inverse_parts[b, :, size:] = low


def combine_kernel(
    place_ref, main, first_in, second_in, source, keep, send1, send2, send3, total, by_pulse
):
    n, rows, size = main.shape
    pulses = rows // 2
    line = lax.broadcasted_iota(jnp.int32, (rows, size), 0)
    for b in range(n):
        value = main[b]
        for t in range(2):
            mine = line == place_ref[1] + t * pulses
            value = value - jnp.where(mine, source[t, b : b + 1, :], 0.0)
        total[b] = value
    take_in(place_ref, total, first_in, second_in)
    flat = total.reshape(n * rows, size)
    for p in range(pulses):
        for t in range(2):
            by_pulse[p, t] = flat[pl.ds(t * pulses + p, n, stride=rows), :].astype(BF16)
    for distance, out in enumerate((keep, send1, send2, send3)):
        out[...] = by_pulse[pl.ds(quarter_of(place_ref, distance, out.shape[0]), out.shape[0])]


def quarter_of(place_ref, distance, quarter):
    return ((place_ref[1] & 3) ^ distance) * quarter


def by_row(place_ref, parts, t, scratch):
    quarter, _, n, _ = parts[0].shape
    for distance, part in enumerate(parts):
        start = quarter_of(place_ref, distance, quarter)
        for i in range(quarter):
            scratch[pl.ds(pl.multiple_of((start + i) * n, n), n), :] = part[i, t].astype(F32)


def solve(rest, inverse_part):
    pulses, size = rest.shape
    high, low = split(-rest)
    lhs = jnp.concatenate(
        [jnp.concatenate([high, high], 1), jnp.concatenate([low, jnp.zeros_like(low)], 1)], 0
    )
    out = lax.dot_general(lhs, inverse_part, NT, preferred_element_type=F32)
    return out[:pulses] + out[pulses:]


def first_step_kernel(
    total_blocks, place_ref, offsets_ref, rest0, rest1, rest2, rest3, inverse_parts, blocks,
    current, own_pulse, main, first_out, second_out, scratch, window,
):
    n, pulses, size = current.shape
    mine = lax.broadcasted_iota(jnp.int32, (pulses, size), 0) == place_ref[1]
    by_row(place_ref, (rest0, rest1, rest2, rest3), 0, scratch)
    for b in range(n):
        new = solve(scratch[pl.ds(b, pulses, stride=n), :], inverse_parts[b])
        current[b] = new.astype(BF16)
        own_pulse[b : b + 1, :] = jnp.sum(jnp.where(mine, new, 0.0), axis=0, keepdims=True)
    banded(place_ref, offsets_ref, lambda c: current[c], blocks, window, total_blocks, 2)
    hand_out(place_ref, (window,), main, first_out, second_out)


def second_step_kernel(
    place_ref, rest0, rest1, rest2, rest3, main, first_in, second_in, inverse_parts, current0, oldest,
    aged, by_pulse, scratch, total,
):
    n, pulses, size = aged.shape
    total[...] = main[...]
    take_in(place_ref, total, first_in, second_in)
    by_row(place_ref, (rest0, rest1, rest2, rest3), 1, scratch)
    for b in range(n):
        value = scratch[pl.ds(b, pulses, stride=n), :] + total[b]
        new = solve(value, inverse_parts[b])
        aged[b] = new.astype(BF16)
        scratch[pl.ds(b, pulses, stride=n), :] = new
    for p in range(pulses):
        by_pulse[p] = scratch[p * n : (p + 1) * n, :].astype(BF16)

    @pl.when(place_ref[1] == 1)
    def _():
        aged[...] = current0[...]

    @pl.when(place_ref[1] > 1)
    def _():
        aged[...] = oldest[...]


def call(kernel, name, out_shape, in_specs, scratch_shapes=(), mib=16, aliases={}):
    return pl.pallas_call(
        kernel,
        name=name,
        out_shape=out_shape,
        in_specs=in_specs,
        out_specs=[VMEM] * len(out_shape),
        scratch_shapes=scratch_shapes,
        input_output_aliases=aliases,
        compiler_params=pltpu.CompilerParams(vmem_limit_bytes=mib * 2**20),
    )


def exchange(block, distance):
    return lax.ppermute(block, "lag", [(i, i ^ distance) for i in range(16)])


def added(own, others):
    return sum((other.astype(F32) for other in others), own.astype(F32)).astype(BF16)


def trade(first_out, second_out):
    n = lax.axis_size("col")
    pairs = [(i, i ^ 1) for i in range(n)]
    others = [(i, i + 1 if i % 2 else i - 1) for i in range(1, n - 1)]
    return lax.ppermute(first_out, "col", pairs), lax.ppermute(second_out, "col", others)


def body(blocks, offsets, history, instant_inverse, incident, element_map):
    lag_index = lax.axis_index("lag")
    lags = lax.axis_size("lag")
    n, pulses, size = history.shape[1:]
    total_blocks = n * lax.axis_size("col")
    col_index = lax.axis_index("col")
    place = jnp.stack([col_index * n, lag_index, col_index % 2]).astype(jnp.int32)
    blocks = blocks[0]
    band_rows = offsets[0].T
    shells = history[0]

    def shape(*dims, dtype=F32):
        return jax.ShapeDtypeStruct(dims, dtype)

    def partial_out(rows):
        edge = shape(HALF, rows, size, dtype=BF16)
        return shape(n, rows, size), edge, edge

    def window(rows):
        return pltpu.VMEM((n + 2 * HALF, rows, size), F32)

    kept = shape(*blocks.shape, dtype=BF16)
    first_shells = call(
        functools.partial(first_shells_kernel, total_blocks), "first_shells",
        (shape(n + 2 * HALF, pulses, size), kept), [SMEM, HBM, HBM, HBM],
        [
            pltpu.VMEM(shells.shape, BF16), pltpu.SMEM(band_rows.shape, jnp.int32),
            pltpu.SemaphoreType.DMA((6,)),
        ],
        mib=40,
    )
    second_shells = call(
        functools.partial(second_shells_kernel, total_blocks), "second_shells",
        partial_out(2 * pulses) + (kept,), [SMEM, SMEM, VMEM, VMEM, VMEM], [window(pulses)],
        aliases={4: 3},
    )
    prepare = call(
        prepare_kernel, "prepare",
        (shape(2, n, size), shape(n, size, 2 * size, dtype=BF16)), [VMEM] * 3,
    )
    combine = call(
        combine_kernel, "combine", (shape(pulses // 4, 2, n, size, dtype=BF16),) * 4,
        [SMEM] + [VMEM] * 4,
        [pltpu.VMEM((n, 2 * pulses, size), F32), pltpu.VMEM((pulses, 2, n, size), BF16)],
    )
    first_step = call(
        functools.partial(first_step_kernel, total_blocks), "first_step",
        (shape(n, pulses, size, dtype=BF16), shape(n, size)) + partial_out(pulses),
        [SMEM, SMEM] + [VMEM] * 6, [pltpu.VMEM((pulses * n, size), F32), window(pulses)],
    )
    second_step = call(
        second_step_kernel, "second_step",
        (shape(n, pulses, size, dtype=BF16), shape(pulses, n, size, dtype=BF16)),
        [SMEM] + [VMEM] * 10,
        [pltpu.VMEM((n * pulses, size), F32), pltpu.VMEM((n, pulses, size), F32)],
    )

    older = lax.ppermute(shells, "lag", [(i, i + 1) for i in range(lags - 1)])
    with jax.named_scope("shells"):
        window0, blocks = first_shells(place, band_rows, shells, blocks)
        main, first_out, second_out, blocks = second_shells(
            place, band_rows, older, window0, blocks
        )
    with jax.named_scope("halo"):
        first_in, second_in = trade(first_out, second_out)
    source, inverse_parts = prepare(incident, element_map, instant_inverse)
    shells, source = lax.optimization_barrier((shells, source))
    oldest = lax.ppermute(shells, "lag", [(i, (i + 2) % lags) for i in range(lags)])
    first_in, second_in, oldest = lax.optimization_barrier((first_in, second_in, oldest))
    keep, *sent = combine(place, main, first_in, second_in, source)
    with jax.named_scope("near"):
        quarter = added(keep, [exchange(part, d) for d, part in zip((1, 2, 3), sent)])
    with jax.named_scope("far"):
        quarter = added(quarter, [exchange(quarter, d) for d in (4, 8, 12)])
    with jax.named_scope("gather"):
        rest = [quarter] + [exchange(quarter, d) for d in (1, 2, 3)]
    current0, own0, extra, first_out, second_out = first_step(
        place, band_rows, *rest, inverse_parts, blocks
    )
    with jax.named_scope("halo_extra"):
        first_in, second_in = trade(first_out, second_out)
    aged, by_pulse1 = second_step(
        place, *rest, extra, first_in, second_in, inverse_parts, current0, oldest
    )
    with jax.named_scope("spread"):
        group = pulses // 4
        parts = [
            lax.ppermute(by_pulse1[group * g : group * (g + 1)], "lag", [(0, 4 * g)])
            for g in (1, 2, 3)
        ]
        leader = jnp.where(lag_index == 0, by_pulse1[:group], parts[0] + parts[1] + parts[2])
        parts = [
            lax.ppermute(leader[d], "lag", [(4 * g, 4 * g + d) for g in range(4)])
            for d in (1, 2, 3)
        ]
        own1 = jnp.where(lag_index % 4 == 0, leader[0], parts[0] + parts[1] + parts[2])
    currents = jnp.stack([own0.astype(BF16), own1])[:, :, None, :]
    return currents, aged[None]


def solution(mesh):
    placed = (
        P("lag", "col", None, None, None),
        P("lag", "col", None),
        P("lag", "col", None, None),
        P("col", None, None),
        P(None, "col", "lag", None),
        P("col", None),
    )
    return jax.shard_map(
        body,
        mesh=mesh,
        in_specs=placed,
        out_specs=(P(None, "col", "lag", None), P("lag", "col", None, None)),
        check_vma=False,
    )
```

time: 109 us -> 90 us (0.83)
  the two profiles are of different devices: /device:TPU:47 before, /device:TPU:46 now
where the time goes in v2:
time: 90 us; the launch traced here: 89.6 us
  waiting for transfers between devices  36.9 us (41%)
  starting transfers between devices  33.4 us (37%)
  Pallas kernels  16.1 us (18%)
  local copies, waits for them, and re-layouts  1.61 us (2%)
  between operations  0.9 us (1%)
    ppermute x9, starting transfers between devices, exchange(): return lax.ppermute(block, 'lag', [(i, i ^ distance) for i in range(16)])  17.7 us
    ppermute x9, waiting for transfers between devices, exchange(): return lax.ppermute(block, 'lag', [(i, i ^ distance) for i in range(16)])  15.7 us
    ppermute x3, waiting for transfers between devices, body(): lax.ppermute(leader[d], 'lag', [(4 * g, 4 * g + d) for g in range(4)])  12.5 us
    pallas_call x1, Pallas kernels, body(): window0, blocks = first_shells(place, band_rows, shells, blocks)  5.08 us
    ppermute x1, starting transfers between devices, body(): older = lax.ppermute(shells, 'lag', [(i, i + 1) for i in range(lags - 1)])  4.67 us
    ppermute x1, waiting for transfers between devices, body(): lax.ppermute(shells, 'lag', [(i, (i + 2) % lags) for i in range(lags)])  4.38 us
    ppermute x2, starting transfers between devices, trade(): lax.ppermute(second_out, 'col', others)  4.27 us
    ppermute x2, waiting for transfers between devices, trade(): lax.ppermute(second_out, 'col', others)  4.26 us
  transfers between devices with their start and end apart: 21, of which 11 were waited for; matrix products, arithmetic and copies ran while one was open for 0% of the time, Pallas kernels for 7%

profile of v2, /device:TPU:46, one launch (start us, length us, event | category | flops | bytes accessed | tf_op | source)
XLA Modules:
  0.0 89.6 jit_solution(9945034052382706056)
XLA Ops:
  0.6 4.7 %collective-permute-start = (bf16[32,16,128]{2,1,0:T(8,128)(2,1)}, bf16[32,16,128]{2,1,0:T(8,128)(2,1)S(1)}, u32[]{:S(2)}, u32[]{:S(2)}) collective-permute-start(bf16[32,16,128]{2,1,0:T(8,128)(2,1)} %bitcast.29), channel_id=1, source_target_pairs={{0,16},{16,32},{32,48},{48,64},{64,80},{80,96},{96,112},{112,128},... | collective-permute-start | bytes 393224 | tf_op jit(solution)/shard_map/ppermute | solution.py:283
  5.4 0.9 %copy-done.1 = bf16[1,32,16,128]{3,2,1,0:T(8,128)(2,1)S(1)} copy-done((bf16[1,32,16,128]{3,2,1,0:T(8,128)(2,1)S(1)}, bf16[1,32,16,128]{3,2,1,0:T(8,128)(2,1)}, u32[]{:S(2)}) %copy-start.1) | copy-done | bytes 131096
  6.3 0.7 copy-done.3
  7.0 5.1 %first_shells.1 = (f32[80,16,128]{2,1,0:T(8,128)S(1)}, bf16[32,8,128,128]{3,2,1,0:T(8,128)(2,1)S(1)}) custom-call(s32[3]{0:T(128)S(1)} %pad_add_fusion.place_ref, s32[8,32]{1,0:T(8,128)S(1)} %bitcast.32, bf16[32,16,128]{2,1,0:T(8,128)(2,1)S(1)} %bitcast.30, bf16[32,8,128,128]{3,2,1,0:T(8,128)(2,1)} %bitcast.35), custom_call_target="tpu_custom_call" | custom-call | tf_op jit(solution)/shard_map/shells/first_shells/pallas_call | solution.py:285
  12.1 3.2 %second_shells.1 = (f32[32,32,128]{2,1,0:T(8,128)S(1)}, bf16[24,32,128]{2,1,0:T(8,128)(2,1)S(1)}, bf16[24,32,128]{2,1,0:T(8,128)(2,1)S(1)}, bf16[32,8,128,128]{3,2,1,0:T(8,128)(2,1)S(1)}) custom-call(s32[3]{0:T(128)S(1)} %pad_add_fusion.place_ref, s32[8,32]{1,0:T(8,128)S(1)} %bitcast.33, ...), custom_call_target="tpu_custom_call", output_to_operand_aliasing={{3}: (4, {})} | custom-call | tf_op jit(solution)/shard_map/shells/second_shells/pallas_call | solution.py:286
  15.4 1.9 %collective-permute-start.2 = (bf16[24,32,128]{2,1,0:T(8,128)(2,1)S(1)}, bf16[24,32,128]{2,1,0:T(8,128)(2,1)S(1)}, u32[]{:S(2)}, u32[]{:S(2)}) collective-permute-start(bf16[24,32,128]{2,1,0:T(8,128)(2,1)S(1)} %get-tuple-element.30), channel_id=1, source_target_pairs={{1,2},{2,1},{3,4},{4,3},{5,6},{6,5},{7,8},{8,7},{9,10},{10,9},{11,... | collective-permute-start | bytes 589832 | tf_op jit(solution)/shard_map/halo/ppermute | solution.py:223
  17.3 0.9 prepare.1
  18.2 1.9 %collective-permute-start.3 = (bf16[32,16,128]{2,1,0:T(8,128)(2,1)S(1)}, bf16[32,16,128]{2,1,0:T(8,128)(2,1)S(1)}, u32[]{:S(2)}, u32[]{:S(2)}) collective-permute-start(bf16[32,16,128]{2,1,0:T(8,128)(2,1)S(1)} %bitcast.31), channel_id=1, source_target_pairs={{0,32},{16,48},{32,64},{48,80},{64,96},{80,112},{96,128},{112,144}... | collective-permute-start | bytes 393224 | tf_op jit(solution)/shard_map/ppermute | solution.py:293
  20.1 4.4 %collective-permute-done.3.oldest = bf16[32,16,128]{2,1,0:T(8,128)(2,1)S(1)} collective-permute-done((bf16[32,16,128]{2,1,0:T(8,128)(2,1)S(1)}, bf16[32,16,128]{2,1,0:T(8,128)(2,1)S(1)}, u32[]{:S(2)}, u32[]{:S(2)}) %collective-permute-start.3) | collective-permute-done | bytes 131104 | tf_op jit(solution)/shard_map/ppermute | solution.py:293
  24.5 1.0 %combine.1 = (bf16[4,2,32,128]{3,2,1,0:T(8,128)(2,1)S(1)}, bf16[4,2,32,128]{3,2,1,0:T(8,128)(2,1)S(1)}, bf16[4,2,32,128]{3,2,1,0:T(8,128)(2,1)S(1)}, bf16[4,2,32,128]{3,2,1,0:T(8,128)(2,1)S(1)}) custom-call(s32[3]{0:T(128)S(1)} %pad_add_fusion.place_ref, f32[32,32,128]{2,1,0:T(8,128)S(1)} %get-tuple-element.28.main, ...), custom_call_target="tpu_custom_call" | custom-call | tf_op jit(solution)/shard_map/combine/pallas_call | solution.py:295
  25.5 2.4 %collective-permute-start.4 = (bf16[4,2,32,128]{3,2,1,0:T(8,128)(2,1)S(1)}, bf16[4,2,32,128]{3,2,1,0:T(8,128)(2,1)S(1)}, u32[]{:S(2)}, u32[]{:S(2)}) collective-permute-start(bf16[4,2,32,128]{3,2,1,0:T(8,128)(2,1)S(1)} %get-tuple-element.37), channel_id=1, source_target_pairs={{0,16},{16,0},{32,48},{48,32},{64,80},{80,64},{96,112},{112,96},{1... | collective-permute-start | bytes 196616 | tf_op jit(solution)/shard_map/near/ppermute | solution.py:212
  27.9 3.7 %collective-permute-start.5 = (bf16[4,2,32,128]{3,2,1,0:T(8,128)(2,1)S(1)}, bf16[4,2,32,128]{3,2,1,0:T(8,128)(2,1)S(1)}, u32[]{:S(2)}, u32[]{:S(2)}) collective-permute-start(bf16[4,2,32,128]{3,2,1,0:T(8,128)(2,1)S(1)} %get-tuple-element.38), channel_id=1, source_target_pairs={{0,32},{16,48},{32,0},{48,16},{64,96},{80,112},{96,64},{112,80},{1... | collective-permute-start | bytes 196616 | tf_op jit(solution)/shard_map/near/ppermute | solution.py:212
  31.9 2.2 %collective-permute-done.5 = bf16[4,2,32,128]{3,2,1,0:T(8,128)(2,1)S(1)} collective-permute-done((bf16[4,2,32,128]{3,2,1,0:T(8,128)(2,1)S(1)}, bf16[4,2,32,128]{3,2,1,0:T(8,128)(2,1)S(1)}, u32[]{:S(2)}, u32[]{:S(2)}) %collective-permute-start.5) | collective-permute-done | bytes 65568 | tf_op jit(solution)/shard_map/near/ppermute | solution.py:212
  34.1 4.1 %collective-permute-done.6 = bf16[4,2,32,128]{3,2,1,0:T(8,128)(2,1)S(1)} collective-permute-done((bf16[4,2,32,128]{3,2,1,0:T(8,128)(2,1)S(1)}, bf16[4,2,32,128]{3,2,1,0:T(8,128)(2,1)S(1)}, u32[]{:S(2)}, u32[]{:S(2)}) %collective-permute-start.6) | collective-permute-done | bytes 65568 | tf_op jit(solution)/shard_map/near/ppermute | solution.py:212
  38.3 0.8 collective-permute-start.7
  39.1 4.3 %collective-permute-start.8 = (bf16[4,2,32,128]{3,2,1,0:T(8,128)(2,1)S(1)}, bf16[4,2,32,128]{3,2,1,0:T(8,128)(2,1)S(1)}, u32[]{:S(2)}, u32[]{:S(2)}) collective-permute-start(bf16[4,2,32,128]{3,2,1,0:T(8,128)(2,1)S(1)} %add_convert_fusion.1), channel_id=1, source_target_pairs={{0,128},{16,144},{32,160},{48,176},{64,192},{80,208},{96,224},{112... | collective-permute-start | bytes 196616 | tf_op jit(solution)/shard_map/far/ppermute | solution.py:212
  43.4 1.4 %collective-permute-start.9 = (bf16[4,2,32,128]{3,2,1,0:T(8,128)(2,1)S(1)}, bf16[4,2,32,128]{3,2,1,0:T(8,128)(2,1)S(1)}, u32[]{:S(2)}, u32[]{:S(2)}) collective-permute-start(bf16[4,2,32,128]{3,2,1,0:T(8,128)(2,1)S(1)} %add_convert_fusion.1), channel_id=1, source_target_pairs={{0,192},{16,208},{32,224},{48,240},{64,128},{80,144},{96,160},{112... | collective-permute-start | bytes 196616 | tf_op jit(solution)/shard_map/far/ppermute | solution.py:212
  44.9 3.1 %collective-permute-done.8 = bf16[4,2,32,128]{3,2,1,0:T(8,128)(2,1)S(1)} collective-permute-done((bf16[4,2,32,128]{3,2,1,0:T(8,128)(2,1)S(1)}, bf16[4,2,32,128]{3,2,1,0:T(8,128)(2,1)S(1)}, u32[]{:S(2)}, u32[]{:S(2)}) %collective-permute-start.8) | collective-permute-done | bytes 65568 | tf_op jit(solution)/shard_map/far/ppermute | solution.py:212
  48.0 2.6 %collective-permute-done.9 = bf16[4,2,32,128]{3,2,1,0:T(8,128)(2,1)S(1)} collective-permute-done((bf16[4,2,32,128]{3,2,1,0:T(8,128)(2,1)S(1)}, bf16[4,2,32,128]{3,2,1,0:T(8,128)(2,1)S(1)}, u32[]{:S(2)}, u32[]{:S(2)}) %collective-permute-start.9) | collective-permute-done | bytes 65568 | tf_op jit(solution)/shard_map/far/ppermute | solution.py:212
  50.6 1.8 %collective-permute-start.10 = (bf16[4,2,32,128]{3,2,1,0:T(8,128)(2,1)S(1)}, bf16[4,2,32,128]{3,2,1,0:T(8,128)(2,1)S(1)}, u32[]{:S(2)}, u32[]{:S(2)}) collective-permute-start(bf16[4,2,32,128]{3,2,1,0:T(8,128)(2,1)S(1)} %add_convert_fusion.rest0), channel_id=1, source_target_pairs={{0,16},{16,0},{32,48},{48,32},{64,80},{80,64},{96,112},{112,96},{1... | collective-permute-start | bytes 196616 | tf_op jit(solution)/shard_map/gather/ppermute | solution.py:212
  52.3 3.3 %collective-permute-start.12 = (bf16[4,2,32,128]{3,2,1,0:T(8,128)(2,1)S(1)}, bf16[4,2,32,128]{3,2,1,0:T(8,128)(2,1)S(1)}, u32[]{:S(2)}, u32[]{:S(2)}) collective-permute-start(bf16[4,2,32,128]{3,2,1,0:T(8,128)(2,1)S(1)} %add_convert_fusion.rest0), channel_id=1, source_target_pairs={{0,48},{16,32},{32,16},{48,0},{64,112},{80,96},{96,80},{112,64},{1... | collective-permute-start | bytes 196616 | tf_op jit(solution)/shard_map/gather/ppermute | solution.py:212
  55.6 0.8 collective-permute-done.10.rest1
  56.6 2.4 %collective-permute-done.12.rest3 = bf16[4,2,32,128]{3,2,1,0:T(8,128)(2,1)S(1)} collective-permute-done((bf16[4,2,32,128]{3,2,1,0:T(8,128)(2,1)S(1)}, bf16[4,2,32,128]{3,2,1,0:T(8,128)(2,1)S(1)}, u32[]{:S(2)}, u32[]{:S(2)}) %collective-permute-start.12) | collective-permute-done | bytes 65568 | tf_op jit(solution)/shard_map/gather/ppermute | solution.py:212
  59.0 3.9 %first_step.1 = (bf16[32,16,128]{2,1,0:T(8,128)(2,1)S(1)}, f32[32,128]{1,0:T(8,128)S(1)}, f32[32,16,128]{2,1,0:T(8,128)S(1)}, bf16[24,16,128]{2,1,0:T(8,128)(2,1)S(1)}, bf16[24,16,128]{2,1,0:T(8,128)(2,1)S(1)}) custom-call(s32[3]{0:T(128)S(1)} %pad_add_fusion.place_ref, s32[8,32]{1,0:T(8,128)S(1)} %bitcast.34, ...), custom_call_target="tpu_custom_call" | custom-call | tf_op jit(solution)/shard_map/first_step/pallas_call | solution.py:302
  63.0 2.3 %collective-permute-start.14 = (bf16[24,16,128]{2,1,0:T(8,128)(2,1)S(1)}, bf16[24,16,128]{2,1,0:T(8,128)(2,1)S(1)}, u32[]{:S(2)}, u32[]{:S(2)}) collective-permute-start(bf16[24,16,128]{2,1,0:T(8,128)(2,1)S(1)} %get-tuple-element.45), channel_id=1, source_target_pairs={{1,2},{2,1},{3,4},{4,3},{5,6},{6,5},{7,8},{8,7},{9,10},{10,9},{11,... | collective-permute-start | bytes 294920 | tf_op jit(solution)/shard_map/halo_extra/ppermute | solution.py:223
  65.3 4.3 %collective-permute-done.14.second_in = bf16[24,16,128]{2,1,0:T(8,128)(2,1)S(1)} collective-permute-done((bf16[24,16,128]{2,1,0:T(8,128)(2,1)S(1)}, bf16[24,16,128]{2,1,0:T(8,128)(2,1)S(1)}, u32[]{:S(2)}, u32[]{:S(2)}) %collective-permute-start.14) | collective-permute-done | bytes 98336 | tf_op jit(solution)/shard_map/halo_extra/ppermute | solution.py:223
  69.6 2.1 %second_step.1 = (bf16[32,16,128]{2,1,0:T(8,128)(2,1)}, bf16[16,32,128]{2,1,0:T(8,128)(2,1)S(1)}) custom-call(s32[3]{0:T(128)S(1)} %pad_add_fusion.place_ref, bf16[4,2,32,128]{3,2,1,0:T(8,128)(2,1)S(1)} %add_convert_fusion.rest0, bf16[4,2,32,128]{3,2,1,0:T(8,128)(2,1)S(1)} %collective-permute-done.10.rest1, ...), custom_call_target="tpu_custom_call" | custom-call | tf_op jit(solution)/shard_map/second_step/pallas_call | solution.py:307
  71.7 0.7 collective-permute-start.15
  72.4 0.7 collective-permute-start.16
  73.0 0.7 collective-permute-start.17
  75.1 1.3 %collective-permute-start.20 = (bf16[32,128]{1,0:T(8,128)(2,1)S(1)}, bf16[32,128]{1,0:T(8,128)(2,1)S(1)}, u32[]{:S(2)}, u32[]{:S(2)}) collective-permute-start(bf16[32,128]{1,0:T(8,128)(2,1)S(1)} %get-tuple-element.56), channel_id=1, source_target_pairs={{0,48},{64,112},{128,176},{192,240},{1,49},{65,113},{129,177},{193... | collective-permute-start | bytes 24584 | tf_op jit(solution)/shard_map/spread/ppermute | solution.py:318
  76.4 12.5 %collective-permute-done.20 = bf16[32,128]{1,0:T(8,128)(2,1)S(1)} collective-permute-done((bf16[32,128]{1,0:T(8,128)(2,1)S(1)}, bf16[32,128]{1,0:T(8,128)(2,1)S(1)}, u32[]{:S(2)}, u32[]{:S(2)}) %collective-permute-start.20) | collective-permute-done | bytes 8224 | tf_op jit(solution)/shard_map/spread/ppermute | solution.py:318
  (35 shorter events, 2.8 us)
Async XLA Ops:
  0.6 11.5 %collective-permute-start = (bf16[32,16,128]{2,1,0:T(8,128)(2,1)}, bf16[32,16,128]{2,1,0:T(8,128)(2,1)S(1)}, u32[]{:S(2)}, u32[]{:S(2)}) collective-permute-start(bf16[32,16,128]{2,1,0:T(8,128)(2,1)} %bitcast.29), channel_id=1, source_target_pairs={{0,16},{16,32},{32,48},{48,64},{64,80},{80,96},{96,112},{112,128},... | collective-permute-start | bytes 393224 | tf_op jit(solution)/shard_map/ppermute | solution.py:283
  5.4 0.9 %copy-start.1 = (bf16[1,32,16,128]{3,2,1,0:T(8,128)(2,1)S(1)}, bf16[1,32,16,128]{3,2,1,0:T(8,128)(2,1)}, u32[]{:S(2)}) copy-start(bf16[1,32,16,128]{3,2,1,0:T(8,128)(2,1)} %param.8) | copy-start | bytes 393220
  6.3 0.7 copy-start.3
  7.0 10.3 %copy-start = (f32[32,128,128]{2,1,0:T(8,128)S(1)}, f32[32,128,128]{2,1,0:T(8,128)}, u32[]{:S(2)}) copy-start(f32[32,128,128]{2,1,0:T(8,128)} %inverse.1) | copy-start | bytes 6291460
  7.0 10.3 %copy-start.2 = (f32[2,32,1,256]{3,2,1,0:T(1,128)S(1)}, f32[2,32,1,256]{3,2,1,0:T(1,128)}, u32[]{:S(2)}) copy-start(f32[2,32,1,256]{3,2,1,0:T(1,128)} %incident.1) | copy-start | bytes 196612
  7.0 10.3 %copy-start.4 = (s32[32,256]{1,0:T(8,128)S(1)}, s32[32,256]{1,0:T(8,128)}, u32[]{:S(2)}) copy-start(s32[32,256]{1,0:T(8,128)} %element_map.1) | copy-start | bytes 98308
  15.3 9.2 %collective-permute-start.1 = (bf16[24,32,128]{2,1,0:T(8,128)(2,1)S(1)}, bf16[24,32,128]{2,1,0:T(8,128)(2,1)S(1)}, u32[]{:S(2)}, u32[]{:S(2)}) collective-permute-start(bf16[24,32,128]{2,1,0:T(8,128)(2,1)S(1)} %get-tuple-element.29), channel_id=1, source_target_pairs={{0,1},{1,0},{2,3},{3,2},{4,5},{5,4},{6,7},{7,6},{8,9},{9,8},{10,11... | collective-permute-start | bytes 589832 | tf_op jit(solution)/shard_map/halo/ppermute | solution.py:223
  15.4 9.1 %collective-permute-start.2 = (bf16[24,32,128]{2,1,0:T(8,128)(2,1)S(1)}, bf16[24,32,128]{2,1,0:T(8,128)(2,1)S(1)}, u32[]{:S(2)}, u32[]{:S(2)}) collective-permute-start(bf16[24,32,128]{2,1,0:T(8,128)(2,1)S(1)} %get-tuple-element.30), channel_id=1, source_target_pairs={{1,2},{2,1},{3,4},{4,3},{5,6},{6,5},{7,8},{8,7},{9,10},{10,9},{11,... | collective-permute-start | bytes 589832 | tf_op jit(solution)/shard_map/halo/ppermute | solution.py:223
  18.2 6.3 %collective-permute-start.3 = (bf16[32,16,128]{2,1,0:T(8,128)(2,1)S(1)}, bf16[32,16,128]{2,1,0:T(8,128)(2,1)S(1)}, u32[]{:S(2)}, u32[]{:S(2)}) collective-permute-start(bf16[32,16,128]{2,1,0:T(8,128)(2,1)S(1)} %bitcast.31), channel_id=1, source_target_pairs={{0,32},{16,48},{32,64},{48,80},{64,96},{80,112},{96,128},{112,144}... | collective-permute-start | bytes 393224 | tf_op jit(solution)/shard_map/ppermute | solution.py:293
  25.5 6.4 %collective-permute-start.4 = (bf16[4,2,32,128]{3,2,1,0:T(8,128)(2,1)S(1)}, bf16[4,2,32,128]{3,2,1,0:T(8,128)(2,1)S(1)}, u32[]{:S(2)}, u32[]{:S(2)}) collective-permute-start(bf16[4,2,32,128]{3,2,1,0:T(8,128)(2,1)S(1)} %get-tuple-element.37), channel_id=1, source_target_pairs={{0,16},{16,0},{32,48},{48,32},{64,80},{80,64},{96,112},{112,96},{1... | collective-permute-start | bytes 196616 | tf_op jit(solution)/shard_map/near/ppermute | solution.py:212
  27.9 6.2 %collective-permute-start.5 = (bf16[4,2,32,128]{3,2,1,0:T(8,128)(2,1)S(1)}, bf16[4,2,32,128]{3,2,1,0:T(8,128)(2,1)S(1)}, u32[]{:S(2)}, u32[]{:S(2)}) collective-permute-start(bf16[4,2,32,128]{3,2,1,0:T(8,128)(2,1)S(1)} %get-tuple-element.38), channel_id=1, source_target_pairs={{0,32},{16,48},{32,0},{48,16},{64,96},{80,112},{96,64},{112,80},{1... | collective-permute-start | bytes 196616 | tf_op jit(solution)/shard_map/near/ppermute | solution.py:212
  31.6 6.7 %collective-permute-start.6 = (bf16[4,2,32,128]{3,2,1,0:T(8,128)(2,1)S(1)}, bf16[4,2,32,128]{3,2,1,0:T(8,128)(2,1)S(1)}, u32[]{:S(2)}, u32[]{:S(2)}) collective-permute-start(bf16[4,2,32,128]{3,2,1,0:T(8,128)(2,1)S(1)} %get-tuple-element.39), channel_id=1, source_target_pairs={{0,48},{16,32},{32,16},{48,0},{64,112},{80,96},{96,80},{112,64},{1... | collective-permute-start | bytes 196616 | tf_op jit(solution)/shard_map/near/ppermute | solution.py:212
  38.3 6.6 %collective-permute-start.7 = (bf16[4,2,32,128]{3,2,1,0:T(8,128)(2,1)S(1)}, bf16[4,2,32,128]{3,2,1,0:T(8,128)(2,1)S(1)}, u32[]{:S(2)}, u32[]{:S(2)}) collective-permute-start(bf16[4,2,32,128]{3,2,1,0:T(8,128)(2,1)S(1)} %add_convert_fusion.1), channel_id=1, source_target_pairs={{0,64},{16,80},{32,96},{48,112},{64,0},{80,16},{96,32},{112,48},{1... | collective-permute-start | bytes 196616 | tf_op jit(solution)/shard_map/far/ppermute | solution.py:212
  39.1 8.9 %collective-permute-start.8 = (bf16[4,2,32,128]{3,2,1,0:T(8,128)(2,1)S(1)}, bf16[4,2,32,128]{3,2,1,0:T(8,128)(2,1)S(1)}, u32[]{:S(2)}, u32[]{:S(2)}) collective-permute-start(bf16[4,2,32,128]{3,2,1,0:T(8,128)(2,1)S(1)} %add_convert_fusion.1), channel_id=1, source_target_pairs={{0,128},{16,144},{32,160},{48,176},{64,192},{80,208},{96,224},{112... | collective-permute-start | bytes 196616 | tf_op jit(solution)/shard_map/far/ppermute | solution.py:212
  43.4 7.1 %collective-permute-start.9 = (bf16[4,2,32,128]{3,2,1,0:T(8,128)(2,1)S(1)}, bf16[4,2,32,128]{3,2,1,0:T(8,128)(2,1)S(1)}, u32[]{:S(2)}, u32[]{:S(2)}) collective-permute-start(bf16[4,2,32,128]{3,2,1,0:T(8,128)(2,1)S(1)} %add_convert_fusion.1), channel_id=1, source_target_pairs={{0,192},{16,208},{32,224},{48,240},{64,128},{80,144},{96,160},{112... | collective-permute-start | bytes 196616 | tf_op jit(solution)/shard_map/far/ppermute | solution.py:212
  50.6 5.9 %collective-permute-start.10 = (bf16[4,2,32,128]{3,2,1,0:T(8,128)(2,1)S(1)}, bf16[4,2,32,128]{3,2,1,0:T(8,128)(2,1)S(1)}, u32[]{:S(2)}, u32[]{:S(2)}) collective-permute-start(bf16[4,2,32,128]{3,2,1,0:T(8,128)(2,1)S(1)} %add_convert_fusion.rest0), channel_id=1, source_target_pairs={{0,16},{16,0},{32,48},{48,32},{64,80},{80,64},{96,112},{112,96},{1... | collective-permute-start | bytes 196616 | tf_op jit(solution)/shard_map/gather/ppermute | solution.py:212
  52.3 4.3 %collective-permute-start.11 = (bf16[4,2,32,128]{3,2,1,0:T(8,128)(2,1)S(1)}, bf16[4,2,32,128]{3,2,1,0:T(8,128)(2,1)S(1)}, u32[]{:S(2)}, u32[]{:S(2)}) collective-permute-start(bf16[4,2,32,128]{3,2,1,0:T(8,128)(2,1)S(1)} %add_convert_fusion.rest0), channel_id=1, source_target_pairs={{0,32},{16,48},{32,0},{48,16},{64,96},{80,112},{96,64},{112,80},{1... | collective-permute-start | bytes 196616 | tf_op jit(solution)/shard_map/gather/ppermute | solution.py:212
  52.3 6.7 %collective-permute-start.12 = (bf16[4,2,32,128]{3,2,1,0:T(8,128)(2,1)S(1)}, bf16[4,2,32,128]{3,2,1,0:T(8,128)(2,1)S(1)}, u32[]{:S(2)}, u32[]{:S(2)}) collective-permute-start(bf16[4,2,32,128]{3,2,1,0:T(8,128)(2,1)S(1)} %add_convert_fusion.rest0), channel_id=1, source_target_pairs={{0,48},{16,32},{32,16},{48,0},{64,112},{80,96},{96,80},{112,64},{1... | collective-permute-start | bytes 196616 | tf_op jit(solution)/shard_map/gather/ppermute | solution.py:212
  62.9 2.5 %collective-permute-start.13 = (bf16[24,16,128]{2,1,0:T(8,128)(2,1)S(1)}, bf16[24,16,128]{2,1,0:T(8,128)(2,1)S(1)}, u32[]{:S(2)}, u32[]{:S(2)}) collective-permute-start(bf16[24,16,128]{2,1,0:T(8,128)(2,1)S(1)} %get-tuple-element.44), channel_id=1, source_target_pairs={{0,1},{1,0},{2,3},{3,2},{4,5},{5,4},{6,7},{7,6},{8,9},{9,8},{10,11... | collective-permute-start | bytes 294920 | tf_op jit(solution)/shard_map/halo_extra/ppermute | solution.py:223
  63.0 6.6 %collective-permute-start.14 = (bf16[24,16,128]{2,1,0:T(8,128)(2,1)S(1)}, bf16[24,16,128]{2,1,0:T(8,128)(2,1)S(1)}, u32[]{:S(2)}, u32[]{:S(2)}) collective-permute-start(bf16[24,16,128]{2,1,0:T(8,128)(2,1)S(1)} %get-tuple-element.45), channel_id=1, source_target_pairs={{1,2},{2,1},{3,4},{4,3},{5,6},{6,5},{7,8},{8,7},{9,10},{10,9},{11,... | collective-permute-start | bytes 294920 | tf_op jit(solution)/shard_map/halo_extra/ppermute | solution.py:223
  71.7 2.0 %collective-permute-start.15 = (bf16[4,32,128]{2,1,0:T(8,128)(2,1)S(1)}, bf16[4,32,128]{2,1,0:T(8,128)(2,1)S(1)}, u32[]{:S(2)}, u32[]{:S(2)}) collective-permute-start(bf16[4,32,128]{2,1,0:T(8,128)(2,1)S(1)} %get-tuple-element.54), channel_id=1, source_target_pairs={{0,64},{1,65},{2,66},{3,67},{4,68},{5,69},{6,70},{7,71},{8,72},{9,... | collective-permute-start | bytes 98312 | tf_op jit(solution)/shard_map/spread/ppermute | solution.py:313
  72.4 1.4 %collective-permute-start.16 = (bf16[4,32,128]{2,1,0:T(8,128)(2,1)S(1)}, bf16[4,32,128]{2,1,0:T(8,128)(2,1)S(1)}, u32[]{:S(2)}, u32[]{:S(2)}) collective-permute-start(bf16[4,32,128]{2,1,0:T(8,128)(2,1)S(1)} %get-tuple-element.52), channel_id=1, source_target_pairs={{0,128},{1,129},{2,130},{3,131},{4,132},{5,133},{6,134},{7,135},{8... | collective-permute-start | bytes 98312 | tf_op jit(solution)/shard_map/spread/ppermute | solution.py:313
  73.0 0.7 collective-permute-start.17
  73.8 2.7 %collective-permute-start.18 = (bf16[32,128]{1,0:T(8,128)(2,1)S(1)}, bf16[32,128]{1,0:T(8,128)(2,1)S(1)}, u32[]{:S(2)}, u32[]{:S(2)}) collective-permute-start(bf16[32,128]{1,0:T(8,128)(2,1)S(1)} %get-tuple-element.57), channel_id=1, source_target_pairs={{0,16},{64,80},{128,144},{192,208},{1,17},{65,81},{129,145},{193,2... | collective-permute-start | bytes 24584 | tf_op jit(solution)/shard_map/spread/ppermute | solution.py:318
  74.4 2.0 %collective-permute-start.19 = (bf16[32,128]{1,0:T(8,128)(2,1)S(1)}, bf16[32,128]{1,0:T(8,128)(2,1)S(1)}, u32[]{:S(2)}, u32[]{:S(2)}) collective-permute-start(bf16[32,128]{1,0:T(8,128)(2,1)S(1)} %get-tuple-element.55), channel_id=1, source_target_pairs={{0,32},{64,96},{128,160},{192,224},{1,33},{65,97},{129,161},{193,2... | collective-permute-start | bytes 24584 | tf_op jit(solution)/shard_map/spread/ppermute | solution.py:318
  75.1 13.9 %collective-permute-start.20 = (bf16[32,128]{1,0:T(8,128)(2,1)S(1)}, bf16[32,128]{1,0:T(8,128)(2,1)S(1)}, u32[]{:S(2)}, u32[]{:S(2)}) collective-permute-start(bf16[32,128]{1,0:T(8,128)(2,1)S(1)} %get-tuple-element.56), channel_id=1, source_target_pairs={{0,48},{64,112},{128,176},{192,240},{1,49},{65,113},{129,177},{193... | collective-permute-start | bytes 24584 | tf_op jit(solution)/shard_map/spread/ppermute | solution.py:318

commit v3 on v2

--- a/solution.py
+++ b/solution.py
@@ -51,11 +51,15 @@
         second_out[:, rows] = window[pl.ds((1 - even) * (HALF + n), HALF)].astype(BF16)
 
 
-def take_in(place_ref, main, first_in, second_in):
-    n = main.shape[0]
-    even = 1 - place_ref[2]
-    main[pl.ds(even * (n - HALF), HALF)] += first_in[...].astype(F32)
-    main[pl.ds((1 - even) * (n - HALF), HALF)] += second_in[...].astype(F32)
+def shared(place_ref, b, n, first_in, second_in):
+    odd = place_ref[2] == 1
+    value = 0.0
+    if b < HALF:
+        value = value + jnp.where(odd, first_in[b], second_in[b]).astype(F32)
+    if b >= n - HALF:
+        edge = b - (n - HALF)
+        value = value + jnp.where(odd, second_in[edge], first_in[edge]).astype(F32)
+    return value
 
 
 def first_shells_kernel(
@@ -88,7 +92,14 @@
     total_blocks, place_ref, offsets_ref, older, first_window, blocks,
     main, first_out, second_out, kept, window,
 ):
-    banded(place_ref, offsets_ref, lambda c: older[c], blocks, window, total_blocks, 2)
+    @pl.when(place_ref[1] > 0)
+    def _():
+        banded(place_ref, offsets_ref, lambda c: older[c], blocks, window, total_blocks, 2)
+
+    @pl.when(place_ref[1] == 0)
+    def _():
+        window[...] = jnp.zeros_like(window)
+
     hand_out(place_ref, (first_window, window), main, first_out, second_out)
 
 
@@ -113,19 +124,17 @@
 
 
 def combine_kernel(
-    place_ref, main, first_in, second_in, source, keep, send1, send2, send3, total, by_pulse
+    place_ref, main, first_in, second_in, source, keep, send1, send2, send3, flat, by_pulse
 ):
     n, rows, size = main.shape
     pulses = rows // 2
     line = lax.broadcasted_iota(jnp.int32, (rows, size), 0)
     for b in range(n):
-        value = main[b]
+        value = main[b] + shared(place_ref, b, n, first_in, second_in)
         for t in range(2):
             mine = line == place_ref[1] + t * pulses
             value = value - jnp.where(mine, source[t, b : b + 1, :], 0.0)
-        total[b] = value
-    take_in(place_ref, total, first_in, second_in)
-    flat = total.reshape(n * rows, size)
+        flat[b * rows : (b + 1) * rows, :] = value
     for p in range(pulses):
         for t in range(2):
             by_pulse[p, t] = flat[pl.ds(t * pulses + p, n, stride=rows), :].astype(BF16)
@@ -166,25 +175,30 @@
         new = solve(scratch[pl.ds(b, pulses, stride=n), :], inverse_parts[b])
         current[b] = new.astype(BF16)
         own_pulse[b : b + 1, :] = jnp.sum(jnp.where(mine, new, 0.0), axis=0, keepdims=True)
-    banded(place_ref, offsets_ref, lambda c: current[c], blocks, window, total_blocks, 2)
-    hand_out(place_ref, (window,), main, first_out, second_out)
+
+    @pl.when(place_ref[1] == 0)
+    def _():
+        banded(place_ref, offsets_ref, lambda c: current[c], blocks, window, total_blocks, 2)
+        hand_out(place_ref, (window,), main, first_out, second_out)
 
 
 def second_step_kernel(
     place_ref, rest0, rest1, rest2, rest3, main, first_in, second_in, inverse_parts, current0, oldest,
-    aged, by_pulse, scratch, total,
+    aged, by_pulse, scratch,
 ):
     n, pulses, size = aged.shape
-    total[...] = main[...]
-    take_in(place_ref, total, first_in, second_in)
-    by_row(place_ref, (rest0, rest1, rest2, rest3), 1, scratch)
-    for b in range(n):
-        value = scratch[pl.ds(b, pulses, stride=n), :] + total[b]
-        new = solve(value, inverse_parts[b])
-        aged[b] = new.astype(BF16)
-        scratch[pl.ds(b, pulses, stride=n), :] = new
-    for p in range(pulses):
-        by_pulse[p] = scratch[p * n : (p + 1) * n, :].astype(BF16)
+
+    @pl.when(place_ref[1] == 0)
+    def _():
+        by_row(place_ref, (rest0, rest1, rest2, rest3), 1, scratch)
+        for b in range(n):
+            value = scratch[pl.ds(b, pulses, stride=n), :] + main[b]
+            value = value + shared(place_ref, b, n, first_in, second_in)
+            new = solve(value, inverse_parts[b])
+            aged[b] = new.astype(BF16)
+            scratch[pl.ds(b, pulses, stride=n), :] = new
+        for p in range(pulses):
+            by_pulse[p] = scratch[p * n : (p + 1) * n, :].astype(BF16)
 
     @pl.when(place_ref[1] == 1)
     def _():
@@ -219,7 +233,7 @@
 def trade(first_out, second_out):
     n = lax.axis_size("col")
     pairs = [(i, i ^ 1) for i in range(n)]
-    others = [(i, i + 1 if i % 2 else i - 1) for i in range(1, n - 1)]
+    others = [(i, (i + 1 if i % 2 else i - 1) % n) for i in range(n)]
     return lax.ppermute(first_out, "col", pairs), lax.ppermute(second_out, "col", others)
 
 
@@ -266,7 +280,7 @@
     combine = call(
         combine_kernel, "combine", (shape(pulses // 4, 2, n, size, dtype=BF16),) * 4,
         [SMEM] + [VMEM] * 4,
-        [pltpu.VMEM((n, 2 * pulses, size), F32), pltpu.VMEM((pulses, 2, n, size), BF16)],
+        [pltpu.VMEM((n * 2 * pulses, size), F32), pltpu.VMEM((pulses, 2, n, size), BF16)],
     )
     first_step = call(
         functools.partial(first_step_kernel, total_blocks), "first_step",
@@ -277,10 +291,10 @@
         second_step_kernel, "second_step",
         (shape(n, pulses, size, dtype=BF16), shape(pulses, n, size, dtype=BF16)),
         [SMEM] + [VMEM] * 10,
-        [pltpu.VMEM((n * pulses, size), F32), pltpu.VMEM((n, pulses, size), F32)],
-    )
-
-    older = lax.ppermute(shells, "lag", [(i, i + 1) for i in range(lags - 1)])
+        [pltpu.VMEM((n * pulses, size), F32)],
+    )
+
+    older = lax.ppermute(shells, "lag", [(i, (i + 1) % lags) for i in range(lags)])
     with jax.named_scope("shells"):
         window0, blocks = first_shells(place, band_rows, shells, blocks)
         main, first_out, second_out, blocks = second_shells(
@@ -289,9 +303,6 @@
     with jax.named_scope("halo"):
         first_in, second_in = trade(first_out, second_out)
     source, inverse_parts = prepare(incident, element_map, instant_inverse)
-    shells, source = lax.optimization_barrier((shells, source))
-    oldest = lax.ppermute(shells, "lag", [(i, (i + 2) % lags) for i in range(lags)])
-    first_in, second_in, oldest = lax.optimization_barrier((first_in, second_in, oldest))
     keep, *sent = combine(place, main, first_in, second_in, source)
     with jax.named_scope("near"):
         quarter = added(keep, [exchange(part, d) for d, part in zip((1, 2, 3), sent)])
@@ -302,6 +313,8 @@
     current0, own0, extra, first_out, second_out = first_step(
         place, band_rows, *rest, inverse_parts, blocks
     )
+    shells, current0 = lax.optimization_barrier((shells, current0))
+    oldest = lax.ppermute(shells, "lag", [(i, (i + 2) % lags) for i in range(lags)])
     with jax.named_scope("halo_extra"):
         first_in, second_in = trade(first_out, second_out)
     aged, by_pulse1 = second_step(
@@ -309,16 +322,14 @@
     )
     with jax.named_scope("spread"):
         group = pulses // 4
-        parts = [
-            lax.ppermute(by_pulse1[group * g : group * (g + 1)], "lag", [(0, 4 * g)])
-            for g in (1, 2, 3)
-        ]
-        leader = jnp.where(lag_index == 0, by_pulse1[:group], parts[0] + parts[1] + parts[2])
-        parts = [
-            lax.ppermute(leader[d], "lag", [(4 * g, 4 * g + d) for g in range(4)])
-            for d in (1, 2, 3)
-        ]
-        own1 = jnp.where(lag_index % 4 == 0, leader[0], parts[0] + parts[1] + parts[2])
+        leader = by_pulse1[:group]
+        for g in (1, 2, 3):
+            part = lax.ppermute(by_pulse1[group * g : group * (g + 1)], "lag", [(0, 4 * g)])
+            leader = jnp.where(lag_index == 4 * g, part, leader)
+        own1 = leader[0]
+        for d in (1, 2, 3):
+            part = lax.ppermute(leader[d], "lag", [(4 * g, 4 * g + d) for g in range(4)])
+            own1 = jnp.where(lag_index % 4 == d, part, own1)
     currents = jnp.stack([own0.astype(BF16), own1])[:, :, None, :]
     return currents, aged[None]
 

time: 90 us -> 84 us (0.933)
  the two profiles are of different devices: /device:TPU:46 before, /device:TPU:4 now
where the time goes in v3:
time: 84 us; the launch traced here: 83.7 us
  starting transfers between devices  34.4 us (41%)
  waiting for transfers between devices  33.3 us (40%)
  Pallas kernels  12.8 us (15%)
  local copies, waits for them, and re-layouts  1.61 us (2%)
    ppermute x9, starting transfers between devices, exchange(): return lax.ppermute(block, 'lag', [(i, i ^ distance) for i in range(16)])  18.1 us
    ppermute x9, waiting for transfers between devices, exchange(): return lax.ppermute(block, 'lag', [(i, i ^ distance) for i in range(16)])  14.9 us
    ppermute x3, waiting for transfers between devices, body(): lax.ppermute(leader[d], 'lag', [(4 * g, 4 * g + d) for g in range(4)])  10.6 us
    ppermute x2, waiting for transfers between devices, trade(): lax.ppermute(second_out, 'col', others)  7.83 us
    ppermute x2, starting transfers between devices, trade(): lax.ppermute(second_out, 'col', others)  7.77 us
    pallas_call x1, Pallas kernels, body(): window0, blocks = first_shells(place, band_rows, shells, blocks)  5.1 us
    pallas_call x1, Pallas kernels, body(): second_shells(place, band_rows, older, window0, blocks)  3.19 us
    ppermute x3, starting transfers between devices, body(): lax.ppermute(leader[d], 'lag', [(4 * g, 4 * g + d) for g in range(4)])  2.62 us
  transfers between devices with their start and end apart: 21, of which 9 were waited for; matrix products, arithmetic and copies ran while one was open for 0% of the time, Pallas kernels for 7%

profile of v3, /device:TPU:4, one launch (start us, length us, event | category | flops | bytes accessed | tf_op | source)
XLA Modules:
  0.0 83.7 jit_solution(1704593926843617841)
XLA Ops:
  0.6 1.9 %collective-permute-start = (bf16[32,16,128]{2,1,0:T(8,128)(2,1)}, bf16[32,16,128]{2,1,0:T(8,128)(2,1)S(1)}, u32[]{:S(2)}, u32[]{:S(2)}) collective-permute-start(bf16[32,16,128]{2,1,0:T(8,128)(2,1)} %bitcast.33), channel_id=1, source_target_pairs={{0,16},{16,32},{32,48},{48,64},{64,80},{80,96},{96,112},{112,128},... | collective-permute-start | bytes 393224 | tf_op jit(solution)/shard_map/ppermute | solution.py:297
  2.6 0.9 %copy-done.1 = bf16[1,32,16,128]{3,2,1,0:T(8,128)(2,1)S(1)} copy-done((bf16[1,32,16,128]{3,2,1,0:T(8,128)(2,1)S(1)}, bf16[1,32,16,128]{3,2,1,0:T(8,128)(2,1)}, u32[]{:S(2)}) %copy-start.1) | copy-done | bytes 131096
  3.6 0.7 copy-done.3
  4.2 5.1 %first_shells.1 = (f32[80,16,128]{2,1,0:T(8,128)S(1)}, bf16[32,8,128,128]{3,2,1,0:T(8,128)(2,1)S(1)}) custom-call(s32[3]{0:T(128)S(1)} %pad_add_fusion.place_ref, s32[8,32]{1,0:T(8,128)S(1)} %bitcast.36, bf16[32,16,128]{2,1,0:T(8,128)(2,1)S(1)} %bitcast.34, bf16[32,8,128,128]{3,2,1,0:T(8,128)(2,1)} %bitcast.39), custom_call_target="tpu_custom_call" | custom-call | tf_op jit(solution)/shard_map/shells/first_shells/pallas_call | solution.py:299
  9.4 3.2 %second_shells.1 = (f32[32,32,128]{2,1,0:T(8,128)S(1)}, bf16[24,32,128]{2,1,0:T(8,128)(2,1)S(1)}, bf16[24,32,128]{2,1,0:T(8,128)(2,1)S(1)}, bf16[32,8,128,128]{3,2,1,0:T(8,128)(2,1)S(1)}) custom-call(s32[3]{0:T(128)S(1)} %pad_add_fusion.place_ref, s32[8,32]{1,0:T(8,128)S(1)} %bitcast.37, ...), custom_call_target="tpu_custom_call", output_to_operand_aliasing={{3}: (4, {})} | custom-call | tf_op jit(solution)/shard_map/shells/second_shells/pallas_call | solution.py:300
  12.7 4.6 %collective-permute-start.2 = (bf16[24,32,128]{2,1,0:T(8,128)(2,1)S(1)}, bf16[24,32,128]{2,1,0:T(8,128)(2,1)S(1)}, u32[]{:S(2)}, u32[]{:S(2)}) collective-permute-start(bf16[24,32,128]{2,1,0:T(8,128)(2,1)S(1)} %get-tuple-element.27), channel_id=1, source_target_pairs={{0,15},{1,2},{2,1},{3,4},{4,3},{5,6},{6,5},{7,8},{8,7},{9,10},{10,... | collective-permute-start | bytes 589832 | tf_op jit(solution)/shard_map/halo/ppermute | solution.py:237
  17.3 0.9 %prepare.1 = (f32[2,32,128]{2,1,0:T(8,128)S(1)}, bf16[32,128,256]{2,1,0:T(8,128)(2,1)S(1)}) custom-call(f32[2,32,1,256]{3,2,1,0:T(1,128)S(1)} %copy-done.2, s32[32,256]{1,0:T(8,128)S(1)} %copy-done.4, f32[32,128,128]{2,1,0:T(8,128)S(1)} %copy-done), custom_call_target="tpu_custom_call" | custom-call | tf_op jit(solution)/shard_map/prepare/pallas_call | solution.py:305
  18.1 4.3 %collective-permute-done.2.second_in = bf16[24,32,128]{2,1,0:T(8,128)(2,1)S(1)} collective-permute-done((bf16[24,32,128]{2,1,0:T(8,128)(2,1)S(1)}, bf16[24,32,128]{2,1,0:T(8,128)(2,1)S(1)}, u32[]{:S(2)}, u32[]{:S(2)}) %collective-permute-start.2) | collective-permute-done | bytes 196640 | tf_op jit(solution)/shard_map/halo/ppermute | solution.py:237
  22.4 1.0 %combine.1 = (bf16[4,2,32,128]{3,2,1,0:T(8,128)(2,1)S(1)}, bf16[4,2,32,128]{3,2,1,0:T(8,128)(2,1)S(1)}, bf16[4,2,32,128]{3,2,1,0:T(8,128)(2,1)S(1)}, bf16[4,2,32,128]{3,2,1,0:T(8,128)(2,1)S(1)}) custom-call(s32[3]{0:T(128)S(1)} %pad_add_fusion.place_ref, f32[32,32,128]{2,1,0:T(8,128)S(1)} %get-tuple-element.25.main, ...), custom_call_target="tpu_custom_call" | custom-call | tf_op jit(solution)/shard_map/combine/pallas_call | solution.py:306
  23.7 2.2 %collective-permute-start.4 = (bf16[4,2,32,128]{3,2,1,0:T(8,128)(2,1)S(1)}, bf16[4,2,32,128]{3,2,1,0:T(8,128)(2,1)S(1)}, u32[]{:S(2)}, u32[]{:S(2)}) collective-permute-start(bf16[4,2,32,128]{3,2,1,0:T(8,128)(2,1)S(1)} %get-tuple-element.31), channel_id=1, source_target_pairs={{0,32},{16,48},{32,0},{48,16},{64,96},{80,112},{96,64},{112,80},{1... | collective-permute-start | bytes 196616 | tf_op jit(solution)/shard_map/near/ppermute | solution.py:226
  25.9 2.7 %collective-permute-start.5 = (bf16[4,2,32,128]{3,2,1,0:T(8,128)(2,1)S(1)}, bf16[4,2,32,128]{3,2,1,0:T(8,128)(2,1)S(1)}, u32[]{:S(2)}, u32[]{:S(2)}) collective-permute-start(bf16[4,2,32,128]{3,2,1,0:T(8,128)(2,1)S(1)} %get-tuple-element.32), channel_id=1, source_target_pairs={{0,48},{16,32},{32,16},{48,0},{64,112},{80,96},{96,80},{112,64},{1... | collective-permute-start | bytes 196616 | tf_op jit(solution)/shard_map/near/ppermute | solution.py:226
  28.6 0.8 collective-permute-done.3
  29.3 3.2 %collective-permute-done.5 = bf16[4,2,32,128]{3,2,1,0:T(8,128)(2,1)S(1)} collective-permute-done((bf16[4,2,32,128]{3,2,1,0:T(8,128)(2,1)S(1)}, bf16[4,2,32,128]{3,2,1,0:T(8,128)(2,1)S(1)}, u32[]{:S(2)}, u32[]{:S(2)}) %collective-permute-start.5) | collective-permute-done | bytes 65568 | tf_op jit(solution)/shard_map/near/ppermute | solution.py:226
  32.6 4.3 %collective-permute-start.6 = (bf16[4,2,32,128]{3,2,1,0:T(8,128)(2,1)S(1)}, bf16[4,2,32,128]{3,2,1,0:T(8,128)(2,1)S(1)}, u32[]{:S(2)}, u32[]{:S(2)}) collective-permute-start(bf16[4,2,32,128]{3,2,1,0:T(8,128)(2,1)S(1)} %add_convert_fusion.1), channel_id=1, source_target_pairs={{0,64},{16,80},{32,96},{48,112},{64,0},{80,16},{96,32},{112,48},{1... | collective-permute-start | bytes 196616 | tf_op jit(solution)/shard_map/far/ppermute | solution.py:226
  36.9 3.6 %collective-permute-start.7 = (bf16[4,2,32,128]{3,2,1,0:T(8,128)(2,1)S(1)}, bf16[4,2,32,128]{3,2,1,0:T(8,128)(2,1)S(1)}, u32[]{:S(2)}, u32[]{:S(2)}) collective-permute-start(bf16[4,2,32,128]{3,2,1,0:T(8,128)(2,1)S(1)} %add_convert_fusion.1), channel_id=1, source_target_pairs={{0,128},{16,144},{32,160},{48,176},{64,192},{80,208},{96,224},{112... | collective-permute-start | bytes 196616 | tf_op jit(solution)/shard_map/far/ppermute | solution.py:226
  40.5 4.5 %collective-permute-done.7 = bf16[4,2,32,128]{3,2,1,0:T(8,128)(2,1)S(1)} collective-permute-done((bf16[4,2,32,128]{3,2,1,0:T(8,128)(2,1)S(1)}, bf16[4,2,32,128]{3,2,1,0:T(8,128)(2,1)S(1)}, u32[]{:S(2)}, u32[]{:S(2)}) %collective-permute-start.7) | collective-permute-done | bytes 65568 | tf_op jit(solution)/shard_map/far/ppermute | solution.py:226
  45.0 2.2 %collective-permute-done.8 = bf16[4,2,32,128]{3,2,1,0:T(8,128)(2,1)S(1)} collective-permute-done((bf16[4,2,32,128]{3,2,1,0:T(8,128)(2,1)S(1)}, bf16[4,2,32,128]{3,2,1,0:T(8,128)(2,1)S(1)}, u32[]{:S(2)}, u32[]{:S(2)}) %collective-permute-start.8) | collective-permute-done | bytes 65568 | tf_op jit(solution)/shard_map/far/ppermute | solution.py:226
  47.3 1.1 %collective-permute-start.10 = (bf16[4,2,32,128]{3,2,1,0:T(8,128)(2,1)S(1)}, bf16[4,2,32,128]{3,2,1,0:T(8,128)(2,1)S(1)}, u32[]{:S(2)}, u32[]{:S(2)}) collective-permute-start(bf16[4,2,32,128]{3,2,1,0:T(8,128)(2,1)S(1)} %add_convert_fusion.rest0), channel_id=1, source_target_pairs={{0,32},{16,48},{32,0},{48,16},{64,96},{80,112},{96,64},{112,80},{1... | collective-permute-start | bytes 196616 | tf_op jit(solution)/shard_map/gather/ppermute | solution.py:226
  48.4 2.4 %collective-permute-start.11 = (bf16[4,2,32,128]{3,2,1,0:T(8,128)(2,1)S(1)}, bf16[4,2,32,128]{3,2,1,0:T(8,128)(2,1)S(1)}, u32[]{:S(2)}, u32[]{:S(2)}) collective-permute-start(bf16[4,2,32,128]{3,2,1,0:T(8,128)(2,1)S(1)} %add_convert_fusion.rest0), channel_id=1, source_target_pairs={{0,48},{16,32},{32,16},{48,0},{64,112},{80,96},{96,80},{112,64},{1... | collective-permute-start | bytes 196616 | tf_op jit(solution)/shard_map/gather/ppermute | solution.py:226
  50.8 1.6 %collective-permute-start.9 = (bf16[4,2,32,128]{3,2,1,0:T(8,128)(2,1)S(1)}, bf16[4,2,32,128]{3,2,1,0:T(8,128)(2,1)S(1)}, u32[]{:S(2)}, u32[]{:S(2)}) collective-permute-start(bf16[4,2,32,128]{3,2,1,0:T(8,128)(2,1)S(1)} %add_convert_fusion.rest0), channel_id=1, source_target_pairs={{0,16},{16,0},{32,48},{48,32},{64,80},{80,64},{96,112},{112,96},{1... | collective-permute-start | bytes 196616 | tf_op jit(solution)/shard_map/gather/ppermute | solution.py:226
  52.4 2.7 %collective-permute-done.11.rest3 = bf16[4,2,32,128]{3,2,1,0:T(8,128)(2,1)S(1)} collective-permute-done((bf16[4,2,32,128]{3,2,1,0:T(8,128)(2,1)S(1)}, bf16[4,2,32,128]{3,2,1,0:T(8,128)(2,1)S(1)}, u32[]{:S(2)}, u32[]{:S(2)}) %collective-permute-start.11) | collective-permute-done | bytes 65568 | tf_op jit(solution)/shard_map/gather/ppermute | solution.py:226
  55.1 1.5 %collective-permute-done.9.rest1 = bf16[4,2,32,128]{3,2,1,0:T(8,128)(2,1)S(1)} collective-permute-done((bf16[4,2,32,128]{3,2,1,0:T(8,128)(2,1)S(1)}, bf16[4,2,32,128]{3,2,1,0:T(8,128)(2,1)S(1)}, u32[]{:S(2)}, u32[]{:S(2)}) %collective-permute-start.9) | collective-permute-done | bytes 65568 | tf_op jit(solution)/shard_map/gather/ppermute | solution.py:226
  56.6 1.4 %first_step.1 = (bf16[32,16,128]{2,1,0:T(8,128)(2,1)S(1)}, f32[32,128]{1,0:T(8,128)S(1)}, f32[32,16,128]{2,1,0:T(8,128)S(1)}, bf16[24,16,128]{2,1,0:T(8,128)(2,1)S(1)}, bf16[24,16,128]{2,1,0:T(8,128)(2,1)S(1)}) custom-call(s32[3]{0:T(128)S(1)} %pad_add_fusion.place_ref, s32[8,32]{1,0:T(8,128)S(1)} %bitcast.38, ...), custom_call_target="tpu_custom_call" | custom-call | tf_op jit(solution)/shard_map/first_step/pallas_call | solution.py:313
  57.9 1.9 %collective-permute-start.14 = (bf16[32,16,128]{2,1,0:T(8,128)(2,1)S(1)}, bf16[32,16,128]{2,1,0:T(8,128)(2,1)S(1)}, u32[]{:S(2)}, u32[]{:S(2)}) collective-permute-start(bf16[32,16,128]{2,1,0:T(8,128)(2,1)S(1)} %bitcast.35), channel_id=1, source_target_pairs={{0,32},{16,48},{32,64},{48,80},{64,96},{80,112},{96,128},{112,144}... | collective-permute-start | bytes 393224 | tf_op jit(solution)/shard_map/ppermute | solution.py:317
  59.9 3.1 %collective-permute-start.13 = (bf16[24,16,128]{2,1,0:T(8,128)(2,1)S(1)}, bf16[24,16,128]{2,1,0:T(8,128)(2,1)S(1)}, u32[]{:S(2)}, u32[]{:S(2)}) collective-permute-start(bf16[24,16,128]{2,1,0:T(8,128)(2,1)S(1)} %get-tuple-element.38), channel_id=1, source_target_pairs={{0,15},{1,2},{2,1},{3,4},{4,3},{5,6},{6,5},{7,8},{8,7},{9,10},{10,... | collective-permute-start | bytes 294920 | tf_op jit(solution)/shard_map/halo_extra/ppermute | solution.py:237
  63.0 3.5 %collective-permute-done.13.second_in = bf16[24,16,128]{2,1,0:T(8,128)(2,1)S(1)} collective-permute-done((bf16[24,16,128]{2,1,0:T(8,128)(2,1)S(1)}, bf16[24,16,128]{2,1,0:T(8,128)(2,1)S(1)}, u32[]{:S(2)}, u32[]{:S(2)}) %collective-permute-start.13) | collective-permute-done | bytes 98336 | tf_op jit(solution)/shard_map/halo_extra/ppermute | solution.py:237
  66.6 1.2 %second_step.1 = (bf16[32,16,128]{2,1,0:T(8,128)(2,1)}, bf16[16,32,128]{2,1,0:T(8,128)(2,1)S(1)}) custom-call(s32[3]{0:T(128)S(1)} %pad_add_fusion.place_ref, bf16[4,2,32,128]{3,2,1,0:T(8,128)(2,1)S(1)} %add_convert_fusion.rest0, bf16[4,2,32,128]{3,2,1,0:T(8,128)(2,1)S(1)} %collective-permute-done.9.rest1, ...), custom_call_target="tpu_custom_call" | custom-call | tf_op jit(solution)/shard_map/second_step/pallas_call | solution.py:320
  67.8 0.7 collective-permute-start.15
  68.5 0.7 collective-permute-start.16
  69.1 0.7 collective-permute-start.17
  71.2 1.3 %collective-permute-start.20 = (bf16[32,128]{1,0:T(8,128)(2,1)S(1)}, bf16[32,128]{1,0:T(8,128)(2,1)S(1)}, u32[]{:S(2)}, u32[]{:S(2)}) collective-permute-start(bf16[32,128]{1,0:T(8,128)(2,1)S(1)} %get-tuple-element.49), channel_id=1, source_target_pairs={{0,16},{64,80},{128,144},{192,208},{1,17},{65,81},{129,145},{193,2... | collective-permute-start | bytes 24584 | tf_op jit(solution)/shard_map/spread/ppermute | solution.py:331
  72.6 10.6 %collective-permute-done.20 = bf16[32,128]{1,0:T(8,128)(2,1)S(1)} collective-permute-done((bf16[32,128]{1,0:T(8,128)(2,1)S(1)}, bf16[32,128]{1,0:T(8,128)(2,1)S(1)}, u32[]{:S(2)}, u32[]{:S(2)}) %collective-permute-start.20) | collective-permute-done | bytes 8224 | tf_op jit(solution)/shard_map/spread/ppermute | solution.py:331
  (35 shorter events, 2.6 us)
Async XLA Ops:
  0.6 8.7 %collective-permute-start = (bf16[32,16,128]{2,1,0:T(8,128)(2,1)}, bf16[32,16,128]{2,1,0:T(8,128)(2,1)S(1)}, u32[]{:S(2)}, u32[]{:S(2)}) collective-permute-start(bf16[32,16,128]{2,1,0:T(8,128)(2,1)} %bitcast.33), channel_id=1, source_target_pairs={{0,16},{16,32},{32,48},{48,64},{64,80},{80,96},{96,112},{112,128},... | collective-permute-start | bytes 393224 | tf_op jit(solution)/shard_map/ppermute | solution.py:297
  2.6 0.9 %copy-start.1 = (bf16[1,32,16,128]{3,2,1,0:T(8,128)(2,1)S(1)}, bf16[1,32,16,128]{3,2,1,0:T(8,128)(2,1)}, u32[]{:S(2)}) copy-start(bf16[1,32,16,128]{3,2,1,0:T(8,128)(2,1)} %param.8) | copy-start | bytes 393220
  3.5 0.7 copy-start.3
  4.2 13.0 %copy-start = (f32[32,128,128]{2,1,0:T(8,128)S(1)}, f32[32,128,128]{2,1,0:T(8,128)}, u32[]{:S(2)}) copy-start(f32[32,128,128]{2,1,0:T(8,128)} %inverse.1) | copy-start | bytes 6291460
  4.2 13.0 %copy-start.2 = (f32[2,32,1,256]{3,2,1,0:T(1,128)S(1)}, f32[2,32,1,256]{3,2,1,0:T(1,128)}, u32[]{:S(2)}) copy-start(f32[2,32,1,256]{3,2,1,0:T(1,128)} %incident.1) | copy-start | bytes 196612
  4.2 13.0 %copy-start.4 = (s32[32,256]{1,0:T(8,128)S(1)}, s32[32,256]{1,0:T(8,128)}, u32[]{:S(2)}) copy-start(s32[32,256]{1,0:T(8,128)} %element_map.1) | copy-start | bytes 98308
  12.6 5.6 %collective-permute-start.1 = (bf16[24,32,128]{2,1,0:T(8,128)(2,1)S(1)}, bf16[24,32,128]{2,1,0:T(8,128)(2,1)S(1)}, u32[]{:S(2)}, u32[]{:S(2)}) collective-permute-start(bf16[24,32,128]{2,1,0:T(8,128)(2,1)S(1)} %get-tuple-element.26), channel_id=1, source_target_pairs={{0,1},{1,0},{2,3},{3,2},{4,5},{5,4},{6,7},{7,6},{8,9},{9,8},{10,11... | collective-permute-start | bytes 589832 | tf_op jit(solution)/shard_map/halo/ppermute | solution.py:237
  12.7 9.8 %collective-permute-start.2 = (bf16[24,32,128]{2,1,0:T(8,128)(2,1)S(1)}, bf16[24,32,128]{2,1,0:T(8,128)(2,1)S(1)}, u32[]{:S(2)}, u32[]{:S(2)}) collective-permute-start(bf16[24,32,128]{2,1,0:T(8,128)(2,1)S(1)} %get-tuple-element.27), channel_id=1, source_target_pairs={{0,15},{1,2},{2,1},{3,4},{4,3},{5,6},{6,5},{7,8},{8,7},{9,10},{10,... | collective-permute-start | bytes 589832 | tf_op jit(solution)/shard_map/halo/ppermute | solution.py:237
  23.5 5.9 %collective-permute-start.3 = (bf16[4,2,32,128]{3,2,1,0:T(8,128)(2,1)S(1)}, bf16[4,2,32,128]{3,2,1,0:T(8,128)(2,1)S(1)}, u32[]{:S(2)}, u32[]{:S(2)}) collective-permute-start(bf16[4,2,32,128]{3,2,1,0:T(8,128)(2,1)S(1)} %get-tuple-element.30), channel_id=1, source_target_pairs={{0,16},{16,0},{32,48},{48,32},{64,80},{80,64},{96,112},{112,96},{1... | collective-permute-start | bytes 196616 | tf_op jit(solution)/shard_map/near/ppermute | solution.py:226
  23.7 5.7 %collective-permute-start.4 = (bf16[4,2,32,128]{3,2,1,0:T(8,128)(2,1)S(1)}, bf16[4,2,32,128]{3,2,1,0:T(8,128)(2,1)S(1)}, u32[]{:S(2)}, u32[]{:S(2)}) collective-permute-start(bf16[4,2,32,128]{3,2,1,0:T(8,128)(2,1)S(1)} %get-tuple-element.31), channel_id=1, source_target_pairs={{0,32},{16,48},{32,0},{48,16},{64,96},{80,112},{96,64},{112,80},{1... | collective-permute-start | bytes 196616 | tf_op jit(solution)/shard_map/near/ppermute | solution.py:226
  25.9 6.7 %collective-permute-start.5 = (bf16[4,2,32,128]{3,2,1,0:T(8,128)(2,1)S(1)}, bf16[4,2,32,128]{3,2,1,0:T(8,128)(2,1)S(1)}, u32[]{:S(2)}, u32[]{:S(2)}) collective-permute-start(bf16[4,2,32,128]{3,2,1,0:T(8,128)(2,1)S(1)} %get-tuple-element.32), channel_id=1, source_target_pairs={{0,48},{16,32},{32,16},{48,0},{64,112},{80,96},{96,80},{112,64},{1... | collective-permute-start | bytes 196616 | tf_op jit(solution)/shard_map/near/ppermute | solution.py:226
  32.6 7.9 %collective-permute-start.6 = (bf16[4,2,32,128]{3,2,1,0:T(8,128)(2,1)S(1)}, bf16[4,2,32,128]{3,2,1,0:T(8,128)(2,1)S(1)}, u32[]{:S(2)}, u32[]{:S(2)}) collective-permute-start(bf16[4,2,32,128]{3,2,1,0:T(8,128)(2,1)S(1)} %add_convert_fusion.1), channel_id=1, source_target_pairs={{0,64},{16,80},{32,96},{48,112},{64,0},{80,16},{96,32},{112,48},{1... | collective-permute-start | bytes 196616 | tf_op jit(solution)/shard_map/far/ppermute | solution.py:226
  36.9 8.2 %collective-permute-start.7 = (bf16[4,2,32,128]{3,2,1,0:T(8,128)(2,1)S(1)}, bf16[4,2,32,128]{3,2,1,0:T(8,128)(2,1)S(1)}, u32[]{:S(2)}, u32[]{:S(2)}) collective-permute-start(bf16[4,2,32,128]{3,2,1,0:T(8,128)(2,1)S(1)} %add_convert_fusion.1), channel_id=1, source_target_pairs={{0,128},{16,144},{32,160},{48,176},{64,192},{80,208},{96,224},{112... | collective-permute-start | bytes 196616 | tf_op jit(solution)/shard_map/far/ppermute | solution.py:226
  40.4 6.8 %collective-permute-start.8 = (bf16[4,2,32,128]{3,2,1,0:T(8,128)(2,1)S(1)}, bf16[4,2,32,128]{3,2,1,0:T(8,128)(2,1)S(1)}, u32[]{:S(2)}, u32[]{:S(2)}) collective-permute-start(bf16[4,2,32,128]{3,2,1,0:T(8,128)(2,1)S(1)} %add_convert_fusion.1), channel_id=1, source_target_pairs={{0,192},{16,208},{32,224},{48,240},{64,128},{80,144},{96,160},{112... | collective-permute-start | bytes 196616 | tf_op jit(solution)/shard_map/far/ppermute | solution.py:226
  47.3 5.1 %collective-permute-start.10 = (bf16[4,2,32,128]{3,2,1,0:T(8,128)(2,1)S(1)}, bf16[4,2,32,128]{3,2,1,0:T(8,128)(2,1)S(1)}, u32[]{:S(2)}, u32[]{:S(2)}) collective-permute-start(bf16[4,2,32,128]{3,2,1,0:T(8,128)(2,1)S(1)} %add_convert_fusion.rest0), channel_id=1, source_target_pairs={{0,32},{16,48},{32,0},{48,16},{64,96},{80,112},{96,64},{112,80},{1... | collective-permute-start | bytes 196616 | tf_op jit(solution)/shard_map/gather/ppermute | solution.py:226
  48.4 6.7 %collective-permute-start.11 = (bf16[4,2,32,128]{3,2,1,0:T(8,128)(2,1)S(1)}, bf16[4,2,32,128]{3,2,1,0:T(8,128)(2,1)S(1)}, u32[]{:S(2)}, u32[]{:S(2)}) collective-permute-start(bf16[4,2,32,128]{3,2,1,0:T(8,128)(2,1)S(1)} %add_convert_fusion.rest0), channel_id=1, source_target_pairs={{0,48},{16,32},{32,16},{48,0},{64,112},{80,96},{96,80},{112,64},{1... | collective-permute-start | bytes 196616 | tf_op jit(solution)/shard_map/gather/ppermute | solution.py:226
  50.8 5.8 %collective-permute-start.9 = (bf16[4,2,32,128]{3,2,1,0:T(8,128)(2,1)S(1)}, bf16[4,2,32,128]{3,2,1,0:T(8,128)(2,1)S(1)}, u32[]{:S(2)}, u32[]{:S(2)}) collective-permute-start(bf16[4,2,32,128]{3,2,1,0:T(8,128)(2,1)S(1)} %add_convert_fusion.rest0), channel_id=1, source_target_pairs={{0,16},{16,0},{32,48},{48,32},{64,80},{80,64},{96,112},{112,96},{1... | collective-permute-start | bytes 196616 | tf_op jit(solution)/shard_map/gather/ppermute | solution.py:226
  57.9 8.6 %collective-permute-start.14 = (bf16[32,16,128]{2,1,0:T(8,128)(2,1)S(1)}, bf16[32,16,128]{2,1,0:T(8,128)(2,1)S(1)}, u32[]{:S(2)}, u32[]{:S(2)}) collective-permute-start(bf16[32,16,128]{2,1,0:T(8,128)(2,1)S(1)} %bitcast.35), channel_id=1, source_target_pairs={{0,32},{16,48},{32,64},{48,80},{64,96},{80,112},{96,128},{112,144}... | collective-permute-start | bytes 393224 | tf_op jit(solution)/shard_map/ppermute | solution.py:317
  59.9 3.2 %collective-permute-start.12 = (bf16[24,16,128]{2,1,0:T(8,128)(2,1)S(1)}, bf16[24,16,128]{2,1,0:T(8,128)(2,1)S(1)}, u32[]{:S(2)}, u32[]{:S(2)}) collective-permute-start(bf16[24,16,128]{2,1,0:T(8,128)(2,1)S(1)} %get-tuple-element.37), channel_id=1, source_target_pairs={{0,1},{1,0},{2,3},{3,2},{4,5},{5,4},{6,7},{7,6},{8,9},{9,8},{10,11... | collective-permute-start | bytes 294920 | tf_op jit(solution)/shard_map/halo_extra/ppermute | solution.py:237
  59.9 6.7 %collective-permute-start.13 = (bf16[24,16,128]{2,1,0:T(8,128)(2,1)S(1)}, bf16[24,16,128]{2,1,0:T(8,128)(2,1)S(1)}, u32[]{:S(2)}, u32[]{:S(2)}) collective-permute-start(bf16[24,16,128]{2,1,0:T(8,128)(2,1)S(1)} %get-tuple-element.38), channel_id=1, source_target_pairs={{0,15},{1,2},{2,1},{3,4},{4,3},{5,6},{6,5},{7,8},{8,7},{9,10},{10,... | collective-permute-start | bytes 294920 | tf_op jit(solution)/shard_map/halo_extra/ppermute | solution.py:237
  67.8 2.0 %collective-permute-start.15 = (bf16[4,32,128]{2,1,0:T(8,128)(2,1)S(1)}, bf16[4,32,128]{2,1,0:T(8,128)(2,1)S(1)}, u32[]{:S(2)}, u32[]{:S(2)}) collective-permute-start(bf16[4,32,128]{2,1,0:T(8,128)(2,1)S(1)} %get-tuple-element.48), channel_id=1, source_target_pairs={{0,192},{1,193},{2,194},{3,195},{4,196},{5,197},{6,198},{7,199},{8... | collective-permute-start | bytes 98312 | tf_op jit(solution)/shard_map/spread/ppermute | solution.py:327
  68.5 1.4 %collective-permute-start.16 = (bf16[4,32,128]{2,1,0:T(8,128)(2,1)S(1)}, bf16[4,32,128]{2,1,0:T(8,128)(2,1)S(1)}, u32[]{:S(2)}, u32[]{:S(2)}) collective-permute-start(bf16[4,32,128]{2,1,0:T(8,128)(2,1)S(1)} %get-tuple-element.47), channel_id=1, source_target_pairs={{0,128},{1,129},{2,130},{3,131},{4,132},{5,133},{6,134},{7,135},{8... | collective-permute-start | bytes 98312 | tf_op jit(solution)/shard_map/spread/ppermute | solution.py:327
  69.1 0.7 collective-permute-start.17
  69.9 2.7 %collective-permute-start.18 = (bf16[32,128]{1,0:T(8,128)(2,1)S(1)}, bf16[32,128]{1,0:T(8,128)(2,1)S(1)}, u32[]{:S(2)}, u32[]{:S(2)}) collective-permute-start(bf16[32,128]{1,0:T(8,128)(2,1)S(1)} %get-tuple-element.51), channel_id=1, source_target_pairs={{0,48},{64,112},{128,176},{192,240},{1,49},{65,113},{129,177},{193... | collective-permute-start | bytes 24584 | tf_op jit(solution)/shard_map/spread/ppermute | solution.py:331
  70.6 2.0 %collective-permute-start.19 = (bf16[32,128]{1,0:T(8,128)(2,1)S(1)}, bf16[32,128]{1,0:T(8,128)(2,1)S(1)}, u32[]{:S(2)}, u32[]{:S(2)}) collective-permute-start(bf16[32,128]{1,0:T(8,128)(2,1)S(1)} %get-tuple-element.50), channel_id=1, source_target_pairs={{0,32},{64,96},{128,160},{192,224},{1,33},{65,97},{129,161},{193,2... | collective-permute-start | bytes 24584 | tf_op jit(solution)/shard_map/spread/ppermute | solution.py:331
  71.2 11.9 %collective-permute-start.20 = (bf16[32,128]{1,0:T(8,128)(2,1)S(1)}, bf16[32,128]{1,0:T(8,128)(2,1)S(1)}, u32[]{:S(2)}, u32[]{:S(2)}) collective-permute-start(bf16[32,128]{1,0:T(8,128)(2,1)S(1)} %get-tuple-element.49), channel_id=1, source_target_pairs={{0,16},{64,80},{128,144},{192,208},{1,17},{65,81},{129,145},{193,2... | collective-permute-start | bytes 24584 | tf_op jit(solution)/shard_map/spread/ppermute | solution.py:331

commit v4 on v3

v4 whole, which is shorter than its diff:
```python
import functools

import jax
import jax.numpy as jnp
from jax import lax
from jax.experimental import pallas as pl
from jax.experimental.pallas import tpu as pltpu
from jax.sharding import PartitionSpec as P

F32 = jnp.float32
BF16 = jnp.bfloat16
HALF = 24
NT = (((1,), (1,)), ((), ()))
VMEM = pl.BlockSpec(memory_space=pltpu.VMEM)
HBM = pl.BlockSpec(memory_space=pltpu.HBM)
SMEM = pl.BlockSpec(memory_space=pltpu.SMEM)


def split(x):
    high = x.astype(BF16)
    return high, (x - high.astype(F32)).astype(BF16)


def banded(place_ref, offsets_ref, rows_of, blocks, window, total_blocks):
    block_cols, width, size, _ = blocks.shape
    first = place_ref[0]
    window[...] = jnp.zeros_like(window)
    for c in range(block_cols):
        column = blocks[c].reshape(width * size, size)
        prod = lax.dot_general(rows_of(c), column, NT, preferred_element_type=F32)
        for k in range(width):
            row = jnp.clip(first + c + offsets_ref[k, c], 0, total_blocks - 1) - first + HALF
            window[row] += prod[:, size * k : size * (k + 1)]


def hand_out(place_ref, window, main, first_out, second_out):
    n = main.shape[0]
    main[...] = window[HALF : HALF + n]
    even = 1 - place_ref[2]
    first_out[...] = window[pl.ds(even * (HALF + n), HALF)].astype(BF16)
    second_out[...] = window[pl.ds((1 - even) * (HALF + n), HALF)].astype(BF16)


def shared(place_ref, b, n, first_in, second_in):
    odd = place_ref[2] == 1
    value = 0.0
    if b < HALF:
        value = value + jnp.where(odd, first_in[b], second_in[b]).astype(F32)
    if b >= n - HALF:
        edge = b - (n - HALF)
        value = value + jnp.where(odd, second_in[edge], first_in[edge]).astype(F32)
    return value


def fetch_kernel(place_ref, blocks_hbm, blocks, follows, sems):
    chunks = sems.shape[0]
    some = blocks.shape[0] // chunks
    copies = []
    for i in range(chunks):
        part = pl.ds(i * some, some)
        copies.append(pltpu.make_async_copy(blocks_hbm.at[part], blocks.at[part], sems.at[i]))
    for copy in copies:
        copy.start()
    follows[...] = jnp.where(place_ref[1] > 0, jnp.ones_like(follows), jnp.zeros_like(follows))
    for copy in copies:
        copy.wait()


def shells_kernel(
    total_blocks, place_ref, offsets_ref, shells, older, blocks, follows,
    main, first_out, second_out, kept, window,
):
    banded(
        place_ref, offsets_ref, lambda c: jnp.concatenate([shells[c], older[c] * follows[...]], 0),
        blocks, window, total_blocks,
    )
    hand_out(place_ref, window, main, first_out, second_out)


def prepare_kernel(incident, element_map, inverse, source, inverse_parts):
    n, size, _ = inverse.shape
    samples = element_map.shape[1]
    unknown = lax.broadcasted_iota(jnp.int32, (size, samples), 0)
    line = lax.broadcasted_iota(jnp.int32, (8, samples), 0)
    for b in range(n):
        load = (unknown == element_map[b : b + 1, :]).astype(F32).astype(BF16)
        rows = jnp.zeros((8, samples), F32)
        for t in range(2):
            sample = jnp.broadcast_to(incident[t, b], (8, samples))
            high = sample.astype(BF16).astype(F32)
            rows = jnp.where(line == 2 * t, high, jnp.where(line == 2 * t + 1, sample - high, rows))
        out = lax.dot_general(rows.astype(BF16), load, NT, preferred_element_type=F32)
        for t in range(2):
            source[t, b : b + 1, :] = out[2 * t : 2 * t + 1] + out[2 * t + 1 : 2 * t + 2]
        high, low = split(inverse[b])
        inverse_parts[b, :, :size] = high
        inverse_parts[b, :, size:] = low


def combine_kernel(
    place_ref, main, first_in, second_in, source, keep, send1, send2, send3, total
):
    n, both, size = main.shape
    line = lax.broadcasted_iota(jnp.int32, (both, size), 0)
    for b in range(n):
        value = main[b] + shared(place_ref, b, n, first_in, second_in)
        for t in range(2):
            mine = line == place_ref[1] + t * (both // 2)
            value = value - jnp.where(mine, source[t, b : b + 1, :], 0.0)
        total[b] = value.astype(BF16)
    for distance, out in enumerate((keep, send1, send2, send3)):
        out[...] = total[quarter_of(place_ref, distance, n)]


def quarter_of(place_ref, distance, n):
    return pl.ds(((place_ref[1] & 3) ^ distance) * (n // 4), n // 4)


def gathered(place_ref, parts, rest):
    for distance, part in enumerate(parts):
        rest[quarter_of(place_ref, distance, rest.shape[0])] = part[...]


def solve(rest, inverse_part):
    pulses, size = rest.shape
    high, low = split(-rest)
    lhs = jnp.concatenate(
        [jnp.concatenate([high, high], 1), jnp.concatenate([low, jnp.zeros_like(low)], 1)], 0
    )
    out = lax.dot_general(lhs, inverse_part, NT, preferred_element_type=F32)
    return out[:pulses] + out[pulses:]


def first_step_kernel(
    total_blocks, place_ref, offsets_ref, rest0, rest1, rest2, rest3, inverse_parts, blocks,
    current, main, first_out, second_out, rest, window,
):
    n, pulses, size = current.shape
    gathered(place_ref, (rest0, rest1, rest2, rest3), rest)
    for b in range(n):
        current[b] = solve(rest[b, :pulses].astype(F32), inverse_parts[b]).astype(BF16)

    @pl.when(place_ref[1] == 0)
    def _():
        banded(place_ref, offsets_ref, lambda c: current[c], blocks, window, total_blocks)
        hand_out(place_ref, window, main, first_out, second_out)


def second_sum_kernel(
    place_ref, rest0, rest1, rest2, rest3, main, current0, total, own_pulse, rest
):
    n, pulses, size = main.shape
    mine = lax.broadcasted_iota(jnp.int32, (pulses, size), 0) == place_ref[1]
    gathered(place_ref, (rest0, rest1, rest2, rest3), rest)
    for b in range(n):
        total[b] = rest[b, pulses:].astype(F32) + main[b]
        own = jnp.where(mine, current0[b].astype(F32), 0.0)
        own_pulse[b : b + 1, :] = jnp.sum(own, axis=0, keepdims=True)


def second_step_kernel(
    place_ref, total, first_in, second_in, inverse_parts, current, by_pulse, scratch
):
    n, pulses, size = current.shape

    @pl.when(place_ref[1] == 0)
    def _():
        for b in range(n):
            value = total[b] + shared(place_ref, b, n, first_in, second_in)
            new = solve(value, inverse_parts[b])
            current[b] = new.astype(BF16)
            scratch[b * pulses : (b + 1) * pulses, :] = new
        for p in range(pulses):
            by_pulse[p] = scratch[pl.ds(p, n, stride=pulses), :].astype(BF16)


def call(kernel, name, out_shape, in_specs, scratch_shapes=(), mib=16, aliases={}):
    return pl.pallas_call(
        kernel,
        name=name,
        out_shape=out_shape,
        in_specs=in_specs,
        out_specs=[VMEM] * len(out_shape),
        scratch_shapes=scratch_shapes,
        input_output_aliases=aliases,
        compiler_params=pltpu.CompilerParams(vmem_limit_bytes=mib * 2**20),
    )


def exchange(block, distance):
    return lax.ppermute(block, "lag", [(i, i ^ distance) for i in range(16)])


def added(own, others):
    return sum((other.astype(F32) for other in others), own.astype(F32)).astype(BF16)


def trade(first_out, second_out):
    n = lax.axis_size("col")
    pairs = [(i, i ^ 1) for i in range(n)]
    others = [(i, (i + 1 if i % 2 else i - 1) % n) for i in range(n)]
    return lax.ppermute(first_out, "col", pairs), lax.ppermute(second_out, "col", others)


def body(blocks, offsets, history, instant_inverse, incident, element_map):
    lag_index = lax.axis_index("lag")
    lags = lax.axis_size("lag")
    n, pulses, size = history.shape[1:]
    total_blocks = n * lax.axis_size("col")
    col_index = lax.axis_index("col")
    place = jnp.stack([col_index * n, lag_index, col_index % 2]).astype(jnp.int32)
    blocks = blocks[0]
    band_rows = offsets[0].T
    shells = history[0]

    def shape(*dims, dtype=F32):
        return jax.ShapeDtypeStruct(dims, dtype)

    def partial_out(rows):
        edge = shape(HALF, rows, size, dtype=BF16)
        return shape(n, rows, size), edge, edge

    def window(rows):
        return pltpu.VMEM((n + 2 * HALF, rows, size), F32)

    kept = shape(*blocks.shape, dtype=BF16)
    fetch = call(
        fetch_kernel, "fetch", (kept, shape(pulses, size, dtype=BF16)), [SMEM, HBM], [pltpu.SemaphoreType.DMA((8,))], mib=40
    )
    shell_sums = call(
        functools.partial(shells_kernel, total_blocks), "shell_sums",
        partial_out(2 * pulses) + (kept,), [SMEM, SMEM] + [VMEM] * 4, [window(2 * pulses)],
        aliases={4: 3},
    )
    prepare = call(
        prepare_kernel, "prepare",
        (shape(2, n, size), shape(n, size, 2 * size, dtype=BF16)), [VMEM] * 3,
    )
    quarters = (shape(n // 4, 2 * pulses, size, dtype=BF16),) * 4
    rows = pltpu.VMEM((n, 2 * pulses, size), BF16)
    combine = call(combine_kernel, "combine", quarters, [SMEM] + [VMEM] * 4, [rows])
    first_step = call(
        functools.partial(first_step_kernel, total_blocks), "first_step",
        (shape(n, pulses, size, dtype=BF16),) + partial_out(pulses),
        [SMEM, SMEM] + [VMEM] * 6, [rows, window(pulses)],
    )
    second_sum = call(
        second_sum_kernel, "second_sum",
        (shape(n, pulses, size), shape(n, size)), [SMEM] + [VMEM] * 6, [rows],
    )
    second_step = call(
        second_step_kernel, "second_step",
        (shape(n, pulses, size, dtype=BF16), shape(pulses, n, size, dtype=BF16)),
        [SMEM] + [VMEM] * 4, [pltpu.VMEM((n * pulses, size), F32)],
    )

    older = lax.ppermute(shells, "lag", [(i, (i + 1) % lags) for i in range(lags)])
    with jax.named_scope("shells"):
        blocks, follows = fetch(place, blocks)
        main, first_out, second_out, blocks = shell_sums(
            place, band_rows, shells, older, blocks, follows
        )
    with jax.named_scope("halo"):
        first_in, second_in = trade(first_out, second_out)
    source, inverse_parts = prepare(incident, element_map, instant_inverse)
    keep, *sent = combine(place, main, first_in, second_in, source)
    with jax.named_scope("near"):
        quarter = added(keep, [exchange(part, d) for d, part in zip((1, 2, 3), sent)])
    with jax.named_scope("far"):
        quarter = added(quarter, [exchange(quarter, d) for d in (8, 4, 12)])
    with jax.named_scope("gather"):
        rest = [quarter] + [exchange(quarter, d) for d in (1, 2, 3)]
    current0, extra, first_out, second_out = first_step(
        place, band_rows, *rest, inverse_parts, blocks
    )
    shells, current0 = lax.optimization_barrier((shells, current0))
    oldest = lax.ppermute(shells, "lag", [(i, (i + 2) % lags) for i in range(lags)])
    with jax.named_scope("halo_extra"):
        first_in, second_in = trade(first_out, second_out)
    total, own0 = second_sum(place, *rest, extra, current0)
    current1, by_pulse1 = second_step(place, total, first_in, second_in, inverse_parts)
    with jax.named_scope("spread"):
        quarter = pulses // 4
        groups = [by_pulse1[quarter * g : quarter * (g + 1)] for g in range(4)]
        arrived = [lax.ppermute(groups[g], "lag", [(0, 4 * g)]) for g in (1, 2, 3)]
        leader = groups[0]
        for g in (1, 2, 3):
            leader = jnp.where(lag_index == 4 * g, arrived[g - 1], leader)
        arrived = [
            lax.ppermute(leader[d], "lag", [(4 * g, 4 * g + d) for g in range(4)]) for d in (1, 2, 3)
        ]
        own1 = leader[0]
        for d in (1, 2, 3):
            own1 = jnp.where(lag_index % 4 == d, arrived[d - 1], own1)
    currents = jnp.stack([own0.astype(BF16), own1])[:, :, None, :]
    aged = jnp.where(lag_index == 0, current1, jnp.where(lag_index == 1, current0, oldest))
    return currents, aged[None]


def solution(mesh):
    placed = (
        P("lag", "col", None, None, None),
        P("lag", "col", None),
        P("lag", "col", None, None),
        P("col", None, None),
        P(None, "col", "lag", None),
        P("col", None),
    )
    return jax.shard_map(
        body,
        mesh=mesh,
        in_specs=placed,
        out_specs=(P(None, "col", "lag", None), P("lag", "col", None, None)),
        check_vma=False,
    )
```

time: 84 us -> 80.7 us (0.961)
  starting transfers between devices: 34.4 us -> 32.5 us
  local copies, waits for them, and re-layouts: 1.61 us -> 0.03 us
    ppermute x2, starting transfers between devices: 7.77 us -> 5.89 us  [trade(): lax.ppermute(second_out, 'col', others)]
    unnamed x10, local copies, waits for them, and re-layouts: 1.6 us -> 0.02 us
    ppermute x1, starting transfers between devices: 1.93 us -> 0.99 us  [body(): lax.ppermute(shells, 'lag', [(i, (i + 2) % lags) for i in range(lags)])]
    ppermute x1, waiting for transfers between devices: 0.01 us -> 0.87 us  [body(): lax.ppermute(shells, 'lag', [(i, (i + 1) % lags) for i in range(lags)])]
    pallas_call x3 -> x4, Pallas kernels: 9.51 us -> 9.01 us  [the longest x1 4.13 us: body(): blocks, follows = fetch(place, blocks)]
  transfers between devices with their start and end apart: 21 -> 21, of which waited for: 9 -> 12; matrix products, arithmetic and copies ran while one was open for 0% -> 1% of each run, Pallas kernels for 7% -> 8%
where the time goes in v4:
time: 80.7 us; the launch traced here: 80.5 us
  waiting for transfers between devices  33.6 us (42%)
  starting transfers between devices  32.5 us (40%)
  Pallas kernels  12.1 us (15%)
  other arithmetic  1.48 us (2%)
  between operations  0.84 us (1%)
    ppermute x9, starting transfers between devices, exchange(): return lax.ppermute(block, 'lag', [(i, i ^ distance) for i in range(16)])  18.9 us
    ppermute x9, waiting for transfers between devices, exchange(): return lax.ppermute(block, 'lag', [(i, i ^ distance) for i in range(16)])  15.4 us
    ppermute x3, waiting for transfers between devices, body(): lax.ppermute(leader[d], 'lag', [(4 * g, 4 * g + d) for g in range(4)])  10.2 us
    ppermute x2, waiting for transfers between devices, trade(): lax.ppermute(second_out, 'col', others)  7.06 us
    ppermute x2, starting transfers between devices, trade(): lax.ppermute(second_out, 'col', others)  5.89 us
    pallas_call x1, Pallas kernels, body(): blocks, follows = fetch(place, blocks)  4.13 us
    pallas_call x1, Pallas kernels, body(): shell_sums(place, band_rows, shells, older, blocks, follows)  3.7 us
    ppermute x3, starting transfers between devices, body(): lax.ppermute(leader[d], 'lag', [(4 * g, 4 * g + d) for g in range(4)])  2.62 us
  transfers between devices with their start and end apart: 21, of which 12 were waited for; matrix products, arithmetic and copies ran while one was open for 1% of the time, Pallas kernels for 8%

profile of v4, /device:TPU:4, one launch (start us, length us, event | category | flops | bytes accessed | tf_op | source)
XLA Modules:
  0.0 80.5 jit_solution(3863622905780553892)
XLA Ops:
  0.6 1.9 %collective-permute-start = (bf16[32,16,128]{2,1,0:T(8,128)(2,1)}, bf16[32,16,128]{2,1,0:T(8,128)(2,1)S(1)}, u32[]{:S(2)}, u32[]{:S(2)}) collective-permute-start(bf16[32,16,128]{2,1,0:T(8,128)(2,1)} %bitcast.34), channel_id=1, source_target_pairs={{0,16},{16,32},{32,48},{48,64},{64,80},{80,96},{96,112},{112,128},... | collective-permute-start | bytes 393224 | tf_op jit(solution)/shard_map/ppermute | solution.py:257
  2.7 4.1 %fetch.1 = (bf16[32,8,128,128]{3,2,1,0:T(8,128)(2,1)S(1)}, bf16[16,128]{1,0:T(8,128)(2,1)S(1)}) custom-call(s32[3]{0:T(128)S(1)} %pad_add_fusion.place_ref, bf16[32,8,128,128]{3,2,1,0:T(8,128)(2,1)} %bitcast.39), custom_call_target="tpu_custom_call" | custom-call | tf_op jit(solution)/shard_map/shells/fetch/pallas_call | solution.py:259
  6.8 0.9 %collective-permute-done.older = bf16[32,16,128]{2,1,0:T(8,128)(2,1)S(1)} collective-permute-done((bf16[32,16,128]{2,1,0:T(8,128)(2,1)}, bf16[32,16,128]{2,1,0:T(8,128)(2,1)S(1)}, u32[]{:S(2)}, u32[]{:S(2)}) %collective-permute-start) | collective-permute-done | bytes 131104 | tf_op jit(solution)/shard_map/ppermute | solution.py:257
  7.7 3.7 %shell_sums.1 = (f32[32,32,128]{2,1,0:T(8,128)S(1)}, bf16[24,32,128]{2,1,0:T(8,128)(2,1)S(1)}, bf16[24,32,128]{2,1,0:T(8,128)(2,1)S(1)}, bf16[32,8,128,128]{3,2,1,0:T(8,128)(2,1)S(1)}) custom-call(s32[3]{0:T(128)S(1)} %pad_add_fusion.place_ref, s32[8,32]{1,0:T(8,128)S(1)} %bitcast.37, ...), custom_call_target="tpu_custom_call", output_to_operand_aliasing={{3}: (4, {})} | custom-call | tf_op jit(solution)/shard_map/shells/shell_sums/pallas_call | solution.py:260
  11.5 3.8 %collective-permute-start.2 = (bf16[24,32,128]{2,1,0:T(8,128)(2,1)S(1)}, bf16[24,32,128]{2,1,0:T(8,128)(2,1)S(1)}, u32[]{:S(2)}, u32[]{:S(2)}) collective-permute-start(bf16[24,32,128]{2,1,0:T(8,128)(2,1)S(1)} %get-tuple-element.28), channel_id=1, source_target_pairs={{0,15},{1,2},{2,1},{3,4},{4,3},{5,6},{6,5},{7,8},{8,7},{9,10},{10,... | collective-permute-start | bytes 589832 | tf_op jit(solution)/shard_map/halo/ppermute | solution.py:202
  15.3 0.9 %prepare.1 = (f32[2,32,128]{2,1,0:T(8,128)S(1)}, bf16[32,128,256]{2,1,0:T(8,128)(2,1)S(1)}) custom-call(f32[2,32,1,256]{3,2,1,0:T(1,128)S(1)} %copy-done.2, s32[32,256]{1,0:T(8,128)S(1)} %copy-done.3, f32[32,128,128]{2,1,0:T(8,128)S(1)} %copy-done), custom_call_target="tpu_custom_call" | custom-call | tf_op jit(solution)/shard_map/prepare/pallas_call | solution.py:265
  16.1 3.9 %collective-permute-done.2.second_in = bf16[24,32,128]{2,1,0:T(8,128)(2,1)S(1)} collective-permute-done((bf16[24,32,128]{2,1,0:T(8,128)(2,1)S(1)}, bf16[24,32,128]{2,1,0:T(8,128)(2,1)S(1)}, u32[]{:S(2)}, u32[]{:S(2)}) %collective-permute-start.2) | collective-permute-done | bytes 196640 | tf_op jit(solution)/shard_map/halo/ppermute | solution.py:202
  20.0 0.8 combine.1
  20.8 5.6 %collective-permute-start.3 = (bf16[8,32,128]{2,1,0:T(8,128)(2,1)S(1)}, bf16[8,32,128]{2,1,0:T(8,128)(2,1)S(1)}, u32[]{:S(2)}, u32[]{:S(2)}) collective-permute-start(bf16[8,32,128]{2,1,0:T(8,128)(2,1)S(1)} %get-tuple-element.31), channel_id=1, source_target_pairs={{0,16},{16,0},{32,48},{48,32},{64,80},{80,64},{96,112},{112,96},{1... | collective-permute-start | bytes 196616 | tf_op jit(solution)/shard_map/near/ppermute | solution.py:191
  26.4 1.6 %collective-permute-start.5 = (bf16[8,32,128]{2,1,0:T(8,128)(2,1)S(1)}, bf16[8,32,128]{2,1,0:T(8,128)(2,1)S(1)}, u32[]{:S(2)}, u32[]{:S(2)}) collective-permute-start(bf16[8,32,128]{2,1,0:T(8,128)(2,1)S(1)} %get-tuple-element.33), channel_id=1, source_target_pairs={{0,48},{16,32},{32,16},{48,0},{64,112},{80,96},{96,80},{112,64},{1... | collective-permute-start | bytes 196616 | tf_op jit(solution)/shard_map/near/ppermute | solution.py:191
  28.0 1.0 %collective-permute-done.3 = bf16[8,32,128]{2,1,0:T(8,128)(2,1)S(1)} collective-permute-done((bf16[8,32,128]{2,1,0:T(8,128)(2,1)S(1)}, bf16[8,32,128]{2,1,0:T(8,128)(2,1)S(1)}, u32[]{:S(2)}, u32[]{:S(2)}) %collective-permute-start.3) | collective-permute-done | bytes 65568 | tf_op jit(solution)/shard_map/near/ppermute | solution.py:191
  28.9 1.7 %collective-permute-done.4 = bf16[8,32,128]{2,1,0:T(8,128)(2,1)S(1)} collective-permute-done((bf16[8,32,128]{2,1,0:T(8,128)(2,1)S(1)}, bf16[8,32,128]{2,1,0:T(8,128)(2,1)S(1)}, u32[]{:S(2)}, u32[]{:S(2)}) %collective-permute-start.4) | collective-permute-done | bytes 65568 | tf_op jit(solution)/shard_map/near/ppermute | solution.py:191
  30.7 2.4 %collective-permute-done.5 = bf16[8,32,128]{2,1,0:T(8,128)(2,1)S(1)} collective-permute-done((bf16[8,32,128]{2,1,0:T(8,128)(2,1)S(1)}, bf16[8,32,128]{2,1,0:T(8,128)(2,1)S(1)}, u32[]{:S(2)}, u32[]{:S(2)}) %collective-permute-start.5) | collective-permute-done | bytes 65568 | tf_op jit(solution)/shard_map/near/ppermute | solution.py:191
  33.1 4.5 %collective-permute-start.6 = (bf16[8,32,128]{2,1,0:T(8,128)(2,1)S(1)}, bf16[8,32,128]{2,1,0:T(8,128)(2,1)S(1)}, u32[]{:S(2)}, u32[]{:S(2)}) collective-permute-start(bf16[8,32,128]{2,1,0:T(8,128)(2,1)S(1)} %add_convert_fusion.1), channel_id=1, source_target_pairs={{0,128},{16,144},{32,160},{48,176},{64,192},{80,208},{96,224},{112... | collective-permute-start | bytes 196616 | tf_op jit(solution)/shard_map/far/ppermute | solution.py:191
  37.6 1.3 %collective-permute-start.7 = (bf16[8,32,128]{2,1,0:T(8,128)(2,1)S(1)}, bf16[8,32,128]{2,1,0:T(8,128)(2,1)S(1)}, u32[]{:S(2)}, u32[]{:S(2)}) collective-permute-start(bf16[8,32,128]{2,1,0:T(8,128)(2,1)S(1)} %add_convert_fusion.1), channel_id=1, source_target_pairs={{0,64},{16,80},{32,96},{48,112},{64,0},{80,16},{96,32},{112,48},{1... | collective-permute-start | bytes 196616 | tf_op jit(solution)/shard_map/far/ppermute | solution.py:191
  38.9 0.8 %collective-permute-start.8 = (bf16[8,32,128]{2,1,0:T(8,128)(2,1)S(1)}, bf16[8,32,128]{2,1,0:T(8,128)(2,1)S(1)}, u32[]{:S(2)}, u32[]{:S(2)}) collective-permute-start(bf16[8,32,128]{2,1,0:T(8,128)(2,1)S(1)} %add_convert_fusion.1), channel_id=1, source_target_pairs={{0,192},{16,208},{32,224},{48,240},{64,128},{80,144},{96,160},{112... | collective-permute-start | bytes 196616 | tf_op jit(solution)/shard_map/far/ppermute | solution.py:191
  39.7 1.8 %collective-permute-done.6 = bf16[8,32,128]{2,1,0:T(8,128)(2,1)S(1)} collective-permute-done((bf16[8,32,128]{2,1,0:T(8,128)(2,1)S(1)}, bf16[8,32,128]{2,1,0:T(8,128)(2,1)S(1)}, u32[]{:S(2)}, u32[]{:S(2)}) %collective-permute-start.6) | collective-permute-done | bytes 65568 | tf_op jit(solution)/shard_map/far/ppermute | solution.py:191
  41.5 1.4 %collective-permute-done.7 = bf16[8,32,128]{2,1,0:T(8,128)(2,1)S(1)} collective-permute-done((bf16[8,32,128]{2,1,0:T(8,128)(2,1)S(1)}, bf16[8,32,128]{2,1,0:T(8,128)(2,1)S(1)}, u32[]{:S(2)}, u32[]{:S(2)}) %collective-permute-start.7) | collective-permute-done | bytes 65568 | tf_op jit(solution)/shard_map/far/ppermute | solution.py:191
  42.9 2.9 %collective-permute-done.8 = bf16[8,32,128]{2,1,0:T(8,128)(2,1)S(1)} collective-permute-done((bf16[8,32,128]{2,1,0:T(8,128)(2,1)S(1)}, bf16[8,32,128]{2,1,0:T(8,128)(2,1)S(1)}, u32[]{:S(2)}, u32[]{:S(2)}) %collective-permute-start.8) | collective-permute-done | bytes 65568 | tf_op jit(solution)/shard_map/far/ppermute | solution.py:191
  45.8 1.1 %collective-permute-start.10 = (bf16[8,32,128]{2,1,0:T(8,128)(2,1)S(1)}, bf16[8,32,128]{2,1,0:T(8,128)(2,1)S(1)}, u32[]{:S(2)}, u32[]{:S(2)}) collective-permute-start(bf16[8,32,128]{2,1,0:T(8,128)(2,1)S(1)} %add_convert_fusion.rest0), channel_id=1, source_target_pairs={{0,32},{16,48},{32,0},{48,16},{64,96},{80,112},{96,64},{112,80},{1... | collective-permute-start | bytes 196616 | tf_op jit(solution)/shard_map/gather/ppermute | solution.py:191
  46.9 2.5 %collective-permute-start.11 = (bf16[8,32,128]{2,1,0:T(8,128)(2,1)S(1)}, bf16[8,32,128]{2,1,0:T(8,128)(2,1)S(1)}, u32[]{:S(2)}, u32[]{:S(2)}) collective-permute-start(bf16[8,32,128]{2,1,0:T(8,128)(2,1)S(1)} %add_convert_fusion.rest0), channel_id=1, source_target_pairs={{0,48},{16,32},{32,16},{48,0},{64,112},{80,96},{96,80},{112,64},{1... | collective-permute-start | bytes 196616 | tf_op jit(solution)/shard_map/gather/ppermute | solution.py:191
  49.4 1.4 %collective-permute-start.9 = (bf16[8,32,128]{2,1,0:T(8,128)(2,1)S(1)}, bf16[8,32,128]{2,1,0:T(8,128)(2,1)S(1)}, u32[]{:S(2)}, u32[]{:S(2)}) collective-permute-start(bf16[8,32,128]{2,1,0:T(8,128)(2,1)S(1)} %add_convert_fusion.rest0), channel_id=1, source_target_pairs={{0,16},{16,0},{32,48},{48,32},{64,80},{80,64},{96,112},{112,96},{1... | collective-permute-start | bytes 196616 | tf_op jit(solution)/shard_map/gather/ppermute | solution.py:191
  50.8 2.7 %collective-permute-done.11.rest3 = bf16[8,32,128]{2,1,0:T(8,128)(2,1)S(1)} collective-permute-done((bf16[8,32,128]{2,1,0:T(8,128)(2,1)S(1)}, bf16[8,32,128]{2,1,0:T(8,128)(2,1)S(1)}, u32[]{:S(2)}, u32[]{:S(2)}) %collective-permute-start.11) | collective-permute-done | bytes 65568 | tf_op jit(solution)/shard_map/gather/ppermute | solution.py:191
  53.6 1.6 %collective-permute-done.9.rest1 = bf16[8,32,128]{2,1,0:T(8,128)(2,1)S(1)} collective-permute-done((bf16[8,32,128]{2,1,0:T(8,128)(2,1)S(1)}, bf16[8,32,128]{2,1,0:T(8,128)(2,1)S(1)}, u32[]{:S(2)}, u32[]{:S(2)}) %collective-permute-start.9) | collective-permute-done | bytes 65568 | tf_op jit(solution)/shard_map/gather/ppermute | solution.py:191
  55.2 1.5 %first_step.1 = (bf16[32,16,128]{2,1,0:T(8,128)(2,1)S(1)}, f32[32,16,128]{2,1,0:T(8,128)S(1)}, bf16[24,16,128]{2,1,0:T(8,128)(2,1)S(1)}, bf16[24,16,128]{2,1,0:T(8,128)(2,1)S(1)}) custom-call(s32[3]{0:T(128)S(1)} %pad_add_fusion.place_ref, s32[8,32]{1,0:T(8,128)S(1)} %bitcast.38, bf16[8,32,128]{2,1,0:T(8,128)(2,1)S(1)} %add_convert_fusion.rest0, ...), custom_call_target="tpu_custom_call" | custom-call | tf_op jit(solution)/shard_map/first_step/pallas_call | solution.py:273
  56.8 2.1 %collective-permute-start.13 = (bf16[24,16,128]{2,1,0:T(8,128)(2,1)S(1)}, bf16[24,16,128]{2,1,0:T(8,128)(2,1)S(1)}, u32[]{:S(2)}, u32[]{:S(2)}) collective-permute-start(bf16[24,16,128]{2,1,0:T(8,128)(2,1)S(1)} %get-tuple-element.42), channel_id=1, source_target_pairs={{0,15},{1,2},{2,1},{3,4},{4,3},{5,6},{6,5},{7,8},{8,7},{9,10},{10,... | collective-permute-start | bytes 294920 | tf_op jit(solution)/shard_map/halo_extra/ppermute | solution.py:202
  58.9 1.0 %collective-permute-start.20 = (bf16[32,16,128]{2,1,0:T(8,128)(2,1)S(1)}, bf16[32,16,128]{2,1,0:T(8,128)(2,1)S(1)}, u32[]{:S(2)}, u32[]{:S(2)}) collective-permute-start(bf16[32,16,128]{2,1,0:T(8,128)(2,1)S(1)} %bitcast.36), channel_id=1, source_target_pairs={{0,32},{16,48},{32,64},{48,80},{64,96},{80,112},{96,128},{112,144}... | collective-permute-start | bytes 393224 | tf_op jit(solution)/shard_map/ppermute | solution.py:277
  60.5 3.2 %collective-permute-done.13.second_in = bf16[24,16,128]{2,1,0:T(8,128)(2,1)S(1)} collective-permute-done((bf16[24,16,128]{2,1,0:T(8,128)(2,1)S(1)}, bf16[24,16,128]{2,1,0:T(8,128)(2,1)S(1)}, u32[]{:S(2)}, u32[]{:S(2)}) %collective-permute-start.13) | collective-permute-done | bytes 98336 | tf_op jit(solution)/shard_map/halo_extra/ppermute | solution.py:202
  64.3 0.7 collective-permute-start.14
  67.7 1.3 %collective-permute-start.19 = (bf16[32,128]{1,0:T(8,128)(2,1)S(1)}, bf16[32,128]{1,0:T(8,128)(2,1)S(1)}, u32[]{:S(2)}, u32[]{:S(2)}) collective-permute-start(bf16[32,128]{1,0:T(8,128)(2,1)S(1)} %get-tuple-element.51), channel_id=1, source_target_pairs={{0,16},{64,80},{128,144},{192,208},{1,17},{65,81},{129,145},{193,2... | collective-permute-start | bytes 24584 | tf_op jit(solution)/shard_map/spread/ppermute | solution.py:290
  69.0 0.7 select_bitcast_fusion
  69.7 10.2 %collective-permute-done.19 = bf16[32,128]{1,0:T(8,128)(2,1)S(1)} collective-permute-done((bf16[32,128]{1,0:T(8,128)(2,1)S(1)}, bf16[32,128]{1,0:T(8,128)(2,1)S(1)}, u32[]{:S(2)}, u32[]{:S(2)}) %collective-permute-start.19) | collective-permute-done | bytes 8224 | tf_op jit(solution)/shard_map/spread/ppermute | solution.py:290
  (37 shorter events, 4.9 us)
Async XLA Ops:
  0.6 7.1 %copy-start.1 = (bf16[1,32,16,128]{3,2,1,0:T(8,128)(2,1)S(1)}, bf16[1,32,16,128]{3,2,1,0:T(8,128)(2,1)}, u32[]{:S(2)}) copy-start(bf16[1,32,16,128]{3,2,1,0:T(8,128)(2,1)} %param.8) | copy-start | bytes 393220
  0.6 7.0 %copy-start.4 = (s32[1,32,8]{1,2,0:T(8,128)S(1)}, s32[1,32,8]{1,2,0:T(8,128)}, u32[]{:S(2)}) copy-start(s32[1,32,8]{1,2,0:T(8,128)} %param.7) | copy-start | bytes 3076
  0.6 7.0 %collective-permute-start = (bf16[32,16,128]{2,1,0:T(8,128)(2,1)}, bf16[32,16,128]{2,1,0:T(8,128)(2,1)S(1)}, u32[]{:S(2)}, u32[]{:S(2)}) collective-permute-start(bf16[32,16,128]{2,1,0:T(8,128)(2,1)} %bitcast.34), channel_id=1, source_target_pairs={{0,16},{16,32},{32,48},{48,64},{64,80},{80,96},{96,112},{112,128},... | collective-permute-start | bytes 393224 | tf_op jit(solution)/shard_map/ppermute | solution.py:257
  2.7 12.6 %copy-start = (f32[32,128,128]{2,1,0:T(8,128)S(1)}, f32[32,128,128]{2,1,0:T(8,128)}, u32[]{:S(2)}) copy-start(f32[32,128,128]{2,1,0:T(8,128)} %inverse.1) | copy-start | bytes 6291460
  2.7 12.6 %copy-start.2 = (f32[2,32,1,256]{3,2,1,0:T(1,128)S(1)}, f32[2,32,1,256]{3,2,1,0:T(1,128)}, u32[]{:S(2)}) copy-start(f32[2,32,1,256]{3,2,1,0:T(1,128)} %incident.1) | copy-start | bytes 196612
  2.7 12.6 %copy-start.3 = (s32[32,256]{1,0:T(8,128)S(1)}, s32[32,256]{1,0:T(8,128)}, u32[]{:S(2)}) copy-start(s32[32,256]{1,0:T(8,128)} %element_map.1) | copy-start | bytes 98308
  11.4 4.7 %collective-permute-start.1 = (bf16[24,32,128]{2,1,0:T(8,128)(2,1)S(1)}, bf16[24,32,128]{2,1,0:T(8,128)(2,1)S(1)}, u32[]{:S(2)}, u32[]{:S(2)}) collective-permute-start(bf16[24,32,128]{2,1,0:T(8,128)(2,1)S(1)} %get-tuple-element.27), channel_id=1, source_target_pairs={{0,1},{1,0},{2,3},{3,2},{4,5},{5,4},{6,7},{7,6},{8,9},{9,8},{10,11... | collective-permute-start | bytes 589832 | tf_op jit(solution)/shard_map/halo/ppermute | solution.py:202
  11.5 8.5 %collective-permute-start.2 = (bf16[24,32,128]{2,1,0:T(8,128)(2,1)S(1)}, bf16[24,32,128]{2,1,0:T(8,128)(2,1)S(1)}, u32[]{:S(2)}, u32[]{:S(2)}) collective-permute-start(bf16[24,32,128]{2,1,0:T(8,128)(2,1)S(1)} %get-tuple-element.28), channel_id=1, source_target_pairs={{0,15},{1,2},{2,1},{3,4},{4,3},{5,6},{6,5},{7,8},{8,7},{9,10},{10,... | collective-permute-start | bytes 589832 | tf_op jit(solution)/shard_map/halo/ppermute | solution.py:202
  20.8 8.2 %collective-permute-start.3 = (bf16[8,32,128]{2,1,0:T(8,128)(2,1)S(1)}, bf16[8,32,128]{2,1,0:T(8,128)(2,1)S(1)}, u32[]{:S(2)}, u32[]{:S(2)}) collective-permute-start(bf16[8,32,128]{2,1,0:T(8,128)(2,1)S(1)} %get-tuple-element.31), channel_id=1, source_target_pairs={{0,16},{16,0},{32,48},{48,32},{64,80},{80,64},{96,112},{112,96},{1... | collective-permute-start | bytes 196616 | tf_op jit(solution)/shard_map/near/ppermute | solution.py:191
  26.4 4.3 %collective-permute-start.4 = (bf16[8,32,128]{2,1,0:T(8,128)(2,1)S(1)}, bf16[8,32,128]{2,1,0:T(8,128)(2,1)S(1)}, u32[]{:S(2)}, u32[]{:S(2)}) collective-permute-start(bf16[8,32,128]{2,1,0:T(8,128)(2,1)S(1)} %get-tuple-element.32), channel_id=1, source_target_pairs={{0,32},{16,48},{32,0},{48,16},{64,96},{80,112},{96,64},{112,80},{1... | collective-permute-start | bytes 196616 | tf_op jit(solution)/shard_map/near/ppermute | solution.py:191
  26.4 6.7 %collective-permute-start.5 = (bf16[8,32,128]{2,1,0:T(8,128)(2,1)S(1)}, bf16[8,32,128]{2,1,0:T(8,128)(2,1)S(1)}, u32[]{:S(2)}, u32[]{:S(2)}) collective-permute-start(bf16[8,32,128]{2,1,0:T(8,128)(2,1)S(1)} %get-tuple-element.33), channel_id=1, source_target_pairs={{0,48},{16,32},{32,16},{48,0},{64,112},{80,96},{96,80},{112,64},{1... | collective-permute-start | bytes 196616 | tf_op jit(solution)/shard_map/near/ppermute | solution.py:191
  33.1 8.4 %collective-permute-start.6 = (bf16[8,32,128]{2,1,0:T(8,128)(2,1)S(1)}, bf16[8,32,128]{2,1,0:T(8,128)(2,1)S(1)}, u32[]{:S(2)}, u32[]{:S(2)}) collective-permute-start(bf16[8,32,128]{2,1,0:T(8,128)(2,1)S(1)} %add_convert_fusion.1), channel_id=1, source_target_pairs={{0,128},{16,144},{32,160},{48,176},{64,192},{80,208},{96,224},{112... | collective-permute-start | bytes 196616 | tf_op jit(solution)/shard_map/far/ppermute | solution.py:191
  37.6 5.3 %collective-permute-start.7 = (bf16[8,32,128]{2,1,0:T(8,128)(2,1)S(1)}, bf16[8,32,128]{2,1,0:T(8,128)(2,1)S(1)}, u32[]{:S(2)}, u32[]{:S(2)}) collective-permute-start(bf16[8,32,128]{2,1,0:T(8,128)(2,1)S(1)} %add_convert_fusion.1), channel_id=1, source_target_pairs={{0,64},{16,80},{32,96},{48,112},{64,0},{80,16},{96,32},{112,48},{1... | collective-permute-start | bytes 196616 | tf_op jit(solution)/shard_map/far/ppermute | solution.py:191
  38.9 6.8 %collective-permute-start.8 = (bf16[8,32,128]{2,1,0:T(8,128)(2,1)S(1)}, bf16[8,32,128]{2,1,0:T(8,128)(2,1)S(1)}, u32[]{:S(2)}, u32[]{:S(2)}) collective-permute-start(bf16[8,32,128]{2,1,0:T(8,128)(2,1)S(1)} %add_convert_fusion.1), channel_id=1, source_target_pairs={{0,192},{16,208},{32,224},{48,240},{64,128},{80,144},{96,160},{112... | collective-permute-start | bytes 196616 | tf_op jit(solution)/shard_map/far/ppermute | solution.py:191
  45.8 5.1 %collective-permute-start.10 = (bf16[8,32,128]{2,1,0:T(8,128)(2,1)S(1)}, bf16[8,32,128]{2,1,0:T(8,128)(2,1)S(1)}, u32[]{:S(2)}, u32[]{:S(2)}) collective-permute-start(bf16[8,32,128]{2,1,0:T(8,128)(2,1)S(1)} %add_convert_fusion.rest0), channel_id=1, source_target_pairs={{0,32},{16,48},{32,0},{48,16},{64,96},{80,112},{96,64},{112,80},{1... | collective-permute-start | bytes 196616 | tf_op jit(solution)/shard_map/gather/ppermute | solution.py:191
  46.9 6.7 %collective-permute-start.11 = (bf16[8,32,128]{2,1,0:T(8,128)(2,1)S(1)}, bf16[8,32,128]{2,1,0:T(8,128)(2,1)S(1)}, u32[]{:S(2)}, u32[]{:S(2)}) collective-permute-start(bf16[8,32,128]{2,1,0:T(8,128)(2,1)S(1)} %add_convert_fusion.rest0), channel_id=1, source_target_pairs={{0,48},{16,32},{32,16},{48,0},{64,112},{80,96},{96,80},{112,64},{1... | collective-permute-start | bytes 196616 | tf_op jit(solution)/shard_map/gather/ppermute | solution.py:191
  49.4 5.8 %collective-permute-start.9 = (bf16[8,32,128]{2,1,0:T(8,128)(2,1)S(1)}, bf16[8,32,128]{2,1,0:T(8,128)(2,1)S(1)}, u32[]{:S(2)}, u32[]{:S(2)}) collective-permute-start(bf16[8,32,128]{2,1,0:T(8,128)(2,1)S(1)} %add_convert_fusion.rest0), channel_id=1, source_target_pairs={{0,16},{16,0},{32,48},{48,32},{64,80},{80,64},{96,112},{112,96},{1... | collective-permute-start | bytes 196616 | tf_op jit(solution)/shard_map/gather/ppermute | solution.py:191
  56.7 3.8 %collective-permute-start.12 = (bf16[24,16,128]{2,1,0:T(8,128)(2,1)S(1)}, bf16[24,16,128]{2,1,0:T(8,128)(2,1)S(1)}, u32[]{:S(2)}, u32[]{:S(2)}) collective-permute-start(bf16[24,16,128]{2,1,0:T(8,128)(2,1)S(1)} %get-tuple-element.41), channel_id=1, source_target_pairs={{0,1},{1,0},{2,3},{3,2},{4,5},{5,4},{6,7},{7,6},{8,9},{9,8},{10,11... | collective-permute-start | bytes 294920 | tf_op jit(solution)/shard_map/halo_extra/ppermute | solution.py:202
  56.8 7.0 %collective-permute-start.13 = (bf16[24,16,128]{2,1,0:T(8,128)(2,1)S(1)}, bf16[24,16,128]{2,1,0:T(8,128)(2,1)S(1)}, u32[]{:S(2)}, u32[]{:S(2)}) collective-permute-start(bf16[24,16,128]{2,1,0:T(8,128)(2,1)S(1)} %get-tuple-element.42), channel_id=1, source_target_pairs={{0,15},{1,2},{2,1},{3,4},{4,3},{5,6},{6,5},{7,8},{8,7},{9,10},{10,... | collective-permute-start | bytes 294920 | tf_op jit(solution)/shard_map/halo_extra/ppermute | solution.py:202
  58.9 10.1 %collective-permute-start.20 = (bf16[32,16,128]{2,1,0:T(8,128)(2,1)S(1)}, bf16[32,16,128]{2,1,0:T(8,128)(2,1)S(1)}, u32[]{:S(2)}, u32[]{:S(2)}) collective-permute-start(bf16[32,16,128]{2,1,0:T(8,128)(2,1)S(1)} %bitcast.36), channel_id=1, source_target_pairs={{0,32},{16,48},{32,64},{48,80},{64,96},{80,112},{96,128},{112,144}... | collective-permute-start | bytes 393224 | tf_op jit(solution)/shard_map/ppermute | solution.py:277
  64.3 2.0 %collective-permute-start.14 = (bf16[4,32,128]{2,1,0:T(8,128)(2,1)S(1)}, bf16[4,32,128]{2,1,0:T(8,128)(2,1)S(1)}, u32[]{:S(2)}, u32[]{:S(2)}) collective-permute-start(bf16[4,32,128]{2,1,0:T(8,128)(2,1)S(1)} %get-tuple-element.50), channel_id=1, source_target_pairs={{0,192},{1,193},{2,194},{3,195},{4,196},{5,197},{6,198},{7,199},{8... | collective-permute-start | bytes 98312 | tf_op jit(solution)/shard_map/spread/ppermute | solution.py:285
  64.9 1.4 %collective-permute-start.15 = (bf16[4,32,128]{2,1,0:T(8,128)(2,1)S(1)}, bf16[4,32,128]{2,1,0:T(8,128)(2,1)S(1)}, u32[]{:S(2)}, u32[]{:S(2)}) collective-permute-start(bf16[4,32,128]{2,1,0:T(8,128)(2,1)S(1)} %get-tuple-element.49), channel_id=1, source_target_pairs={{0,128},{1,129},{2,130},{3,131},{4,132},{5,133},{6,134},{7,135},{8... | collective-permute-start | bytes 98312 | tf_op jit(solution)/shard_map/spread/ppermute | solution.py:285
  65.6 0.7 collective-permute-start.16
  66.4 3.3 %collective-permute-start.17 = (bf16[32,128]{1,0:T(8,128)(2,1)S(1)}, bf16[32,128]{1,0:T(8,128)(2,1)S(1)}, u32[]{:S(2)}, u32[]{:S(2)}) collective-permute-start(bf16[32,128]{1,0:T(8,128)(2,1)S(1)} %get-tuple-element.53), channel_id=1, source_target_pairs={{0,48},{64,112},{128,176},{192,240},{1,49},{65,113},{129,177},{193... | collective-permute-start | bytes 24584 | tf_op jit(solution)/shard_map/spread/ppermute | solution.py:290
  67.0 2.7 %collective-permute-start.18 = (bf16[32,128]{1,0:T(8,128)(2,1)S(1)}, bf16[32,128]{1,0:T(8,128)(2,1)S(1)}, u32[]{:S(2)}, u32[]{:S(2)}) collective-permute-start(bf16[32,128]{1,0:T(8,128)(2,1)S(1)} %get-tuple-element.52), channel_id=1, source_target_pairs={{0,32},{64,96},{128,160},{192,224},{1,33},{65,97},{129,161},{193,2... | collective-permute-start | bytes 24584 | tf_op jit(solution)/shard_map/spread/ppermute | solution.py:290
  67.7 12.2 %collective-permute-start.19 = (bf16[32,128]{1,0:T(8,128)(2,1)S(1)}, bf16[32,128]{1,0:T(8,128)(2,1)S(1)}, u32[]{:S(2)}, u32[]{:S(2)}) collective-permute-start(bf16[32,128]{1,0:T(8,128)(2,1)S(1)} %get-tuple-element.51), channel_id=1, source_target_pairs={{0,16},{64,80},{128,144},{192,208},{1,17},{65,81},{129,145},{193,2... | collective-permute-start | bytes 24584 | tf_op jit(solution)/shard_map/spread/ppermute | solution.py:290

commit v5 on v4

--- a/solution.py
+++ b/solution.py
@@ -199,7 +199,8 @@
     n = lax.axis_size("col")
     pairs = [(i, i ^ 1) for i in range(n)]
     others = [(i, (i + 1 if i % 2 else i - 1) % n) for i in range(n)]
-    return lax.ppermute(first_out, "col", pairs), lax.ppermute(second_out, "col", others)
+    second_in = lax.ppermute(second_out, "col", others)
+    return lax.ppermute(first_out, "col", pairs), second_in
 
 
 def body(blocks, offsets, history, instant_inverse, incident, element_map):
@@ -265,11 +266,12 @@
     source, inverse_parts = prepare(incident, element_map, instant_inverse)
     keep, *sent = combine(place, main, first_in, second_in, source)
     with jax.named_scope("near"):
-        quarter = added(keep, [exchange(part, d) for d, part in zip((1, 2, 3), sent)])
+        quarter = added(keep, [exchange(sent[d - 1], d) for d in (3, 1, 2)])
     with jax.named_scope("far"):
         quarter = added(quarter, [exchange(quarter, d) for d in (8, 4, 12)])
     with jax.named_scope("gather"):
-        rest = [quarter] + [exchange(quarter, d) for d in (1, 2, 3)]
+        by_distance = {d: exchange(quarter, d) for d in (3, 1, 2)}
+        rest = [quarter] + [by_distance[d] for d in (1, 2, 3)]
     current0, extra, first_out, second_out = first_step(
         place, band_rows, *rest, inverse_parts, blocks
     )

time: 80.7 us -> 79.4 us (0.984)
  waiting for transfers between devices: 33.6 us -> 29.5 us
  starting transfers between devices: 32.5 us -> 35.2 us
    ppermute x9, waiting for transfers between devices: 15.4 us -> 12.7 us  [exchange(): return lax.ppermute(block, 'lag', [(i, i ^ distance) for i in range(16)])]
    ppermute x4, waiting for transfers between devices: 7.06 us -> 5.47 us  [the longest x2 5.46 us: trade(): second_in = lax.ppermute(second_out, 'col', others)]
    ppermute x9, starting transfers between devices: 18.9 us -> 20 us  [exchange(): return lax.ppermute(block, 'lag', [(i, i ^ distance) for i in range(16)])]
    ppermute x4, starting transfers between devices: 6.08 us -> 7.05 us  [the longest x2 6.86 us: trade(): second_in = lax.ppermute(second_out, 'col', others)]
  transfers between devices with their start and end apart: 21 -> 21, of which waited for: 12 -> 11; matrix products, arithmetic and copies ran while one was open for 1% -> 1% of each run, Pallas kernels for 8% -> 8%
where the time goes in v5:
time: 79.4 us; the launch traced here: 79.1 us
  starting transfers between devices  35.2 us (44%)
  waiting for transfers between devices  29.5 us (37%)
  Pallas kernels  12.1 us (15%)
  other arithmetic  1.48 us (2%)
  between operations  0.84 us (1%)
    ppermute x9, starting transfers between devices, exchange(): return lax.ppermute(block, 'lag', [(i, i ^ distance) for i in range(16)])  20 us
    ppermute x9, waiting for transfers between devices, exchange(): return lax.ppermute(block, 'lag', [(i, i ^ distance) for i in range(16)])  12.7 us
    ppermute x3, waiting for transfers between devices, body(): lax.ppermute(leader[d], 'lag', [(4 * g, 4 * g + d) for g in range(4)])  10.4 us
    ppermute x2, starting transfers between devices, trade(): second_in = lax.ppermute(second_out, 'col', others)  6.86 us
    ppermute x2, waiting for transfers between devices, trade(): second_in = lax.ppermute(second_out, 'col', others)  5.46 us
    pallas_call x1, Pallas kernels, body(): blocks, follows = fetch(place, blocks)  4.13 us
    pallas_call x1, Pallas kernels, body(): shell_sums(place, band_rows, shells, older, blocks, follows)  3.7 us
    ppermute x3, starting transfers between devices, body(): lax.ppermute(leader[d], 'lag', [(4 * g, 4 * g + d) for g in range(4)])  2.62 us
  transfers between devices with their start and end apart: 21, of which 11 were waited for; matrix products, arithmetic and copies ran while one was open for 1% of the time, Pallas kernels for 8%

profile of v5, /device:TPU:4, one launch (start us, length us, event | category | flops | bytes accessed | tf_op | source)
XLA Modules:
  0.0 79.1 jit_solution(13323857306637894118)
XLA Ops:
  0.6 1.9 %collective-permute-start = (bf16[32,16,128]{2,1,0:T(8,128)(2,1)}, bf16[32,16,128]{2,1,0:T(8,128)(2,1)S(1)}, u32[]{:S(2)}, u32[]{:S(2)}) collective-permute-start(bf16[32,16,128]{2,1,0:T(8,128)(2,1)} %bitcast.34), channel_id=1, source_target_pairs={{0,16},{16,32},{32,48},{48,64},{64,80},{80,96},{96,112},{112,128},... | collective-permute-start | bytes 393224 | tf_op jit(solution)/shard_map/ppermute | solution.py:258
  2.7 4.1 %fetch.1 = (bf16[32,8,128,128]{3,2,1,0:T(8,128)(2,1)S(1)}, bf16[16,128]{1,0:T(8,128)(2,1)S(1)}) custom-call(s32[3]{0:T(128)S(1)} %pad_add_fusion.place_ref, bf16[32,8,128,128]{3,2,1,0:T(8,128)(2,1)} %bitcast.39), custom_call_target="tpu_custom_call" | custom-call | tf_op jit(solution)/shard_map/shells/fetch/pallas_call | solution.py:260
  6.8 0.9 %collective-permute-done.older = bf16[32,16,128]{2,1,0:T(8,128)(2,1)S(1)} collective-permute-done((bf16[32,16,128]{2,1,0:T(8,128)(2,1)}, bf16[32,16,128]{2,1,0:T(8,128)(2,1)S(1)}, u32[]{:S(2)}, u32[]{:S(2)}) %collective-permute-start) | collective-permute-done | bytes 131104 | tf_op jit(solution)/shard_map/ppermute | solution.py:258
  7.7 3.7 %shell_sums.1 = (f32[32,32,128]{2,1,0:T(8,128)S(1)}, bf16[24,32,128]{2,1,0:T(8,128)(2,1)S(1)}, bf16[24,32,128]{2,1,0:T(8,128)(2,1)S(1)}, bf16[32,8,128,128]{3,2,1,0:T(8,128)(2,1)S(1)}) custom-call(s32[3]{0:T(128)S(1)} %pad_add_fusion.place_ref, s32[8,32]{1,0:T(8,128)S(1)} %bitcast.37, ...), custom_call_target="tpu_custom_call", output_to_operand_aliasing={{3}: (4, {})} | custom-call | tf_op jit(solution)/shard_map/shells/shell_sums/pallas_call | solution.py:261
  11.5 3.8 %collective-permute-start.2 = (bf16[24,32,128]{2,1,0:T(8,128)(2,1)S(1)}, bf16[24,32,128]{2,1,0:T(8,128)(2,1)S(1)}, u32[]{:S(2)}, u32[]{:S(2)}) collective-permute-start(bf16[24,32,128]{2,1,0:T(8,128)(2,1)S(1)} %get-tuple-element.28), channel_id=1, source_target_pairs={{0,15},{1,2},{2,1},{3,4},{4,3},{5,6},{6,5},{7,8},{8,7},{9,10},{10,... | collective-permute-start | bytes 589832 | tf_op jit(solution)/shard_map/halo/ppermute | solution.py:202
  15.3 0.9 %prepare.1 = (f32[2,32,128]{2,1,0:T(8,128)S(1)}, bf16[32,128,256]{2,1,0:T(8,128)(2,1)S(1)}) custom-call(f32[2,32,1,256]{3,2,1,0:T(1,128)S(1)} %copy-done.2, s32[32,256]{1,0:T(8,128)S(1)} %copy-done.3, f32[32,128,128]{2,1,0:T(8,128)S(1)} %copy-done), custom_call_target="tpu_custom_call" | custom-call | tf_op jit(solution)/shard_map/prepare/pallas_call | solution.py:266
  16.1 3.9 %collective-permute-done.2.second_in = bf16[24,32,128]{2,1,0:T(8,128)(2,1)S(1)} collective-permute-done((bf16[24,32,128]{2,1,0:T(8,128)(2,1)S(1)}, bf16[24,32,128]{2,1,0:T(8,128)(2,1)S(1)}, u32[]{:S(2)}, u32[]{:S(2)}) %collective-permute-start.2) | collective-permute-done | bytes 196640 | tf_op jit(solution)/shard_map/halo/ppermute | solution.py:202
  20.0 0.8 combine.1
  20.8 3.0 %collective-permute-start.3 = (bf16[8,32,128]{2,1,0:T(8,128)(2,1)S(1)}, bf16[8,32,128]{2,1,0:T(8,128)(2,1)S(1)}, u32[]{:S(2)}, u32[]{:S(2)}) collective-permute-start(bf16[8,32,128]{2,1,0:T(8,128)(2,1)S(1)} %get-tuple-element.31), channel_id=1, source_target_pairs={{0,48},{16,32},{32,16},{48,0},{64,112},{80,96},{96,80},{112,64},{1... | collective-permute-start | bytes 196616 | tf_op jit(solution)/shard_map/near/ppermute | solution.py:191
  23.8 2.7 %collective-permute-start.4 = (bf16[8,32,128]{2,1,0:T(8,128)(2,1)S(1)}, bf16[8,32,128]{2,1,0:T(8,128)(2,1)S(1)}, u32[]{:S(2)}, u32[]{:S(2)}) collective-permute-start(bf16[8,32,128]{2,1,0:T(8,128)(2,1)S(1)} %get-tuple-element.32), channel_id=1, source_target_pairs={{0,16},{16,0},{32,48},{48,32},{64,80},{80,64},{96,112},{112,96},{1... | collective-permute-start | bytes 196616 | tf_op jit(solution)/shard_map/near/ppermute | solution.py:191
  26.5 1.4 %collective-permute-start.5 = (bf16[8,32,128]{2,1,0:T(8,128)(2,1)S(1)}, bf16[8,32,128]{2,1,0:T(8,128)(2,1)S(1)}, u32[]{:S(2)}, u32[]{:S(2)}) collective-permute-start(bf16[8,32,128]{2,1,0:T(8,128)(2,1)S(1)} %get-tuple-element.33), channel_id=1, source_target_pairs={{0,32},{16,48},{32,0},{48,16},{64,96},{80,112},{96,64},{112,80},{1... | collective-permute-start | bytes 196616 | tf_op jit(solution)/shard_map/near/ppermute | solution.py:191
  27.9 1.7 %collective-permute-done.4 = bf16[8,32,128]{2,1,0:T(8,128)(2,1)S(1)} collective-permute-done((bf16[8,32,128]{2,1,0:T(8,128)(2,1)S(1)}, bf16[8,32,128]{2,1,0:T(8,128)(2,1)S(1)}, u32[]{:S(2)}, u32[]{:S(2)}) %collective-permute-start.4) | collective-permute-done | bytes 65568 | tf_op jit(solution)/shard_map/near/ppermute | solution.py:191
  29.5 1.3 %collective-permute-done.5 = bf16[8,32,128]{2,1,0:T(8,128)(2,1)S(1)} collective-permute-done((bf16[8,32,128]{2,1,0:T(8,128)(2,1)S(1)}, bf16[8,32,128]{2,1,0:T(8,128)(2,1)S(1)}, u32[]{:S(2)}, u32[]{:S(2)}) %collective-permute-start.5) | collective-permute-done | bytes 65568 | tf_op jit(solution)/shard_map/near/ppermute | solution.py:191
  30.8 5.6 %collective-permute-start.6 = (bf16[8,32,128]{2,1,0:T(8,128)(2,1)S(1)}, bf16[8,32,128]{2,1,0:T(8,128)(2,1)S(1)}, u32[]{:S(2)}, u32[]{:S(2)}) collective-permute-start(bf16[8,32,128]{2,1,0:T(8,128)(2,1)S(1)} %add_convert_fusion.1), channel_id=1, source_target_pairs={{0,128},{16,144},{32,160},{48,176},{64,192},{80,208},{96,224},{112... | collective-permute-start | bytes 196616 | tf_op jit(solution)/shard_map/far/ppermute | solution.py:191
  36.4 1.5 %collective-permute-start.7 = (bf16[8,32,128]{2,1,0:T(8,128)(2,1)S(1)}, bf16[8,32,128]{2,1,0:T(8,128)(2,1)S(1)}, u32[]{:S(2)}, u32[]{:S(2)}) collective-permute-start(bf16[8,32,128]{2,1,0:T(8,128)(2,1)S(1)} %add_convert_fusion.1), channel_id=1, source_target_pairs={{0,64},{16,80},{32,96},{48,112},{64,0},{80,16},{96,32},{112,48},{1... | collective-permute-start | bytes 196616 | tf_op jit(solution)/shard_map/far/ppermute | solution.py:191
  37.9 0.8 collective-permute-start.8
  39.1 3.5 %collective-permute-done.7 = bf16[8,32,128]{2,1,0:T(8,128)(2,1)S(1)} collective-permute-done((bf16[8,32,128]{2,1,0:T(8,128)(2,1)S(1)}, bf16[8,32,128]{2,1,0:T(8,128)(2,1)S(1)}, u32[]{:S(2)}, u32[]{:S(2)}) %collective-permute-start.7) | collective-permute-done | bytes 65568 | tf_op jit(solution)/shard_map/far/ppermute | solution.py:191
  42.6 1.7 %collective-permute-done.8 = bf16[8,32,128]{2,1,0:T(8,128)(2,1)S(1)} collective-permute-done((bf16[8,32,128]{2,1,0:T(8,128)(2,1)S(1)}, bf16[8,32,128]{2,1,0:T(8,128)(2,1)S(1)}, u32[]{:S(2)}, u32[]{:S(2)}) %collective-permute-start.8) | collective-permute-done | bytes 65568 | tf_op jit(solution)/shard_map/far/ppermute | solution.py:191
  44.4 1.8 %collective-permute-start.10 = (bf16[8,32,128]{2,1,0:T(8,128)(2,1)S(1)}, bf16[8,32,128]{2,1,0:T(8,128)(2,1)S(1)}, u32[]{:S(2)}, u32[]{:S(2)}) collective-permute-start(bf16[8,32,128]{2,1,0:T(8,128)(2,1)S(1)} %add_convert_fusion.rest0), channel_id=1, source_target_pairs={{0,32},{16,48},{32,0},{48,16},{64,96},{80,112},{96,64},{112,80},{1... | collective-permute-start | bytes 196616 | tf_op jit(solution)/shard_map/gather/ppermute | solution.py:191
  46.2 1.4 %collective-permute-start.11 = (bf16[8,32,128]{2,1,0:T(8,128)(2,1)S(1)}, bf16[8,32,128]{2,1,0:T(8,128)(2,1)S(1)}, u32[]{:S(2)}, u32[]{:S(2)}) collective-permute-start(bf16[8,32,128]{2,1,0:T(8,128)(2,1)S(1)} %add_convert_fusion.rest0), channel_id=1, source_target_pairs={{0,48},{16,32},{32,16},{48,0},{64,112},{80,96},{96,80},{112,64},{1... | collective-permute-start | bytes 196616 | tf_op jit(solution)/shard_map/gather/ppermute | solution.py:191
  47.6 1.9 %collective-permute-start.9 = (bf16[8,32,128]{2,1,0:T(8,128)(2,1)S(1)}, bf16[8,32,128]{2,1,0:T(8,128)(2,1)S(1)}, u32[]{:S(2)}, u32[]{:S(2)}) collective-permute-start(bf16[8,32,128]{2,1,0:T(8,128)(2,1)S(1)} %add_convert_fusion.rest0), channel_id=1, source_target_pairs={{0,16},{16,0},{32,48},{48,32},{64,80},{80,64},{96,112},{112,96},{1... | collective-permute-start | bytes 196616 | tf_op jit(solution)/shard_map/gather/ppermute | solution.py:191
  49.5 3.4 %collective-permute-done.11.rest3 = bf16[8,32,128]{2,1,0:T(8,128)(2,1)S(1)} collective-permute-done((bf16[8,32,128]{2,1,0:T(8,128)(2,1)S(1)}, bf16[8,32,128]{2,1,0:T(8,128)(2,1)S(1)}, u32[]{:S(2)}, u32[]{:S(2)}) %collective-permute-start.11) | collective-permute-done | bytes 65568 | tf_op jit(solution)/shard_map/gather/ppermute | solution.py:191
  52.9 0.7 collective-permute-done.9.rest1
  53.6 1.5 %first_step.1 = (bf16[32,16,128]{2,1,0:T(8,128)(2,1)S(1)}, f32[32,16,128]{2,1,0:T(8,128)S(1)}, bf16[24,16,128]{2,1,0:T(8,128)(2,1)S(1)}, bf16[24,16,128]{2,1,0:T(8,128)(2,1)S(1)}) custom-call(s32[3]{0:T(128)S(1)} %pad_add_fusion.place_ref, s32[8,32]{1,0:T(8,128)S(1)} %bitcast.38, bf16[8,32,128]{2,1,0:T(8,128)(2,1)S(1)} %add_convert_fusion.rest0, ...), custom_call_target="tpu_custom_call" | custom-call | tf_op jit(solution)/shard_map/first_step/pallas_call | solution.py:275
  55.1 3.1 %collective-permute-start.13 = (bf16[24,16,128]{2,1,0:T(8,128)(2,1)S(1)}, bf16[24,16,128]{2,1,0:T(8,128)(2,1)S(1)}, u32[]{:S(2)}, u32[]{:S(2)}) collective-permute-start(bf16[24,16,128]{2,1,0:T(8,128)(2,1)S(1)} %get-tuple-element.42), channel_id=1, source_target_pairs={{0,15},{1,2},{2,1},{3,4},{4,3},{5,6},{6,5},{7,8},{8,7},{9,10},{10,... | collective-permute-start | bytes 294920 | tf_op jit(solution)/shard_map/halo_extra/ppermute | solution.py:202
  58.2 1.6 %collective-permute-start.20 = (bf16[32,16,128]{2,1,0:T(8,128)(2,1)S(1)}, bf16[32,16,128]{2,1,0:T(8,128)(2,1)S(1)}, u32[]{:S(2)}, u32[]{:S(2)}) collective-permute-start(bf16[32,16,128]{2,1,0:T(8,128)(2,1)S(1)} %bitcast.36), channel_id=1, source_target_pairs={{0,32},{16,48},{32,64},{48,80},{64,96},{80,112},{96,128},{112,144}... | collective-permute-start | bytes 393224 | tf_op jit(solution)/shard_map/ppermute | solution.py:279
  60.5 1.6 %collective-permute-done.13.second_in = bf16[24,16,128]{2,1,0:T(8,128)(2,1)S(1)} collective-permute-done((bf16[24,16,128]{2,1,0:T(8,128)(2,1)S(1)}, bf16[24,16,128]{2,1,0:T(8,128)(2,1)S(1)}, u32[]{:S(2)}, u32[]{:S(2)}) %collective-permute-start.13) | collective-permute-done | bytes 98336 | tf_op jit(solution)/shard_map/halo_extra/ppermute | solution.py:202
  62.6 0.7 collective-permute-start.14
  63.3 0.7 collective-permute-start.15
  66.1 1.3 %collective-permute-start.19 = (bf16[32,128]{1,0:T(8,128)(2,1)S(1)}, bf16[32,128]{1,0:T(8,128)(2,1)S(1)}, u32[]{:S(2)}, u32[]{:S(2)}) collective-permute-start(bf16[32,128]{1,0:T(8,128)(2,1)S(1)} %get-tuple-element.51), channel_id=1, source_target_pairs={{0,16},{64,80},{128,144},{192,208},{1,17},{65,81},{129,145},{193,2... | collective-permute-start | bytes 24584 | tf_op jit(solution)/shard_map/spread/ppermute | solution.py:292
  67.4 0.7 select_bitcast_fusion
  68.1 10.4 %collective-permute-done.19 = bf16[32,128]{1,0:T(8,128)(2,1)S(1)} collective-permute-done((bf16[32,128]{1,0:T(8,128)(2,1)S(1)}, bf16[32,128]{1,0:T(8,128)(2,1)S(1)}, u32[]{:S(2)}, u32[]{:S(2)}) %collective-permute-start.19) | collective-permute-done | bytes 8224 | tf_op jit(solution)/shard_map/spread/ppermute | solution.py:292
  (37 shorter events, 4.7 us)
Async XLA Ops:
  0.6 7.1 %copy-start.1 = (bf16[1,32,16,128]{3,2,1,0:T(8,128)(2,1)S(1)}, bf16[1,32,16,128]{3,2,1,0:T(8,128)(2,1)}, u32[]{:S(2)}) copy-start(bf16[1,32,16,128]{3,2,1,0:T(8,128)(2,1)} %param.8) | copy-start | bytes 393220
  0.6 7.0 %copy-start.4 = (s32[1,32,8]{1,2,0:T(8,128)S(1)}, s32[1,32,8]{1,2,0:T(8,128)}, u32[]{:S(2)}) copy-start(s32[1,32,8]{1,2,0:T(8,128)} %param.7) | copy-start | bytes 3076
  0.6 7.0 %collective-permute-start = (bf16[32,16,128]{2,1,0:T(8,128)(2,1)}, bf16[32,16,128]{2,1,0:T(8,128)(2,1)S(1)}, u32[]{:S(2)}, u32[]{:S(2)}) collective-permute-start(bf16[32,16,128]{2,1,0:T(8,128)(2,1)} %bitcast.34), channel_id=1, source_target_pairs={{0,16},{16,32},{32,48},{48,64},{64,80},{80,96},{96,112},{112,128},... | collective-permute-start | bytes 393224 | tf_op jit(solution)/shard_map/ppermute | solution.py:258
  2.7 12.6 %copy-start = (f32[32,128,128]{2,1,0:T(8,128)S(1)}, f32[32,128,128]{2,1,0:T(8,128)}, u32[]{:S(2)}) copy-start(f32[32,128,128]{2,1,0:T(8,128)} %inverse.1) | copy-start | bytes 6291460
  2.7 12.6 %copy-start.2 = (f32[2,32,1,256]{3,2,1,0:T(1,128)S(1)}, f32[2,32,1,256]{3,2,1,0:T(1,128)}, u32[]{:S(2)}) copy-start(f32[2,32,1,256]{3,2,1,0:T(1,128)} %incident.1) | copy-start | bytes 196612
  2.7 12.6 %copy-start.3 = (s32[32,256]{1,0:T(8,128)S(1)}, s32[32,256]{1,0:T(8,128)}, u32[]{:S(2)}) copy-start(s32[32,256]{1,0:T(8,128)} %element_map.1) | copy-start | bytes 98308
  11.4 4.7 %collective-permute-start.1 = (bf16[24,32,128]{2,1,0:T(8,128)(2,1)S(1)}, bf16[24,32,128]{2,1,0:T(8,128)(2,1)S(1)}, u32[]{:S(2)}, u32[]{:S(2)}) collective-permute-start(bf16[24,32,128]{2,1,0:T(8,128)(2,1)S(1)} %get-tuple-element.27), channel_id=1, source_target_pairs={{0,1},{1,0},{2,3},{3,2},{4,5},{5,4},{6,7},{7,6},{8,9},{9,8},{10,11... | collective-permute-start | bytes 589832 | tf_op jit(solution)/shard_map/halo/ppermute | solution.py:203
  11.5 8.5 %collective-permute-start.2 = (bf16[24,32,128]{2,1,0:T(8,128)(2,1)S(1)}, bf16[24,32,128]{2,1,0:T(8,128)(2,1)S(1)}, u32[]{:S(2)}, u32[]{:S(2)}) collective-permute-start(bf16[24,32,128]{2,1,0:T(8,128)(2,1)S(1)} %get-tuple-element.28), channel_id=1, source_target_pairs={{0,15},{1,2},{2,1},{3,4},{4,3},{5,6},{6,5},{7,8},{8,7},{9,10},{10,... | collective-permute-start | bytes 589832 | tf_op jit(solution)/shard_map/halo/ppermute | solution.py:202
  20.8 7.1 %collective-permute-start.3 = (bf16[8,32,128]{2,1,0:T(8,128)(2,1)S(1)}, bf16[8,32,128]{2,1,0:T(8,128)(2,1)S(1)}, u32[]{:S(2)}, u32[]{:S(2)}) collective-permute-start(bf16[8,32,128]{2,1,0:T(8,128)(2,1)S(1)} %get-tuple-element.31), channel_id=1, source_target_pairs={{0,48},{16,32},{32,16},{48,0},{64,112},{80,96},{96,80},{112,64},{1... | collective-permute-start | bytes 196616 | tf_op jit(solution)/shard_map/near/ppermute | solution.py:191
  23.8 5.8 %collective-permute-start.4 = (bf16[8,32,128]{2,1,0:T(8,128)(2,1)S(1)}, bf16[8,32,128]{2,1,0:T(8,128)(2,1)S(1)}, u32[]{:S(2)}, u32[]{:S(2)}) collective-permute-start(bf16[8,32,128]{2,1,0:T(8,128)(2,1)S(1)} %get-tuple-element.32), channel_id=1, source_target_pairs={{0,16},{16,0},{32,48},{48,32},{64,80},{80,64},{96,112},{112,96},{1... | collective-permute-start | bytes 196616 | tf_op jit(solution)/shard_map/near/ppermute | solution.py:191
  26.5 4.3 %collective-permute-start.5 = (bf16[8,32,128]{2,1,0:T(8,128)(2,1)S(1)}, bf16[8,32,128]{2,1,0:T(8,128)(2,1)S(1)}, u32[]{:S(2)}, u32[]{:S(2)}) collective-permute-start(bf16[8,32,128]{2,1,0:T(8,128)(2,1)S(1)} %get-tuple-element.33), channel_id=1, source_target_pairs={{0,32},{16,48},{32,0},{48,16},{64,96},{80,112},{96,64},{112,80},{1... | collective-permute-start | bytes 196616 | tf_op jit(solution)/shard_map/near/ppermute | solution.py:191
  30.8 8.3 %collective-permute-start.6 = (bf16[8,32,128]{2,1,0:T(8,128)(2,1)S(1)}, bf16[8,32,128]{2,1,0:T(8,128)(2,1)S(1)}, u32[]{:S(2)}, u32[]{:S(2)}) collective-permute-start(bf16[8,32,128]{2,1,0:T(8,128)(2,1)S(1)} %add_convert_fusion.1), channel_id=1, source_target_pairs={{0,128},{16,144},{32,160},{48,176},{64,192},{80,208},{96,224},{112... | collective-permute-start | bytes 196616 | tf_op jit(solution)/shard_map/far/ppermute | solution.py:191
  36.4 6.2 %collective-permute-start.7 = (bf16[8,32,128]{2,1,0:T(8,128)(2,1)S(1)}, bf16[8,32,128]{2,1,0:T(8,128)(2,1)S(1)}, u32[]{:S(2)}, u32[]{:S(2)}) collective-permute-start(bf16[8,32,128]{2,1,0:T(8,128)(2,1)S(1)} %add_convert_fusion.1), channel_id=1, source_target_pairs={{0,64},{16,80},{32,96},{48,112},{64,0},{80,16},{96,32},{112,48},{1... | collective-permute-start | bytes 196616 | tf_op jit(solution)/shard_map/far/ppermute | solution.py:191
  37.9 6.5 %collective-permute-start.8 = (bf16[8,32,128]{2,1,0:T(8,128)(2,1)S(1)}, bf16[8,32,128]{2,1,0:T(8,128)(2,1)S(1)}, u32[]{:S(2)}, u32[]{:S(2)}) collective-permute-start(bf16[8,32,128]{2,1,0:T(8,128)(2,1)S(1)} %add_convert_fusion.1), channel_id=1, source_target_pairs={{0,192},{16,208},{32,224},{48,240},{64,128},{80,144},{96,160},{112... | collective-permute-start | bytes 196616 | tf_op jit(solution)/shard_map/far/ppermute | solution.py:191
  44.4 5.1 %collective-permute-start.10 = (bf16[8,32,128]{2,1,0:T(8,128)(2,1)S(1)}, bf16[8,32,128]{2,1,0:T(8,128)(2,1)S(1)}, u32[]{:S(2)}, u32[]{:S(2)}) collective-permute-start(bf16[8,32,128]{2,1,0:T(8,128)(2,1)S(1)} %add_convert_fusion.rest0), channel_id=1, source_target_pairs={{0,32},{16,48},{32,0},{48,16},{64,96},{80,112},{96,64},{112,80},{1... | collective-permute-start | bytes 196616 | tf_op jit(solution)/shard_map/gather/ppermute | solution.py:191
  46.2 6.7 %collective-permute-start.11 = (bf16[8,32,128]{2,1,0:T(8,128)(2,1)S(1)}, bf16[8,32,128]{2,1,0:T(8,128)(2,1)S(1)}, u32[]{:S(2)}, u32[]{:S(2)}) collective-permute-start(bf16[8,32,128]{2,1,0:T(8,128)(2,1)S(1)} %add_convert_fusion.rest0), channel_id=1, source_target_pairs={{0,48},{16,32},{32,16},{48,0},{64,112},{80,96},{96,80},{112,64},{1... | collective-permute-start | bytes 196616 | tf_op jit(solution)/shard_map/gather/ppermute | solution.py:191
  47.6 6.0 %collective-permute-start.9 = (bf16[8,32,128]{2,1,0:T(8,128)(2,1)S(1)}, bf16[8,32,128]{2,1,0:T(8,128)(2,1)S(1)}, u32[]{:S(2)}, u32[]{:S(2)}) collective-permute-start(bf16[8,32,128]{2,1,0:T(8,128)(2,1)S(1)} %add_convert_fusion.rest0), channel_id=1, source_target_pairs={{0,16},{16,0},{32,48},{48,32},{64,80},{80,64},{96,112},{112,96},{1... | collective-permute-start | bytes 196616 | tf_op jit(solution)/shard_map/gather/ppermute | solution.py:191
  55.0 5.4 %collective-permute-start.12 = (bf16[24,16,128]{2,1,0:T(8,128)(2,1)S(1)}, bf16[24,16,128]{2,1,0:T(8,128)(2,1)S(1)}, u32[]{:S(2)}, u32[]{:S(2)}) collective-permute-start(bf16[24,16,128]{2,1,0:T(8,128)(2,1)S(1)} %get-tuple-element.41), channel_id=1, source_target_pairs={{0,1},{1,0},{2,3},{3,2},{4,5},{5,4},{6,7},{7,6},{8,9},{9,8},{10,11... | collective-permute-start | bytes 294920 | tf_op jit(solution)/shard_map/halo_extra/ppermute | solution.py:203
  55.1 6.9 %collective-permute-start.13 = (bf16[24,16,128]{2,1,0:T(8,128)(2,1)S(1)}, bf16[24,16,128]{2,1,0:T(8,128)(2,1)S(1)}, u32[]{:S(2)}, u32[]{:S(2)}) collective-permute-start(bf16[24,16,128]{2,1,0:T(8,128)(2,1)S(1)} %get-tuple-element.42), channel_id=1, source_target_pairs={{0,15},{1,2},{2,1},{3,4},{4,3},{5,6},{6,5},{7,8},{8,7},{9,10},{10,... | collective-permute-start | bytes 294920 | tf_op jit(solution)/shard_map/halo_extra/ppermute | solution.py:202
  58.2 9.1 %collective-permute-start.20 = (bf16[32,16,128]{2,1,0:T(8,128)(2,1)S(1)}, bf16[32,16,128]{2,1,0:T(8,128)(2,1)S(1)}, u32[]{:S(2)}, u32[]{:S(2)}) collective-permute-start(bf16[32,16,128]{2,1,0:T(8,128)(2,1)S(1)} %bitcast.36), channel_id=1, source_target_pairs={{0,32},{16,48},{32,64},{48,80},{64,96},{80,112},{96,128},{112,144}... | collective-permute-start | bytes 393224 | tf_op jit(solution)/shard_map/ppermute | solution.py:279
  62.6 2.0 %collective-permute-start.14 = (bf16[4,32,128]{2,1,0:T(8,128)(2,1)S(1)}, bf16[4,32,128]{2,1,0:T(8,128)(2,1)S(1)}, u32[]{:S(2)}, u32[]{:S(2)}) collective-permute-start(bf16[4,32,128]{2,1,0:T(8,128)(2,1)S(1)} %get-tuple-element.50), channel_id=1, source_target_pairs={{0,192},{1,193},{2,194},{3,195},{4,196},{5,197},{6,198},{7,199},{8... | collective-permute-start | bytes 98312 | tf_op jit(solution)/shard_map/spread/ppermute | solution.py:287
  63.3 1.4 %collective-permute-start.15 = (bf16[4,32,128]{2,1,0:T(8,128)(2,1)S(1)}, bf16[4,32,128]{2,1,0:T(8,128)(2,1)S(1)}, u32[]{:S(2)}, u32[]{:S(2)}) collective-permute-start(bf16[4,32,128]{2,1,0:T(8,128)(2,1)S(1)} %get-tuple-element.49), channel_id=1, source_target_pairs={{0,128},{1,129},{2,130},{3,131},{4,132},{5,133},{6,134},{7,135},{8... | collective-permute-start | bytes 98312 | tf_op jit(solution)/shard_map/spread/ppermute | solution.py:287
  64.0 0.7 collective-permute-start.16
  64.7 3.3 %collective-permute-start.17 = (bf16[32,128]{1,0:T(8,128)(2,1)S(1)}, bf16[32,128]{1,0:T(8,128)(2,1)S(1)}, u32[]{:S(2)}, u32[]{:S(2)}) collective-permute-start(bf16[32,128]{1,0:T(8,128)(2,1)S(1)} %get-tuple-element.53), channel_id=1, source_target_pairs={{0,48},{64,112},{128,176},{192,240},{1,49},{65,113},{129,177},{193... | collective-permute-start | bytes 24584 | tf_op jit(solution)/shard_map/spread/ppermute | solution.py:292
  65.4 2.7 %collective-permute-start.18 = (bf16[32,128]{1,0:T(8,128)(2,1)S(1)}, bf16[32,128]{1,0:T(8,128)(2,1)S(1)}, u32[]{:S(2)}, u32[]{:S(2)}) collective-permute-start(bf16[32,128]{1,0:T(8,128)(2,1)S(1)} %get-tuple-element.52), channel_id=1, source_target_pairs={{0,32},{64,96},{128,160},{192,224},{1,33},{65,97},{129,161},{193,2... | collective-permute-start | bytes 24584 | tf_op jit(solution)/shard_map/spread/ppermute | solution.py:292
  66.1 12.4 %collective-permute-start.19 = (bf16[32,128]{1,0:T(8,128)(2,1)S(1)}, bf16[32,128]{1,0:T(8,128)(2,1)S(1)}, u32[]{:S(2)}, u32[]{:S(2)}) collective-permute-start(bf16[32,128]{1,0:T(8,128)(2,1)S(1)} %get-tuple-element.51), channel_id=1, source_target_pairs={{0,16},{64,80},{128,144},{192,208},{1,17},{65,81},{129,145},{193,2... | collective-permute-start | bytes 24584 | tf_op jit(solution)/shard_map/spread/ppermute | solution.py:292

commit v6 on v5

--- a/solution.py
+++ b/solution.py
@@ -13,7 +13,6 @@
 NT = (((1,), (1,)), ((), ()))
 VMEM = pl.BlockSpec(memory_space=pltpu.VMEM)
 HBM = pl.BlockSpec(memory_space=pltpu.HBM)
-SMEM = pl.BlockSpec(memory_space=pltpu.SMEM)
 
 
 def split(x):
@@ -24,7 +23,6 @@
 def banded(place_ref, offsets_ref, rows_of, blocks, window, total_blocks):
     block_cols, width, size, _ = blocks.shape
     first = place_ref[0]
-    window[...] = jnp.zeros_like(window)
     for c in range(block_cols):
         column = blocks[c].reshape(width * size, size)
         prod = lax.dot_general(rows_of(c), column, NT, preferred_element_type=F32)
@@ -67,11 +65,16 @@
 
 
 def shells_kernel(
-    total_blocks, place_ref, offsets_ref, shells, older, blocks, follows,
-    main, first_out, second_out, kept, window,
-):
+    total_blocks, place_ref, offsets_in, shells, older, blocks, follows,
+    main, first_out, second_out, kept, window, offsets_ref, sem,
+):
+    fetched = pltpu.make_async_copy(offsets_in, offsets_ref, sem)
+    fetched.start()
+    window[...] = jnp.zeros_like(window)
+    fetched.wait()
     banded(
-        place_ref, offsets_ref, lambda c: jnp.concatenate([shells[c], older[c] * follows[...]], 0),
+        place_ref, offsets_ref,
+        lambda c: jnp.concatenate([shells[c], older[c] * follows[...]], 0),
         blocks, window, total_blocks,
     )
     hand_out(place_ref, window, main, first_out, second_out)
@@ -132,16 +135,20 @@
 
 
 def first_step_kernel(
-    total_blocks, place_ref, offsets_ref, rest0, rest1, rest2, rest3, inverse_parts, blocks,
-    current, main, first_out, second_out, rest, window,
+    total_blocks, place_ref, offsets_in, rest0, rest1, rest2, rest3, inverse_parts, blocks,
+    current, main, first_out, second_out, rest, window, offsets_ref, sem,
 ):
     n, pulses, size = current.shape
+    fetched = pltpu.make_async_copy(offsets_in, offsets_ref, sem)
+    fetched.start()
     gathered(place_ref, (rest0, rest1, rest2, rest3), rest)
     for b in range(n):
         current[b] = solve(rest[b, :pulses].astype(F32), inverse_parts[b]).astype(BF16)
+    fetched.wait()
 
     @pl.when(place_ref[1] == 0)
     def _():
+        window[...] = jnp.zeros_like(window)
         banded(place_ref, offsets_ref, lambda c: current[c], blocks, window, total_blocks)
         hand_out(place_ref, window, main, first_out, second_out)
 
@@ -174,9 +181,13 @@
             by_pulse[p] = scratch[pl.ds(p, n, stride=pulses), :].astype(BF16)
 
 
-def call(kernel, name, out_shape, in_specs, scratch_shapes=(), mib=16, aliases={}):
+def call(kernel, name, out_shape, in_specs, scratch_shapes=(), mib=16, aliases={}, cols=None):
+    def placed(*refs):
+        col = lax.axis_index("col")
+        kernel((col * cols, lax.axis_index("lag"), lax.rem(col, 2)), *refs)
+
     return pl.pallas_call(
-        kernel,
+        kernel if cols is None else placed,
         name=name,
         out_shape=out_shape,
         in_specs=in_specs,
@@ -208,8 +219,6 @@
     lags = lax.axis_size("lag")
     n, pulses, size = history.shape[1:]
     total_blocks = n * lax.axis_size("col")
-    col_index = lax.axis_index("col")
-    place = jnp.stack([col_index * n, lag_index, col_index % 2]).astype(jnp.int32)
     blocks = blocks[0]
     band_rows = offsets[0].T
     shells = history[0]
@@ -225,13 +234,14 @@
         return pltpu.VMEM((n + 2 * HALF, rows, size), F32)
 
     kept = shape(*blocks.shape, dtype=BF16)
+    offsets_here = [pltpu.SMEM(band_rows.shape, jnp.int32), pltpu.SemaphoreType.DMA]
     fetch = call(
-        fetch_kernel, "fetch", (kept, shape(pulses, size, dtype=BF16)), [SMEM, HBM], [pltpu.SemaphoreType.DMA((8,))], mib=40
+        fetch_kernel, "fetch", (kept, shape(pulses, size, dtype=BF16)), [HBM], [pltpu.SemaphoreType.DMA((8,))], mib=40, cols=n
     )
     shell_sums = call(
         functools.partial(shells_kernel, total_blocks), "shell_sums",
-        partial_out(2 * pulses) + (kept,), [SMEM, SMEM] + [VMEM] * 4, [window(2 * pulses)],
-        aliases={4: 3},
+        partial_out(2 * pulses) + (kept,), [VMEM] * 5, [window(2 * pulses)] + offsets_here,
+        aliases={3: 3}, cols=n,
     )
     prepare = call(
         prepare_kernel, "prepare",
@@ -239,32 +249,32 @@
     )
     quarters = (shape(n // 4, 2 * pulses, size, dtype=BF16),) * 4
     rows = pltpu.VMEM((n, 2 * pulses, size), BF16)
-    combine = call(combine_kernel, "combine", quarters, [SMEM] + [VMEM] * 4, [rows])
+    combine = call(combine_kernel, "combine", quarters, [VMEM] * 4, [rows], cols=n)
     first_step = call(
         functools.partial(first_step_kernel, total_blocks), "first_step",
         (shape(n, pulses, size, dtype=BF16),) + partial_out(pulses),
-        [SMEM, SMEM] + [VMEM] * 6, [rows, window(pulses)],
+        [VMEM] * 7, [rows, window(pulses)] + offsets_here, cols=n,
     )
     second_sum = call(
         second_sum_kernel, "second_sum",
-        (shape(n, pulses, size), shape(n, size)), [SMEM] + [VMEM] * 6, [rows],
+        (shape(n, pulses, size), shape(n, size)), [VMEM] * 6, [rows], cols=n,
     )
     second_step = call(
         second_step_kernel, "second_step",
         (shape(n, pulses, size, dtype=BF16), shape(pulses, n, size, dtype=BF16)),
-        [SMEM] + [VMEM] * 4, [pltpu.VMEM((n * pulses, size), F32)],
+        [VMEM] * 4, [pltpu.VMEM((n * pulses, size), F32)], cols=n,
     )
 
     older = lax.ppermute(shells, "lag", [(i, (i + 1) % lags) for i in range(lags)])
     with jax.named_scope("shells"):
-        blocks, follows = fetch(place, blocks)
+        blocks, follows = fetch(blocks)
         main, first_out, second_out, blocks = shell_sums(
-            place, band_rows, shells, older, blocks, follows
+            band_rows, shells, older, blocks, follows
         )
     with jax.named_scope("halo"):
         first_in, second_in = trade(first_out, second_out)
     source, inverse_parts = prepare(incident, element_map, instant_inverse)
-    keep, *sent = combine(place, main, first_in, second_in, source)
+    keep, *sent = combine(main, first_in, second_in, source)
     with jax.named_scope("near"):
         quarter = added(keep, [exchange(sent[d - 1], d) for d in (3, 1, 2)])
     with jax.named_scope("far"):
@@ -273,14 +283,14 @@
         by_distance = {d: exchange(quarter, d) for d in (3, 1, 2)}
         rest = [quarter] + [by_distance[d] for d in (1, 2, 3)]
     current0, extra, first_out, second_out = first_step(
-        place, band_rows, *rest, inverse_parts, blocks
+        band_rows, *rest, inverse_parts, blocks
     )
     shells, current0 = lax.optimization_barrier((shells, current0))
     oldest = lax.ppermute(shells, "lag", [(i, (i + 2) % lags) for i in range(lags)])
     with jax.named_scope("halo_extra"):
         first_in, second_in = trade(first_out, second_out)
-    total, own0 = second_sum(place, *rest, extra, current0)
-    current1, by_pulse1 = second_step(place, total, first_in, second_in, inverse_parts)
+    total, own0 = second_sum(*rest, extra, current0)
+    current1, by_pulse1 = second_step(total, first_in, second_in, inverse_parts)
     with jax.named_scope("spread"):
         quarter = pulses // 4
         groups = [by_pulse1[quarter * g : quarter * (g + 1)] for g in range(4)]

time: 79.4 us -> 77.5 us (0.976)
  waiting for transfers between devices: 29.5 us -> 32.5 us
  Pallas kernels: 12.1 us -> 9.41 us
  starting transfers between devices: 35.2 us -> 33.2 us
    pallas_call x6, Pallas kernels: 11.2 us -> 8.55 us  [the longest x1 3.66 us: body(): shell_sums(band_rows, shells, older, blocks, follows)]
    ppermute x2, waiting for transfers between devices: 5.46 us -> 7.06 us  [trade(): second_in = lax.ppermute(second_out, 'col', others)]
    ppermute x1, starting transfers between devices: 1.59 us -> 0.61 us  [body(): lax.ppermute(shells, 'lag', [(i, (i + 2) % lags) for i in range(lags)])]
    ppermute x9, waiting for transfers between devices: 12.7 us -> 13.7 us  [exchange(): return lax.ppermute(block, 'lag', [(i, i ^ distance) for i in range(16)])]
    ppermute x9, starting transfers between devices: 20 us -> 19 us  [exchange(): return lax.ppermute(block, 'lag', [(i, i ^ distance) for i in range(16)])]
  transfers between devices with their start and end apart: 21 -> 21, of which waited for: 11 -> 11; matrix products, arithmetic and copies ran while one was open for 1% -> 1% of each run, Pallas kernels for 8% -> 6%
where the time goes in v6:
time: 77.5 us; the launch traced here: 77.3 us
  starting transfers between devices  33.2 us (43%)
  waiting for transfers between devices  32.5 us (42%)
  Pallas kernels  9.41 us (12%)
  other arithmetic  1.39 us (2%)
  between operations  0.83 us (1%)
    ppermute x9, starting transfers between devices, exchange(): return lax.ppermute(block, 'lag', [(i, i ^ distance) for i in range(16)])  19 us
    ppermute x9, waiting for transfers between devices, exchange(): return lax.ppermute(block, 'lag', [(i, i ^ distance) for i in range(16)])  13.7 us
    ppermute x3, waiting for transfers between devices, body(): lax.ppermute(leader[d], 'lag', [(4 * g, 4 * g + d) for g in range(4)])  10.2 us
    ppermute x2, waiting for transfers between devices, trade(): second_in = lax.ppermute(second_out, 'col', others)  7.06 us
    ppermute x2, starting transfers between devices, trade(): second_in = lax.ppermute(second_out, 'col', others)  6.84 us
    pallas_call x1, Pallas kernels, body(): shell_sums(band_rows, shells, older, blocks, follows)  3.66 us
    pallas_call x1, Pallas kernels, body(): blocks, follows = fetch(blocks)  3.62 us
    ppermute x3, starting transfers between devices, body(): lax.ppermute(leader[d], 'lag', [(4 * g, 4 * g + d) for g in range(4)])  2.62 us
  transfers between devices with their start and end apart: 21, of which 11 were waited for; matrix products, arithmetic and copies ran while one was open for 1% of the time, Pallas kernels for 6%

profile of v6, /device:TPU:4, one launch (start us, length us, event | category | flops | bytes accessed | tf_op | source)
XLA Modules:
  0.0 77.3 jit_solution(8726051154066540763)
XLA Ops:
  0.7 1.9 %collective-permute-start = (bf16[32,16,128]{2,1,0:T(8,128)(2,1)}, bf16[32,16,128]{2,1,0:T(8,128)(2,1)S(1)}, u32[]{:S(2)}, u32[]{:S(2)}) collective-permute-start(bf16[32,16,128]{2,1,0:T(8,128)(2,1)} %bitcast.31), channel_id=1, source_target_pairs={{0,16},{16,32},{32,48},{48,64},{64,80},{80,96},{96,112},{112,128},... | collective-permute-start | bytes 393224 | tf_op jit(solution)/shard_map/ppermute | solution.py:268
  2.6 3.6 %fetch.1 = (bf16[32,8,128,128]{3,2,1,0:T(8,128)(2,1)S(1)}, bf16[16,128]{1,0:T(8,128)(2,1)S(1)}) custom-call(bf16[32,8,128,128]{3,2,1,0:T(8,128)(2,1)} %bitcast.36), custom_call_target="tpu_custom_call" | custom-call | tf_op jit(solution)/shard_map/shells/fetch/pallas_call | solution.py:270
  6.2 1.5 %collective-permute-done.refs_2_ = bf16[32,16,128]{2,1,0:T(8,128)(2,1)S(1)} collective-permute-done((bf16[32,16,128]{2,1,0:T(8,128)(2,1)}, bf16[32,16,128]{2,1,0:T(8,128)(2,1)S(1)}, u32[]{:S(2)}, u32[]{:S(2)}) %collective-permute-start) | collective-permute-done | bytes 131104 | tf_op jit(solution)/shard_map/ppermute | solution.py:268
  7.7 3.7 %shell_sums.1 = (f32[32,32,128]{2,1,0:T(8,128)S(1)}, bf16[24,32,128]{2,1,0:T(8,128)(2,1)S(1)}, bf16[24,32,128]{2,1,0:T(8,128)(2,1)S(1)}, bf16[32,8,128,128]{3,2,1,0:T(8,128)(2,1)S(1)}) custom-call(s32[8,32]{1,0:T(8,128)S(1)} %bitcast.34, bf16[32,16,128]{2,1,0:T(8,128)(2,1)S(1)} %bitcast.32, ...), custom_call_target="tpu_custom_call", output_to_operand_aliasing={{3}: (3, {})} | custom-call | tf_op jit(solution)/shard_map/shells/shell_sums/pallas_call | solution.py:271
  11.5 3.7 %collective-permute-start.2 = (bf16[24,32,128]{2,1,0:T(8,128)(2,1)S(1)}, bf16[24,32,128]{2,1,0:T(8,128)(2,1)S(1)}, u32[]{:S(2)}, u32[]{:S(2)}) collective-permute-start(bf16[24,32,128]{2,1,0:T(8,128)(2,1)S(1)} %get-tuple-element.28), channel_id=1, source_target_pairs={{0,15},{1,2},{2,1},{3,4},{4,3},{5,6},{6,5},{7,8},{8,7},{9,10},{10,... | collective-permute-start | bytes 589832 | tf_op jit(solution)/shard_map/halo/ppermute | solution.py:213
  15.2 0.9 %prepare.1 = (f32[2,32,128]{2,1,0:T(8,128)S(1)}, bf16[32,128,256]{2,1,0:T(8,128)(2,1)S(1)}) custom-call(f32[2,32,1,256]{3,2,1,0:T(1,128)S(1)} %copy-done.2, s32[32,256]{1,0:T(8,128)S(1)} %copy-done.3, f32[32,128,128]{2,1,0:T(8,128)S(1)} %copy-done), custom_call_target="tpu_custom_call" | custom-call | tf_op jit(solution)/shard_map/prepare/pallas_call | solution.py:276
  16.1 3.9 %collective-permute-done.2.refs_2_ = bf16[24,32,128]{2,1,0:T(8,128)(2,1)S(1)} collective-permute-done((bf16[24,32,128]{2,1,0:T(8,128)(2,1)S(1)}, bf16[24,32,128]{2,1,0:T(8,128)(2,1)S(1)}, u32[]{:S(2)}, u32[]{:S(2)}) %collective-permute-start.2) | collective-permute-done | bytes 196640 | tf_op jit(solution)/shard_map/halo/ppermute | solution.py:213
  20.2 3.0 %collective-permute-start.3 = (bf16[8,32,128]{2,1,0:T(8,128)(2,1)S(1)}, bf16[8,32,128]{2,1,0:T(8,128)(2,1)S(1)}, u32[]{:S(2)}, u32[]{:S(2)}) collective-permute-start(bf16[8,32,128]{2,1,0:T(8,128)(2,1)S(1)} %get-tuple-element.31), channel_id=1, source_target_pairs={{0,48},{16,32},{32,16},{48,0},{64,112},{80,96},{96,80},{112,64},{1... | collective-permute-start | bytes 196616 | tf_op jit(solution)/shard_map/near/ppermute | solution.py:202
  23.2 2.7 %collective-permute-start.4 = (bf16[8,32,128]{2,1,0:T(8,128)(2,1)S(1)}, bf16[8,32,128]{2,1,0:T(8,128)(2,1)S(1)}, u32[]{:S(2)}, u32[]{:S(2)}) collective-permute-start(bf16[8,32,128]{2,1,0:T(8,128)(2,1)S(1)} %get-tuple-element.32), channel_id=1, source_target_pairs={{0,16},{16,0},{32,48},{48,32},{64,80},{80,64},{96,112},{112,96},{1... | collective-permute-start | bytes 196616 | tf_op jit(solution)/shard_map/near/ppermute | solution.py:202
  25.9 1.4 %collective-permute-start.5 = (bf16[8,32,128]{2,1,0:T(8,128)(2,1)S(1)}, bf16[8,32,128]{2,1,0:T(8,128)(2,1)S(1)}, u32[]{:S(2)}, u32[]{:S(2)}) collective-permute-start(bf16[8,32,128]{2,1,0:T(8,128)(2,1)S(1)} %get-tuple-element.33), channel_id=1, source_target_pairs={{0,32},{16,48},{32,0},{48,16},{64,96},{80,112},{96,64},{112,80},{1... | collective-permute-start | bytes 196616 | tf_op jit(solution)/shard_map/near/ppermute | solution.py:202
  27.3 1.7 %collective-permute-done.4 = bf16[8,32,128]{2,1,0:T(8,128)(2,1)S(1)} collective-permute-done((bf16[8,32,128]{2,1,0:T(8,128)(2,1)S(1)}, bf16[8,32,128]{2,1,0:T(8,128)(2,1)S(1)}, u32[]{:S(2)}, u32[]{:S(2)}) %collective-permute-start.4) | collective-permute-done | bytes 65568 | tf_op jit(solution)/shard_map/near/ppermute | solution.py:202
  29.0 1.6 %collective-permute-done.5 = bf16[8,32,128]{2,1,0:T(8,128)(2,1)S(1)} collective-permute-done((bf16[8,32,128]{2,1,0:T(8,128)(2,1)S(1)}, bf16[8,32,128]{2,1,0:T(8,128)(2,1)S(1)}, u32[]{:S(2)}, u32[]{:S(2)}) %collective-permute-start.5) | collective-permute-done | bytes 65568 | tf_op jit(solution)/shard_map/near/ppermute | solution.py:202
  30.6 5.3 %collective-permute-start.6 = (bf16[8,32,128]{2,1,0:T(8,128)(2,1)S(1)}, bf16[8,32,128]{2,1,0:T(8,128)(2,1)S(1)}, u32[]{:S(2)}, u32[]{:S(2)}) collective-permute-start(bf16[8,32,128]{2,1,0:T(8,128)(2,1)S(1)} %add_convert_fusion.1), channel_id=1, source_target_pairs={{0,128},{16,144},{32,160},{48,176},{64,192},{80,208},{96,224},{112... | collective-permute-start | bytes 196616 | tf_op jit(solution)/shard_map/far/ppermute | solution.py:202
  35.8 1.5 %collective-permute-start.7 = (bf16[8,32,128]{2,1,0:T(8,128)(2,1)S(1)}, bf16[8,32,128]{2,1,0:T(8,128)(2,1)S(1)}, u32[]{:S(2)}, u32[]{:S(2)}) collective-permute-start(bf16[8,32,128]{2,1,0:T(8,128)(2,1)S(1)} %add_convert_fusion.1), channel_id=1, source_target_pairs={{0,64},{16,80},{32,96},{48,112},{64,0},{80,16},{96,32},{112,48},{1... | collective-permute-start | bytes 196616 | tf_op jit(solution)/shard_map/far/ppermute | solution.py:202
  37.4 1.4 %collective-permute-done.6 = bf16[8,32,128]{2,1,0:T(8,128)(2,1)S(1)} collective-permute-done((bf16[8,32,128]{2,1,0:T(8,128)(2,1)S(1)}, bf16[8,32,128]{2,1,0:T(8,128)(2,1)S(1)}, u32[]{:S(2)}, u32[]{:S(2)}) %collective-permute-start.6) | collective-permute-done | bytes 65568 | tf_op jit(solution)/shard_map/far/ppermute | solution.py:202
  38.8 2.3 %collective-permute-done.7 = bf16[8,32,128]{2,1,0:T(8,128)(2,1)S(1)} collective-permute-done((bf16[8,32,128]{2,1,0:T(8,128)(2,1)S(1)}, bf16[8,32,128]{2,1,0:T(8,128)(2,1)S(1)}, u32[]{:S(2)}, u32[]{:S(2)}) %collective-permute-start.7) | collective-permute-done | bytes 65568 | tf_op jit(solution)/shard_map/far/ppermute | solution.py:202
  41.1 2.7 %collective-permute-done.8 = bf16[8,32,128]{2,1,0:T(8,128)(2,1)S(1)} collective-permute-done((bf16[8,32,128]{2,1,0:T(8,128)(2,1)S(1)}, bf16[8,32,128]{2,1,0:T(8,128)(2,1)S(1)}, u32[]{:S(2)}, u32[]{:S(2)}) %collective-permute-start.8) | collective-permute-done | bytes 65568 | tf_op jit(solution)/shard_map/far/ppermute | solution.py:202
  43.8 1.8 %collective-permute-start.10 = (bf16[8,32,128]{2,1,0:T(8,128)(2,1)S(1)}, bf16[8,32,128]{2,1,0:T(8,128)(2,1)S(1)}, u32[]{:S(2)}, u32[]{:S(2)}) collective-permute-start(bf16[8,32,128]{2,1,0:T(8,128)(2,1)S(1)} %add_convert_fusion.refs_1_.refs_0_), channel_id=1, source_target_pairs={{0,32},{16,48},{32,0},{48,16},{64,96},{80,112},{96,64},{112,80},{1... | collective-permute-start | bytes 196616 | tf_op jit(solution)/shard_map/gather/ppermute | solution.py:202
  45.6 1.4 %collective-permute-start.11 = (bf16[8,32,128]{2,1,0:T(8,128)(2,1)S(1)}, bf16[8,32,128]{2,1,0:T(8,128)(2,1)S(1)}, u32[]{:S(2)}, u32[]{:S(2)}) collective-permute-start(bf16[8,32,128]{2,1,0:T(8,128)(2,1)S(1)} %add_convert_fusion.refs_1_.refs_0_), channel_id=1, source_target_pairs={{0,48},{16,32},{32,16},{48,0},{64,112},{80,96},{96,80},{112,64},{1... | collective-permute-start | bytes 196616 | tf_op jit(solution)/shard_map/gather/ppermute | solution.py:202
  47.0 2.0 %collective-permute-start.9 = (bf16[8,32,128]{2,1,0:T(8,128)(2,1)S(1)}, bf16[8,32,128]{2,1,0:T(8,128)(2,1)S(1)}, u32[]{:S(2)}, u32[]{:S(2)}) collective-permute-start(bf16[8,32,128]{2,1,0:T(8,128)(2,1)S(1)} %add_convert_fusion.refs_1_.refs_0_), channel_id=1, source_target_pairs={{0,16},{16,0},{32,48},{48,32},{64,80},{80,64},{96,112},{112,96},{1... | collective-permute-start | bytes 196616 | tf_op jit(solution)/shard_map/gather/ppermute | solution.py:202
  48.9 3.4 %collective-permute-done.11.refs_4_.refs_3_ = bf16[8,32,128]{2,1,0:T(8,128)(2,1)S(1)} collective-permute-done((bf16[8,32,128]{2,1,0:T(8,128)(2,1)S(1)}, bf16[8,32,128]{2,1,0:T(8,128)(2,1)S(1)}, u32[]{:S(2)}, u32[]{:S(2)}) %collective-permute-start.11) | collective-permute-done | bytes 65568 | tf_op jit(solution)/shard_map/gather/ppermute | solution.py:202
  52.3 0.7 collective-permute-done.9.refs_2_.refs_1_
  53.0 1.0 %first_step.1 = (bf16[32,16,128]{2,1,0:T(8,128)(2,1)S(1)}, f32[32,16,128]{2,1,0:T(8,128)S(1)}, bf16[24,16,128]{2,1,0:T(8,128)(2,1)S(1)}, bf16[24,16,128]{2,1,0:T(8,128)(2,1)S(1)}) custom-call(s32[8,32]{1,0:T(8,128)S(1)} %bitcast.35, bf16[8,32,128]{2,1,0:T(8,128)(2,1)S(1)} %add_convert_fusion.refs_1_.refs_0_, ...), custom_call_target="tpu_custom_call" | custom-call | tf_op jit(solution)/shard_map/first_step/pallas_call | solution.py:285
  54.1 3.1 %collective-permute-start.13 = (bf16[24,16,128]{2,1,0:T(8,128)(2,1)S(1)}, bf16[24,16,128]{2,1,0:T(8,128)(2,1)S(1)}, u32[]{:S(2)}, u32[]{:S(2)}) collective-permute-start(bf16[24,16,128]{2,1,0:T(8,128)(2,1)S(1)} %get-tuple-element.42), channel_id=1, source_target_pairs={{0,15},{1,2},{2,1},{3,4},{4,3},{5,6},{6,5},{7,8},{8,7},{9,10},{10,... | collective-permute-start | bytes 294920 | tf_op jit(solution)/shard_map/halo_extra/ppermute | solution.py:213
  57.9 3.2 %collective-permute-done.13.refs_2_ = bf16[24,16,128]{2,1,0:T(8,128)(2,1)S(1)} collective-permute-done((bf16[24,16,128]{2,1,0:T(8,128)(2,1)S(1)}, bf16[24,16,128]{2,1,0:T(8,128)(2,1)S(1)}, u32[]{:S(2)}, u32[]{:S(2)}) %collective-permute-start.13) | collective-permute-done | bytes 98336 | tf_op jit(solution)/shard_map/halo_extra/ppermute | solution.py:213
  61.0 0.7 collective-permute-start.14
  61.7 0.7 collective-permute-start.15
  62.4 0.7 collective-permute-start.16
  63.1 0.7 collective-permute-start.17
  64.5 1.3 %collective-permute-start.19 = (bf16[32,128]{1,0:T(8,128)(2,1)S(1)}, bf16[32,128]{1,0:T(8,128)(2,1)S(1)}, u32[]{:S(2)}, u32[]{:S(2)}) collective-permute-start(bf16[32,128]{1,0:T(8,128)(2,1)S(1)} %get-tuple-element.51), channel_id=1, source_target_pairs={{0,16},{64,80},{128,144},{192,208},{1,17},{65,81},{129,145},{193,2... | collective-permute-start | bytes 24584 | tf_op jit(solution)/shard_map/spread/ppermute | solution.py:302
  65.8 0.7 select_bitcast_fusion
  66.5 10.2 %collective-permute-done.19 = bf16[32,128]{1,0:T(8,128)(2,1)S(1)} collective-permute-done((bf16[32,128]{1,0:T(8,128)(2,1)S(1)}, bf16[32,128]{1,0:T(8,128)(2,1)S(1)}, u32[]{:S(2)}, u32[]{:S(2)}) %collective-permute-start.19) | collective-permute-done | bytes 8224 | tf_op jit(solution)/shard_map/spread/ppermute | solution.py:302
  (36 shorter events, 2.6 us)
Async XLA Ops:
  0.6 7.1 %copy-start.1 = (bf16[1,32,16,128]{3,2,1,0:T(8,128)(2,1)S(1)}, bf16[1,32,16,128]{3,2,1,0:T(8,128)(2,1)}, u32[]{:S(2)}) copy-start(bf16[1,32,16,128]{3,2,1,0:T(8,128)(2,1)} %param.8) | copy-start | bytes 393220
  0.6 7.0 %copy-start.4 = (s32[1,32,8]{1,2,0:T(8,128)S(1)}, s32[1,32,8]{1,2,0:T(8,128)}, u32[]{:S(2)}) copy-start(s32[1,32,8]{1,2,0:T(8,128)} %param.7) | copy-start | bytes 3076
  0.7 7.0 %collective-permute-start = (bf16[32,16,128]{2,1,0:T(8,128)(2,1)}, bf16[32,16,128]{2,1,0:T(8,128)(2,1)S(1)}, u32[]{:S(2)}, u32[]{:S(2)}) collective-permute-start(bf16[32,16,128]{2,1,0:T(8,128)(2,1)} %bitcast.31), channel_id=1, source_target_pairs={{0,16},{16,32},{32,48},{48,64},{64,80},{80,96},{96,112},{112,128},... | collective-permute-start | bytes 393224 | tf_op jit(solution)/shard_map/ppermute | solution.py:268
  2.6 12.6 %copy-start = (f32[32,128,128]{2,1,0:T(8,128)S(1)}, f32[32,128,128]{2,1,0:T(8,128)}, u32[]{:S(2)}) copy-start(f32[32,128,128]{2,1,0:T(8,128)} %inverse.1) | copy-start | bytes 6291460
  2.6 12.6 %copy-start.2 = (f32[2,32,1,256]{3,2,1,0:T(1,128)S(1)}, f32[2,32,1,256]{3,2,1,0:T(1,128)}, u32[]{:S(2)}) copy-start(f32[2,32,1,256]{3,2,1,0:T(1,128)} %incident.1) | copy-start | bytes 196612
  2.6 12.6 %copy-start.3 = (s32[32,256]{1,0:T(8,128)S(1)}, s32[32,256]{1,0:T(8,128)}, u32[]{:S(2)}) copy-start(s32[32,256]{1,0:T(8,128)} %element_map.1) | copy-start | bytes 98308
  11.4 4.7 %collective-permute-start.1 = (bf16[24,32,128]{2,1,0:T(8,128)(2,1)S(1)}, bf16[24,32,128]{2,1,0:T(8,128)(2,1)S(1)}, u32[]{:S(2)}, u32[]{:S(2)}) collective-permute-start(bf16[24,32,128]{2,1,0:T(8,128)(2,1)S(1)} %get-tuple-element.27), channel_id=1, source_target_pairs={{0,1},{1,0},{2,3},{3,2},{4,5},{5,4},{6,7},{7,6},{8,9},{9,8},{10,11... | collective-permute-start | bytes 589832 | tf_op jit(solution)/shard_map/halo/ppermute | solution.py:214
  11.5 8.5 %collective-permute-start.2 = (bf16[24,32,128]{2,1,0:T(8,128)(2,1)S(1)}, bf16[24,32,128]{2,1,0:T(8,128)(2,1)S(1)}, u32[]{:S(2)}, u32[]{:S(2)}) collective-permute-start(bf16[24,32,128]{2,1,0:T(8,128)(2,1)S(1)} %get-tuple-element.28), channel_id=1, source_target_pairs={{0,15},{1,2},{2,1},{3,4},{4,3},{5,6},{6,5},{7,8},{8,7},{9,10},{10,... | collective-permute-start | bytes 589832 | tf_op jit(solution)/shard_map/halo/ppermute | solution.py:213
  20.2 7.1 %collective-permute-start.3 = (bf16[8,32,128]{2,1,0:T(8,128)(2,1)S(1)}, bf16[8,32,128]{2,1,0:T(8,128)(2,1)S(1)}, u32[]{:S(2)}, u32[]{:S(2)}) collective-permute-start(bf16[8,32,128]{2,1,0:T(8,128)(2,1)S(1)} %get-tuple-element.31), channel_id=1, source_target_pairs={{0,48},{16,32},{32,16},{48,0},{64,112},{80,96},{96,80},{112,64},{1... | collective-permute-start | bytes 196616 | tf_op jit(solution)/shard_map/near/ppermute | solution.py:202
  23.2 5.8 %collective-permute-start.4 = (bf16[8,32,128]{2,1,0:T(8,128)(2,1)S(1)}, bf16[8,32,128]{2,1,0:T(8,128)(2,1)S(1)}, u32[]{:S(2)}, u32[]{:S(2)}) collective-permute-start(bf16[8,32,128]{2,1,0:T(8,128)(2,1)S(1)} %get-tuple-element.32), channel_id=1, source_target_pairs={{0,16},{16,0},{32,48},{48,32},{64,80},{80,64},{96,112},{112,96},{1... | collective-permute-start | bytes 196616 | tf_op jit(solution)/shard_map/near/ppermute | solution.py:202
  25.9 4.6 %collective-permute-start.5 = (bf16[8,32,128]{2,1,0:T(8,128)(2,1)S(1)}, bf16[8,32,128]{2,1,0:T(8,128)(2,1)S(1)}, u32[]{:S(2)}, u32[]{:S(2)}) collective-permute-start(bf16[8,32,128]{2,1,0:T(8,128)(2,1)S(1)} %get-tuple-element.33), channel_id=1, source_target_pairs={{0,32},{16,48},{32,0},{48,16},{64,96},{80,112},{96,64},{112,80},{1... | collective-permute-start | bytes 196616 | tf_op jit(solution)/shard_map/near/ppermute | solution.py:202
  30.6 8.3 %collective-permute-start.6 = (bf16[8,32,128]{2,1,0:T(8,128)(2,1)S(1)}, bf16[8,32,128]{2,1,0:T(8,128)(2,1)S(1)}, u32[]{:S(2)}, u32[]{:S(2)}) collective-permute-start(bf16[8,32,128]{2,1,0:T(8,128)(2,1)S(1)} %add_convert_fusion.1), channel_id=1, source_target_pairs={{0,128},{16,144},{32,160},{48,176},{64,192},{80,208},{96,224},{112... | collective-permute-start | bytes 196616 | tf_op jit(solution)/shard_map/far/ppermute | solution.py:202
  35.8 5.3 %collective-permute-start.7 = (bf16[8,32,128]{2,1,0:T(8,128)(2,1)S(1)}, bf16[8,32,128]{2,1,0:T(8,128)(2,1)S(1)}, u32[]{:S(2)}, u32[]{:S(2)}) collective-permute-start(bf16[8,32,128]{2,1,0:T(8,128)(2,1)S(1)} %add_convert_fusion.1), channel_id=1, source_target_pairs={{0,64},{16,80},{32,96},{48,112},{64,0},{80,16},{96,32},{112,48},{1... | collective-permute-start | bytes 196616 | tf_op jit(solution)/shard_map/far/ppermute | solution.py:202
  37.3 6.5 %collective-permute-start.8 = (bf16[8,32,128]{2,1,0:T(8,128)(2,1)S(1)}, bf16[8,32,128]{2,1,0:T(8,128)(2,1)S(1)}, u32[]{:S(2)}, u32[]{:S(2)}) collective-permute-start(bf16[8,32,128]{2,1,0:T(8,128)(2,1)S(1)} %add_convert_fusion.1), channel_id=1, source_target_pairs={{0,192},{16,208},{32,224},{48,240},{64,128},{80,144},{96,160},{112... | collective-permute-start | bytes 196616 | tf_op jit(solution)/shard_map/far/ppermute | solution.py:202
  43.8 5.1 %collective-permute-start.10 = (bf16[8,32,128]{2,1,0:T(8,128)(2,1)S(1)}, bf16[8,32,128]{2,1,0:T(8,128)(2,1)S(1)}, u32[]{:S(2)}, u32[]{:S(2)}) collective-permute-start(bf16[8,32,128]{2,1,0:T(8,128)(2,1)S(1)} %add_convert_fusion.refs_1_.refs_0_), channel_id=1, source_target_pairs={{0,32},{16,48},{32,0},{48,16},{64,96},{80,112},{96,64},{112,80},{1... | collective-permute-start | bytes 196616 | tf_op jit(solution)/shard_map/gather/ppermute | solution.py:202
  45.6 6.7 %collective-permute-start.11 = (bf16[8,32,128]{2,1,0:T(8,128)(2,1)S(1)}, bf16[8,32,128]{2,1,0:T(8,128)(2,1)S(1)}, u32[]{:S(2)}, u32[]{:S(2)}) collective-permute-start(bf16[8,32,128]{2,1,0:T(8,128)(2,1)S(1)} %add_convert_fusion.refs_1_.refs_0_), channel_id=1, source_target_pairs={{0,48},{16,32},{32,16},{48,0},{64,112},{80,96},{96,80},{112,64},{1... | collective-permute-start | bytes 196616 | tf_op jit(solution)/shard_map/gather/ppermute | solution.py:202
  47.0 6.0 %collective-permute-start.9 = (bf16[8,32,128]{2,1,0:T(8,128)(2,1)S(1)}, bf16[8,32,128]{2,1,0:T(8,128)(2,1)S(1)}, u32[]{:S(2)}, u32[]{:S(2)}) collective-permute-start(bf16[8,32,128]{2,1,0:T(8,128)(2,1)S(1)} %add_convert_fusion.refs_1_.refs_0_), channel_id=1, source_target_pairs={{0,16},{16,0},{32,48},{48,32},{64,80},{80,64},{96,112},{112,96},{1... | collective-permute-start | bytes 196616 | tf_op jit(solution)/shard_map/gather/ppermute | solution.py:202
  54.0 3.9 %collective-permute-start.12 = (bf16[24,16,128]{2,1,0:T(8,128)(2,1)S(1)}, bf16[24,16,128]{2,1,0:T(8,128)(2,1)S(1)}, u32[]{:S(2)}, u32[]{:S(2)}) collective-permute-start(bf16[24,16,128]{2,1,0:T(8,128)(2,1)S(1)} %get-tuple-element.41), channel_id=1, source_target_pairs={{0,1},{1,0},{2,3},{3,2},{4,5},{5,4},{6,7},{7,6},{8,9},{9,8},{10,11... | collective-permute-start | bytes 294920 | tf_op jit(solution)/shard_map/halo_extra/ppermute | solution.py:214
  54.1 7.0 %collective-permute-start.13 = (bf16[24,16,128]{2,1,0:T(8,128)(2,1)S(1)}, bf16[24,16,128]{2,1,0:T(8,128)(2,1)S(1)}, u32[]{:S(2)}, u32[]{:S(2)}) collective-permute-start(bf16[24,16,128]{2,1,0:T(8,128)(2,1)S(1)} %get-tuple-element.42), channel_id=1, source_target_pairs={{0,15},{1,2},{2,1},{3,4},{4,3},{5,6},{6,5},{7,8},{8,7},{9,10},{10,... | collective-permute-start | bytes 294920 | tf_op jit(solution)/shard_map/halo_extra/ppermute | solution.py:213
  57.2 8.6 %collective-permute-start.20 = (bf16[32,16,128]{2,1,0:T(8,128)(2,1)S(1)}, bf16[32,16,128]{2,1,0:T(8,128)(2,1)S(1)}, u32[]{:S(2)}, u32[]{:S(2)}) collective-permute-start(bf16[32,16,128]{2,1,0:T(8,128)(2,1)S(1)} %bitcast.33), channel_id=1, source_target_pairs={{0,32},{16,48},{32,64},{48,80},{64,96},{80,112},{96,128},{112,144}... | collective-permute-start | bytes 393224 | tf_op jit(solution)/shard_map/ppermute | solution.py:289
  61.0 2.0 %collective-permute-start.14 = (bf16[4,32,128]{2,1,0:T(8,128)(2,1)S(1)}, bf16[4,32,128]{2,1,0:T(8,128)(2,1)S(1)}, u32[]{:S(2)}, u32[]{:S(2)}) collective-permute-start(bf16[4,32,128]{2,1,0:T(8,128)(2,1)S(1)} %get-tuple-element.50), channel_id=1, source_target_pairs={{0,192},{1,193},{2,194},{3,195},{4,196},{5,197},{6,198},{7,199},{8... | collective-permute-start | bytes 98312 | tf_op jit(solution)/shard_map/spread/ppermute | solution.py:297
  61.7 1.4 %collective-permute-start.15 = (bf16[4,32,128]{2,1,0:T(8,128)(2,1)S(1)}, bf16[4,32,128]{2,1,0:T(8,128)(2,1)S(1)}, u32[]{:S(2)}, u32[]{:S(2)}) collective-permute-start(bf16[4,32,128]{2,1,0:T(8,128)(2,1)S(1)} %get-tuple-element.49), channel_id=1, source_target_pairs={{0,128},{1,129},{2,130},{3,131},{4,132},{5,133},{6,134},{7,135},{8... | collective-permute-start | bytes 98312 | tf_op jit(solution)/shard_map/spread/ppermute | solution.py:297
  62.4 0.7 collective-permute-start.16
  63.1 3.3 %collective-permute-start.17 = (bf16[32,128]{1,0:T(8,128)(2,1)S(1)}, bf16[32,128]{1,0:T(8,128)(2,1)S(1)}, u32[]{:S(2)}, u32[]{:S(2)}) collective-permute-start(bf16[32,128]{1,0:T(8,128)(2,1)S(1)} %get-tuple-element.53), channel_id=1, source_target_pairs={{0,48},{64,112},{128,176},{192,240},{1,49},{65,113},{129,177},{193... | collective-permute-start | bytes 24584 | tf_op jit(solution)/shard_map/spread/ppermute | solution.py:302
  63.8 2.7 %collective-permute-start.18 = (bf16[32,128]{1,0:T(8,128)(2,1)S(1)}, bf16[32,128]{1,0:T(8,128)(2,1)S(1)}, u32[]{:S(2)}, u32[]{:S(2)}) collective-permute-start(bf16[32,128]{1,0:T(8,128)(2,1)S(1)} %get-tuple-element.52), channel_id=1, source_target_pairs={{0,32},{64,96},{128,160},{192,224},{1,33},{65,97},{129,161},{193,2... | collective-permute-start | bytes 24584 | tf_op jit(solution)/shard_map/spread/ppermute | solution.py:302
  64.5 12.2 %collective-permute-start.19 = (bf16[32,128]{1,0:T(8,128)(2,1)S(1)}, bf16[32,128]{1,0:T(8,128)(2,1)S(1)}, u32[]{:S(2)}, u32[]{:S(2)}) collective-permute-start(bf16[32,128]{1,0:T(8,128)(2,1)S(1)} %get-tuple-element.51), channel_id=1, source_target_pairs={{0,16},{64,80},{128,144},{192,208},{1,17},{65,81},{129,145},{193,2... | collective-permute-start | bytes 24584 | tf_op jit(solution)/shard_map/spread/ppermute | solution.py:302

commit v7 on v6

--- a/solution.py
+++ b/solution.py
@@ -134,8 +134,18 @@
     return out[:pulses] + out[pulses:]
 
 
+def far_sum_kernel(place_ref, own, far1, far2, far3, inverse_parts, out):
+    rows, both, size = own.shape
+    pulses = both // 2
+    inverse = inverse_parts.at[quarter_of(place_ref, 0, inverse_parts.shape[0])]
+    for b in range(rows):
+        total = sum(part[b].astype(F32) for part in (far1, far2, far3)) + own[b].astype(F32)
+        out[b, :pulses] = solve(total[:pulses], inverse[b]).astype(BF16)
+        out[b, pulses:] = total[pulses:].astype(BF16)
+
+
 def first_step_kernel(
-    total_blocks, place_ref, offsets_in, rest0, rest1, rest2, rest3, inverse_parts, blocks,
+    total_blocks, place_ref, offsets_in, rest0, rest1, rest2, rest3, blocks,
     current, main, first_out, second_out, rest, window, offsets_ref, sem,
 ):
     n, pulses, size = current.shape
@@ -143,12 +153,12 @@
     fetched.start()
     gathered(place_ref, (rest0, rest1, rest2, rest3), rest)
     for b in range(n):
-        current[b] = solve(rest[b, :pulses].astype(F32), inverse_parts[b]).astype(BF16)
+        current[b] = rest[b, :pulses]
+    window[...] = jnp.zeros_like(window)
     fetched.wait()
 
     @pl.when(place_ref[1] == 0)
     def _():
-        window[...] = jnp.zeros_like(window)
         banded(place_ref, offsets_ref, lambda c: current[c], blocks, window, total_blocks)
         hand_out(place_ref, window, main, first_out, second_out)
 
@@ -250,10 +260,11 @@
     quarters = (shape(n // 4, 2 * pulses, size, dtype=BF16),) * 4
     rows = pltpu.VMEM((n, 2 * pulses, size), BF16)
     combine = call(combine_kernel, "combine", quarters, [VMEM] * 4, [rows], cols=n)
+    far_sum = call(far_sum_kernel, "far_sum", quarters[:1], [VMEM] * 5, cols=n)
     first_step = call(
         functools.partial(first_step_kernel, total_blocks), "first_step",
         (shape(n, pulses, size, dtype=BF16),) + partial_out(pulses),
-        [VMEM] * 7, [rows, window(pulses)] + offsets_here, cols=n,
+        [VMEM] * 6, [rows, window(pulses)] + offsets_here, cols=n,
     )
     second_sum = call(
         second_sum_kernel, "second_sum",
@@ -278,12 +289,13 @@
     with jax.named_scope("near"):
         quarter = added(keep, [exchange(sent[d - 1], d) for d in (3, 1, 2)])
     with jax.named_scope("far"):
-        quarter = added(quarter, [exchange(quarter, d) for d in (8, 4, 12)])
+        far = [exchange(quarter, d) for d in (8, 4, 12)]
+        (quarter,) = far_sum(quarter, *far, inverse_parts)
     with jax.named_scope("gather"):
         by_distance = {d: exchange(quarter, d) for d in (3, 1, 2)}
         rest = [quarter] + [by_distance[d] for d in (1, 2, 3)]
     current0, extra, first_out, second_out = first_step(
-        band_rows, *rest, inverse_parts, blocks
+        band_rows, *rest, blocks
     )
     shells, current0 = lax.optimization_barrier((shells, current0))
     oldest = lax.ppermute(shells, "lag", [(i, (i + 2) % lags) for i in range(lags)])

time: 77.5 us -> 77.5 us (level)
  no operation moved by 1% of the time
where the time goes in v7:
time: 77.5 us; the launch traced here: 77.3 us
  starting transfers between devices  33.2 us (43%)
  waiting for transfers between devices  32.4 us (42%)
  Pallas kernels  9.51 us (12%)
  other arithmetic  1.35 us (2%)
  between operations  0.83 us (1%)
    ppermute x9, starting transfers between devices, exchange(): return lax.ppermute(block, 'lag', [(i, i ^ distance) for i in range(16)])  19 us
    ppermute x9, waiting for transfers between devices, exchange(): return lax.ppermute(block, 'lag', [(i, i ^ distance) for i in range(16)])  13.7 us
    ppermute x3, waiting for transfers between devices, body(): lax.ppermute(leader[d], 'lag', [(4 * g, 4 * g + d) for g in range(4)])  10.1 us
    ppermute x2, waiting for transfers between devices, trade(): second_in = lax.ppermute(second_out, 'col', others)  7.12 us
    ppermute x2, starting transfers between devices, trade(): second_in = lax.ppermute(second_out, 'col', others)  6.84 us
    pallas_call x1, Pallas kernels, body(): shell_sums(band_rows, shells, older, blocks, follows)  3.66 us
    pallas_call x1, Pallas kernels, body(): blocks, follows = fetch(blocks)  3.62 us
    ppermute x3, starting transfers between devices, body(): lax.ppermute(leader[d], 'lag', [(4 * g, 4 * g + d) for g in range(4)])  2.62 us
  transfers between devices with their start and end apart: 21, of which 11 were waited for; matrix products, arithmetic and copies ran while one was open for 1% of the time, Pallas kernels for 6%

profile of v7, /device:TPU:4, one launch (start us, length us, event | category | flops | bytes accessed | tf_op | source)
XLA Modules:
  0.0 77.3 jit_solution(15762978141877722372)
XLA Ops:
  0.7 1.9 %collective-permute-start = (bf16[32,16,128]{2,1,0:T(8,128)(2,1)}, bf16[32,16,128]{2,1,0:T(8,128)(2,1)S(1)}, u32[]{:S(2)}, u32[]{:S(2)}) collective-permute-start(bf16[32,16,128]{2,1,0:T(8,128)(2,1)} %bitcast.31), channel_id=1, source_target_pairs={{0,16},{16,32},{32,48},{48,64},{64,80},{80,96},{96,112},{112,128},... | collective-permute-start | bytes 393224 | tf_op jit(solution)/shard_map/ppermute | solution.py:279
  2.6 3.6 %fetch.1 = (bf16[32,8,128,128]{3,2,1,0:T(8,128)(2,1)S(1)}, bf16[16,128]{1,0:T(8,128)(2,1)S(1)}) custom-call(bf16[32,8,128,128]{3,2,1,0:T(8,128)(2,1)} %bitcast.36), custom_call_target="tpu_custom_call" | custom-call | tf_op jit(solution)/shard_map/shells/fetch/pallas_call | solution.py:281
  6.2 1.5 %collective-permute-done.refs_2_ = bf16[32,16,128]{2,1,0:T(8,128)(2,1)S(1)} collective-permute-done((bf16[32,16,128]{2,1,0:T(8,128)(2,1)}, bf16[32,16,128]{2,1,0:T(8,128)(2,1)S(1)}, u32[]{:S(2)}, u32[]{:S(2)}) %collective-permute-start) | collective-permute-done | bytes 131104 | tf_op jit(solution)/shard_map/ppermute | solution.py:279
  7.7 3.7 %shell_sums.1 = (f32[32,32,128]{2,1,0:T(8,128)S(1)}, bf16[24,32,128]{2,1,0:T(8,128)(2,1)S(1)}, bf16[24,32,128]{2,1,0:T(8,128)(2,1)S(1)}, bf16[32,8,128,128]{3,2,1,0:T(8,128)(2,1)S(1)}) custom-call(s32[8,32]{1,0:T(8,128)S(1)} %bitcast.34, bf16[32,16,128]{2,1,0:T(8,128)(2,1)S(1)} %bitcast.32, ...), custom_call_target="tpu_custom_call", output_to_operand_aliasing={{3}: (3, {})} | custom-call | tf_op jit(solution)/shard_map/shells/shell_sums/pallas_call | solution.py:282
  11.5 3.7 %collective-permute-start.2 = (bf16[24,32,128]{2,1,0:T(8,128)(2,1)S(1)}, bf16[24,32,128]{2,1,0:T(8,128)(2,1)S(1)}, u32[]{:S(2)}, u32[]{:S(2)}) collective-permute-start(bf16[24,32,128]{2,1,0:T(8,128)(2,1)S(1)} %get-tuple-element.28), channel_id=1, source_target_pairs={{0,15},{1,2},{2,1},{3,4},{4,3},{5,6},{6,5},{7,8},{8,7},{9,10},{10,... | collective-permute-start | bytes 589832 | tf_op jit(solution)/shard_map/halo/ppermute | solution.py:223
  15.2 0.9 %prepare.1 = (f32[2,32,128]{2,1,0:T(8,128)S(1)}, bf16[32,128,256]{2,1,0:T(8,128)(2,1)S(1)}) custom-call(f32[2,32,1,256]{3,2,1,0:T(1,128)S(1)} %copy-done.2, s32[32,256]{1,0:T(8,128)S(1)} %copy-done.3, f32[32,128,128]{2,1,0:T(8,128)S(1)} %copy-done), custom_call_target="tpu_custom_call" | custom-call | tf_op jit(solution)/shard_map/prepare/pallas_call | solution.py:287
  16.1 3.9 %collective-permute-done.2.refs_2_ = bf16[24,32,128]{2,1,0:T(8,128)(2,1)S(1)} collective-permute-done((bf16[24,32,128]{2,1,0:T(8,128)(2,1)S(1)}, bf16[24,32,128]{2,1,0:T(8,128)(2,1)S(1)}, u32[]{:S(2)}, u32[]{:S(2)}) %collective-permute-start.2) | collective-permute-done | bytes 196640 | tf_op jit(solution)/shard_map/halo/ppermute | solution.py:223
  20.1 3.0 %collective-permute-start.3 = (bf16[8,32,128]{2,1,0:T(8,128)(2,1)S(1)}, bf16[8,32,128]{2,1,0:T(8,128)(2,1)S(1)}, u32[]{:S(2)}, u32[]{:S(2)}) collective-permute-start(bf16[8,32,128]{2,1,0:T(8,128)(2,1)S(1)} %get-tuple-element.31), channel_id=1, source_target_pairs={{0,48},{16,32},{32,16},{48,0},{64,112},{80,96},{96,80},{112,64},{1... | collective-permute-start | bytes 196616 | tf_op jit(solution)/shard_map/near/ppermute | solution.py:212
  23.2 2.7 %collective-permute-start.4 = (bf16[8,32,128]{2,1,0:T(8,128)(2,1)S(1)}, bf16[8,32,128]{2,1,0:T(8,128)(2,1)S(1)}, u32[]{:S(2)}, u32[]{:S(2)}) collective-permute-start(bf16[8,32,128]{2,1,0:T(8,128)(2,1)S(1)} %get-tuple-element.32), channel_id=1, source_target_pairs={{0,16},{16,0},{32,48},{48,32},{64,80},{80,64},{96,112},{112,96},{1... | collective-permute-start | bytes 196616 | tf_op jit(solution)/shard_map/near/ppermute | solution.py:212
  25.9 1.4 %collective-permute-start.5 = (bf16[8,32,128]{2,1,0:T(8,128)(2,1)S(1)}, bf16[8,32,128]{2,1,0:T(8,128)(2,1)S(1)}, u32[]{:S(2)}, u32[]{:S(2)}) collective-permute-start(bf16[8,32,128]{2,1,0:T(8,128)(2,1)S(1)} %get-tuple-element.33), channel_id=1, source_target_pairs={{0,32},{16,48},{32,0},{48,16},{64,96},{80,112},{96,64},{112,80},{1... | collective-permute-start | bytes 196616 | tf_op jit(solution)/shard_map/near/ppermute | solution.py:212
  27.3 1.7 %collective-permute-done.4 = bf16[8,32,128]{2,1,0:T(8,128)(2,1)S(1)} collective-permute-done((bf16[8,32,128]{2,1,0:T(8,128)(2,1)S(1)}, bf16[8,32,128]{2,1,0:T(8,128)(2,1)S(1)}, u32[]{:S(2)}, u32[]{:S(2)}) %collective-permute-start.4) | collective-permute-done | bytes 65568 | tf_op jit(solution)/shard_map/near/ppermute | solution.py:212
  29.0 1.6 %collective-permute-done.5 = bf16[8,32,128]{2,1,0:T(8,128)(2,1)S(1)} collective-permute-done((bf16[8,32,128]{2,1,0:T(8,128)(2,1)S(1)}, bf16[8,32,128]{2,1,0:T(8,128)(2,1)S(1)}, u32[]{:S(2)}, u32[]{:S(2)}) %collective-permute-start.5) | collective-permute-done | bytes 65568 | tf_op jit(solution)/shard_map/near/ppermute | solution.py:212
  30.6 5.3 %collective-permute-start.6 = (bf16[8,32,128]{2,1,0:T(8,128)(2,1)S(1)}, bf16[8,32,128]{2,1,0:T(8,128)(2,1)S(1)}, u32[]{:S(2)}, u32[]{:S(2)}) collective-permute-start(bf16[8,32,128]{2,1,0:T(8,128)(2,1)S(1)} %add_convert_fusion.refs_0_), channel_id=1, source_target_pairs={{0,128},{16,144},{32,160},{48,176},{64,192},{80,208},{96,224},{112... | collective-permute-start | bytes 196616 | tf_op jit(solution)/shard_map/far/ppermute | solution.py:212
  35.9 1.4 %collective-permute-start.7 = (bf16[8,32,128]{2,1,0:T(8,128)(2,1)S(1)}, bf16[8,32,128]{2,1,0:T(8,128)(2,1)S(1)}, u32[]{:S(2)}, u32[]{:S(2)}) collective-permute-start(bf16[8,32,128]{2,1,0:T(8,128)(2,1)S(1)} %add_convert_fusion.refs_0_), channel_id=1, source_target_pairs={{0,64},{16,80},{32,96},{48,112},{64,0},{80,16},{96,32},{112,48},{1... | collective-permute-start | bytes 196616 | tf_op jit(solution)/shard_map/far/ppermute | solution.py:212
  37.4 1.4 %collective-permute-done.6.refs_1_ = bf16[8,32,128]{2,1,0:T(8,128)(2,1)S(1)} collective-permute-done((bf16[8,32,128]{2,1,0:T(8,128)(2,1)S(1)}, bf16[8,32,128]{2,1,0:T(8,128)(2,1)S(1)}, u32[]{:S(2)}, u32[]{:S(2)}) %collective-permute-start.6) | collective-permute-done | bytes 65568 | tf_op jit(solution)/shard_map/far/ppermute | solution.py:212
  38.8 2.3 %collective-permute-done.7.refs_2_ = bf16[8,32,128]{2,1,0:T(8,128)(2,1)S(1)} collective-permute-done((bf16[8,32,128]{2,1,0:T(8,128)(2,1)S(1)}, bf16[8,32,128]{2,1,0:T(8,128)(2,1)S(1)}, u32[]{:S(2)}, u32[]{:S(2)}) %collective-permute-start.7) | collective-permute-done | bytes 65568 | tf_op jit(solution)/shard_map/far/ppermute | solution.py:212
  41.1 2.7 %collective-permute-done.8.refs_3_ = bf16[8,32,128]{2,1,0:T(8,128)(2,1)S(1)} collective-permute-done((bf16[8,32,128]{2,1,0:T(8,128)(2,1)S(1)}, bf16[8,32,128]{2,1,0:T(8,128)(2,1)S(1)}, u32[]{:S(2)}, u32[]{:S(2)}) %collective-permute-start.8) | collective-permute-done | bytes 65568 | tf_op jit(solution)/shard_map/far/ppermute | solution.py:212
  44.0 1.8 %collective-permute-start.10 = (bf16[8,32,128]{2,1,0:T(8,128)(2,1)S(1)}, bf16[8,32,128]{2,1,0:T(8,128)(2,1)S(1)}, u32[]{:S(2)}, u32[]{:S(2)}) collective-permute-start(bf16[8,32,128]{2,1,0:T(8,128)(2,1)S(1)} %far_sum.1.refs_1_.refs_0_), channel_id=1, source_target_pairs={{0,32},{16,48},{32,0},{48,16},{64,96},{80,112},{96,64},{112,80},{1... | collective-permute-start | bytes 196616 | tf_op jit(solution)/shard_map/gather/ppermute | solution.py:212
  45.8 1.3 %collective-permute-start.11 = (bf16[8,32,128]{2,1,0:T(8,128)(2,1)S(1)}, bf16[8,32,128]{2,1,0:T(8,128)(2,1)S(1)}, u32[]{:S(2)}, u32[]{:S(2)}) collective-permute-start(bf16[8,32,128]{2,1,0:T(8,128)(2,1)S(1)} %far_sum.1.refs_1_.refs_0_), channel_id=1, source_target_pairs={{0,48},{16,32},{32,16},{48,0},{64,112},{80,96},{96,80},{112,64},{1... | collective-permute-start | bytes 196616 | tf_op jit(solution)/shard_map/gather/ppermute | solution.py:212
  47.1 1.9 %collective-permute-start.9 = (bf16[8,32,128]{2,1,0:T(8,128)(2,1)S(1)}, bf16[8,32,128]{2,1,0:T(8,128)(2,1)S(1)}, u32[]{:S(2)}, u32[]{:S(2)}) collective-permute-start(bf16[8,32,128]{2,1,0:T(8,128)(2,1)S(1)} %far_sum.1.refs_1_.refs_0_), channel_id=1, source_target_pairs={{0,16},{16,0},{32,48},{48,32},{64,80},{80,64},{96,112},{112,96},{1... | collective-permute-start | bytes 196616 | tf_op jit(solution)/shard_map/gather/ppermute | solution.py:212
  49.0 3.4 %collective-permute-done.11.refs_4_.refs_3_ = bf16[8,32,128]{2,1,0:T(8,128)(2,1)S(1)} collective-permute-done((bf16[8,32,128]{2,1,0:T(8,128)(2,1)S(1)}, bf16[8,32,128]{2,1,0:T(8,128)(2,1)S(1)}, u32[]{:S(2)}, u32[]{:S(2)}) %collective-permute-start.11) | collective-permute-done | bytes 65568 | tf_op jit(solution)/shard_map/gather/ppermute | solution.py:212
  52.5 0.7 collective-permute-done.9.refs_2_.refs_1_
  53.2 0.8 %first_step.1 = (bf16[32,16,128]{2,1,0:T(8,128)(2,1)S(1)}, f32[32,16,128]{2,1,0:T(8,128)S(1)}, bf16[24,16,128]{2,1,0:T(8,128)(2,1)S(1)}, bf16[24,16,128]{2,1,0:T(8,128)(2,1)S(1)}) custom-call(s32[8,32]{1,0:T(8,128)S(1)} %bitcast.35, bf16[8,32,128]{2,1,0:T(8,128)(2,1)S(1)} %far_sum.1.refs_1_.refs_0_, ...), custom_call_target="tpu_custom_call" | custom-call | tf_op jit(solution)/shard_map/first_step/pallas_call | solution.py:297
  54.1 3.1 %collective-permute-start.13 = (bf16[24,16,128]{2,1,0:T(8,128)(2,1)S(1)}, bf16[24,16,128]{2,1,0:T(8,128)(2,1)S(1)}, u32[]{:S(2)}, u32[]{:S(2)}) collective-permute-start(bf16[24,16,128]{2,1,0:T(8,128)(2,1)S(1)} %get-tuple-element.42), channel_id=1, source_target_pairs={{0,15},{1,2},{2,1},{3,4},{4,3},{5,6},{6,5},{7,8},{8,7},{9,10},{10,... | collective-permute-start | bytes 294920 | tf_op jit(solution)/shard_map/halo_extra/ppermute | solution.py:223
  57.9 3.3 %collective-permute-done.13.refs_2_ = bf16[24,16,128]{2,1,0:T(8,128)(2,1)S(1)} collective-permute-done((bf16[24,16,128]{2,1,0:T(8,128)(2,1)S(1)}, bf16[24,16,128]{2,1,0:T(8,128)(2,1)S(1)}, u32[]{:S(2)}, u32[]{:S(2)}) %collective-permute-start.13) | collective-permute-done | bytes 98336 | tf_op jit(solution)/shard_map/halo_extra/ppermute | solution.py:223
  61.1 0.7 collective-permute-start.14
  61.8 0.7 collective-permute-start.15
  62.5 0.7 collective-permute-start.16
  63.2 0.7 collective-permute-start.17
  64.6 1.3 %collective-permute-start.19 = (bf16[32,128]{1,0:T(8,128)(2,1)S(1)}, bf16[32,128]{1,0:T(8,128)(2,1)S(1)}, u32[]{:S(2)}, u32[]{:S(2)}) collective-permute-start(bf16[32,128]{1,0:T(8,128)(2,1)S(1)} %get-tuple-element.51), channel_id=1, source_target_pairs={{0,16},{64,80},{128,144},{192,208},{1,17},{65,81},{129,145},{193,2... | collective-permute-start | bytes 24584 | tf_op jit(solution)/shard_map/spread/ppermute | solution.py:314
  65.9 0.7 select_bitcast_fusion
  66.6 10.1 %collective-permute-done.19 = bf16[32,128]{1,0:T(8,128)(2,1)S(1)} collective-permute-done((bf16[32,128]{1,0:T(8,128)(2,1)S(1)}, bf16[32,128]{1,0:T(8,128)(2,1)S(1)}, u32[]{:S(2)}, u32[]{:S(2)}) %collective-permute-start.19) | collective-permute-done | bytes 8224 | tf_op jit(solution)/shard_map/spread/ppermute | solution.py:314
  (36 shorter events, 2.9 us)
Async XLA Ops:
  0.6 7.1 %copy-start.1 = (bf16[1,32,16,128]{3,2,1,0:T(8,128)(2,1)S(1)}, bf16[1,32,16,128]{3,2,1,0:T(8,128)(2,1)}, u32[]{:S(2)}) copy-start(bf16[1,32,16,128]{3,2,1,0:T(8,128)(2,1)} %param.8) | copy-start | bytes 393220
  0.6 7.0 %copy-start.4 = (s32[1,32,8]{1,2,0:T(8,128)S(1)}, s32[1,32,8]{1,2,0:T(8,128)}, u32[]{:S(2)}) copy-start(s32[1,32,8]{1,2,0:T(8,128)} %param.7) | copy-start | bytes 3076
  0.7 7.0 %collective-permute-start = (bf16[32,16,128]{2,1,0:T(8,128)(2,1)}, bf16[32,16,128]{2,1,0:T(8,128)(2,1)S(1)}, u32[]{:S(2)}, u32[]{:S(2)}) collective-permute-start(bf16[32,16,128]{2,1,0:T(8,128)(2,1)} %bitcast.31), channel_id=1, source_target_pairs={{0,16},{16,32},{32,48},{48,64},{64,80},{80,96},{96,112},{112,128},... | collective-permute-start | bytes 393224 | tf_op jit(solution)/shard_map/ppermute | solution.py:279
  2.6 12.6 %copy-start = (f32[32,128,128]{2,1,0:T(8,128)S(1)}, f32[32,128,128]{2,1,0:T(8,128)}, u32[]{:S(2)}) copy-start(f32[32,128,128]{2,1,0:T(8,128)} %inverse.1) | copy-start | bytes 6291460
  2.6 12.6 %copy-start.2 = (f32[2,32,1,256]{3,2,1,0:T(1,128)S(1)}, f32[2,32,1,256]{3,2,1,0:T(1,128)}, u32[]{:S(2)}) copy-start(f32[2,32,1,256]{3,2,1,0:T(1,128)} %incident.1) | copy-start | bytes 196612
  2.6 12.6 %copy-start.3 = (s32[32,256]{1,0:T(8,128)S(1)}, s32[32,256]{1,0:T(8,128)}, u32[]{:S(2)}) copy-start(s32[32,256]{1,0:T(8,128)} %element_map.1) | copy-start | bytes 98308
  11.4 4.7 %collective-permute-start.1 = (bf16[24,32,128]{2,1,0:T(8,128)(2,1)S(1)}, bf16[24,32,128]{2,1,0:T(8,128)(2,1)S(1)}, u32[]{:S(2)}, u32[]{:S(2)}) collective-permute-start(bf16[24,32,128]{2,1,0:T(8,128)(2,1)S(1)} %get-tuple-element.27), channel_id=1, source_target_pairs={{0,1},{1,0},{2,3},{3,2},{4,5},{5,4},{6,7},{7,6},{8,9},{9,8},{10,11... | collective-permute-start | bytes 589832 | tf_op jit(solution)/shard_map/halo/ppermute | solution.py:224
  11.5 8.5 %collective-permute-start.2 = (bf16[24,32,128]{2,1,0:T(8,128)(2,1)S(1)}, bf16[24,32,128]{2,1,0:T(8,128)(2,1)S(1)}, u32[]{:S(2)}, u32[]{:S(2)}) collective-permute-start(bf16[24,32,128]{2,1,0:T(8,128)(2,1)S(1)} %get-tuple-element.28), channel_id=1, source_target_pairs={{0,15},{1,2},{2,1},{3,4},{4,3},{5,6},{6,5},{7,8},{8,7},{9,10},{10,... | collective-permute-start | bytes 589832 | tf_op jit(solution)/shard_map/halo/ppermute | solution.py:223
  20.1 7.1 %collective-permute-start.3 = (bf16[8,32,128]{2,1,0:T(8,128)(2,1)S(1)}, bf16[8,32,128]{2,1,0:T(8,128)(2,1)S(1)}, u32[]{:S(2)}, u32[]{:S(2)}) collective-permute-start(bf16[8,32,128]{2,1,0:T(8,128)(2,1)S(1)} %get-tuple-element.31), channel_id=1, source_target_pairs={{0,48},{16,32},{32,16},{48,0},{64,112},{80,96},{96,80},{112,64},{1... | collective-permute-start | bytes 196616 | tf_op jit(solution)/shard_map/near/ppermute | solution.py:212
  23.2 5.8 %collective-permute-start.4 = (bf16[8,32,128]{2,1,0:T(8,128)(2,1)S(1)}, bf16[8,32,128]{2,1,0:T(8,128)(2,1)S(1)}, u32[]{:S(2)}, u32[]{:S(2)}) collective-permute-start(bf16[8,32,128]{2,1,0:T(8,128)(2,1)S(1)} %get-tuple-element.32), channel_id=1, source_target_pairs={{0,16},{16,0},{32,48},{48,32},{64,80},{80,64},{96,112},{112,96},{1... | collective-permute-start | bytes 196616 | tf_op jit(solution)/shard_map/near/ppermute | solution.py:212
  25.9 4.6 %collective-permute-start.5 = (bf16[8,32,128]{2,1,0:T(8,128)(2,1)S(1)}, bf16[8,32,128]{2,1,0:T(8,128)(2,1)S(1)}, u32[]{:S(2)}, u32[]{:S(2)}) collective-permute-start(bf16[8,32,128]{2,1,0:T(8,128)(2,1)S(1)} %get-tuple-element.33), channel_id=1, source_target_pairs={{0,32},{16,48},{32,0},{48,16},{64,96},{80,112},{96,64},{112,80},{1... | collective-permute-start | bytes 196616 | tf_op jit(solution)/shard_map/near/ppermute | solution.py:212
  30.6 8.3 %collective-permute-start.6 = (bf16[8,32,128]{2,1,0:T(8,128)(2,1)S(1)}, bf16[8,32,128]{2,1,0:T(8,128)(2,1)S(1)}, u32[]{:S(2)}, u32[]{:S(2)}) collective-permute-start(bf16[8,32,128]{2,1,0:T(8,128)(2,1)S(1)} %add_convert_fusion.refs_0_), channel_id=1, source_target_pairs={{0,128},{16,144},{32,160},{48,176},{64,192},{80,208},{96,224},{112... | collective-permute-start | bytes 196616 | tf_op jit(solution)/shard_map/far/ppermute | solution.py:212
  35.9 5.2 %collective-permute-start.7 = (bf16[8,32,128]{2,1,0:T(8,128)(2,1)S(1)}, bf16[8,32,128]{2,1,0:T(8,128)(2,1)S(1)}, u32[]{:S(2)}, u32[]{:S(2)}) collective-permute-start(bf16[8,32,128]{2,1,0:T(8,128)(2,1)S(1)} %add_convert_fusion.refs_0_), channel_id=1, source_target_pairs={{0,64},{16,80},{32,96},{48,112},{64,0},{80,16},{96,32},{112,48},{1... | collective-permute-start | bytes 196616 | tf_op jit(solution)/shard_map/far/ppermute | solution.py:212
  37.3 6.5 %collective-permute-start.8 = (bf16[8,32,128]{2,1,0:T(8,128)(2,1)S(1)}, bf16[8,32,128]{2,1,0:T(8,128)(2,1)S(1)}, u32[]{:S(2)}, u32[]{:S(2)}) collective-permute-start(bf16[8,32,128]{2,1,0:T(8,128)(2,1)S(1)} %add_convert_fusion.refs_0_), channel_id=1, source_target_pairs={{0,192},{16,208},{32,224},{48,240},{64,128},{80,144},{96,160},{112... | collective-permute-start | bytes 196616 | tf_op jit(solution)/shard_map/far/ppermute | solution.py:212
  44.0 5.0 %collective-permute-start.10 = (bf16[8,32,128]{2,1,0:T(8,128)(2,1)S(1)}, bf16[8,32,128]{2,1,0:T(8,128)(2,1)S(1)}, u32[]{:S(2)}, u32[]{:S(2)}) collective-permute-start(bf16[8,32,128]{2,1,0:T(8,128)(2,1)S(1)} %far_sum.1.refs_1_.refs_0_), channel_id=1, source_target_pairs={{0,32},{16,48},{32,0},{48,16},{64,96},{80,112},{96,64},{112,80},{1... | collective-permute-start | bytes 196616 | tf_op jit(solution)/shard_map/gather/ppermute | solution.py:212
  45.8 6.7 %collective-permute-start.11 = (bf16[8,32,128]{2,1,0:T(8,128)(2,1)S(1)}, bf16[8,32,128]{2,1,0:T(8,128)(2,1)S(1)}, u32[]{:S(2)}, u32[]{:S(2)}) collective-permute-start(bf16[8,32,128]{2,1,0:T(8,128)(2,1)S(1)} %far_sum.1.refs_1_.refs_0_), channel_id=1, source_target_pairs={{0,48},{16,32},{32,16},{48,0},{64,112},{80,96},{96,80},{112,64},{1... | collective-permute-start | bytes 196616 | tf_op jit(solution)/shard_map/gather/ppermute | solution.py:212
  47.1 6.0 %collective-permute-start.9 = (bf16[8,32,128]{2,1,0:T(8,128)(2,1)S(1)}, bf16[8,32,128]{2,1,0:T(8,128)(2,1)S(1)}, u32[]{:S(2)}, u32[]{:S(2)}) collective-permute-start(bf16[8,32,128]{2,1,0:T(8,128)(2,1)S(1)} %far_sum.1.refs_1_.refs_0_), channel_id=1, source_target_pairs={{0,16},{16,0},{32,48},{48,32},{64,80},{80,64},{96,112},{112,96},{1... | collective-permute-start | bytes 196616 | tf_op jit(solution)/shard_map/gather/ppermute | solution.py:212
  54.0 3.9 %collective-permute-start.12 = (bf16[24,16,128]{2,1,0:T(8,128)(2,1)S(1)}, bf16[24,16,128]{2,1,0:T(8,128)(2,1)S(1)}, u32[]{:S(2)}, u32[]{:S(2)}) collective-permute-start(bf16[24,16,128]{2,1,0:T(8,128)(2,1)S(1)} %get-tuple-element.41), channel_id=1, source_target_pairs={{0,1},{1,0},{2,3},{3,2},{4,5},{5,4},{6,7},{7,6},{8,9},{9,8},{10,11... | collective-permute-start | bytes 294920 | tf_op jit(solution)/shard_map/halo_extra/ppermute | solution.py:224
  54.1 7.1 %collective-permute-start.13 = (bf16[24,16,128]{2,1,0:T(8,128)(2,1)S(1)}, bf16[24,16,128]{2,1,0:T(8,128)(2,1)S(1)}, u32[]{:S(2)}, u32[]{:S(2)}) collective-permute-start(bf16[24,16,128]{2,1,0:T(8,128)(2,1)S(1)} %get-tuple-element.42), channel_id=1, source_target_pairs={{0,15},{1,2},{2,1},{3,4},{4,3},{5,6},{6,5},{7,8},{8,7},{9,10},{10,... | collective-permute-start | bytes 294920 | tf_op jit(solution)/shard_map/halo_extra/ppermute | solution.py:223
  57.2 8.7 %collective-permute-start.20 = (bf16[32,16,128]{2,1,0:T(8,128)(2,1)S(1)}, bf16[32,16,128]{2,1,0:T(8,128)(2,1)S(1)}, u32[]{:S(2)}, u32[]{:S(2)}) collective-permute-start(bf16[32,16,128]{2,1,0:T(8,128)(2,1)S(1)} %bitcast.33), channel_id=1, source_target_pairs={{0,32},{16,48},{32,64},{48,80},{64,96},{80,112},{96,128},{112,144}... | collective-permute-start | bytes 393224 | tf_op jit(solution)/shard_map/ppermute | solution.py:301
  61.1 2.0 %collective-permute-start.14 = (bf16[4,32,128]{2,1,0:T(8,128)(2,1)S(1)}, bf16[4,32,128]{2,1,0:T(8,128)(2,1)S(1)}, u32[]{:S(2)}, u32[]{:S(2)}) collective-permute-start(bf16[4,32,128]{2,1,0:T(8,128)(2,1)S(1)} %get-tuple-element.50), channel_id=1, source_target_pairs={{0,192},{1,193},{2,194},{3,195},{4,196},{5,197},{6,198},{7,199},{8... | collective-permute-start | bytes 98312 | tf_op jit(solution)/shard_map/spread/ppermute | solution.py:309
  61.8 1.4 %collective-permute-start.15 = (bf16[4,32,128]{2,1,0:T(8,128)(2,1)S(1)}, bf16[4,32,128]{2,1,0:T(8,128)(2,1)S(1)}, u32[]{:S(2)}, u32[]{:S(2)}) collective-permute-start(bf16[4,32,128]{2,1,0:T(8,128)(2,1)S(1)} %get-tuple-element.49), channel_id=1, source_target_pairs={{0,128},{1,129},{2,130},{3,131},{4,132},{5,133},{6,134},{7,135},{8... | collective-permute-start | bytes 98312 | tf_op jit(solution)/shard_map/spread/ppermute | solution.py:309
  62.5 0.7 collective-permute-start.16
  63.2 3.3 %collective-permute-start.17 = (bf16[32,128]{1,0:T(8,128)(2,1)S(1)}, bf16[32,128]{1,0:T(8,128)(2,1)S(1)}, u32[]{:S(2)}, u32[]{:S(2)}) collective-permute-start(bf16[32,128]{1,0:T(8,128)(2,1)S(1)} %get-tuple-element.53), channel_id=1, source_target_pairs={{0,48},{64,112},{128,176},{192,240},{1,49},{65,113},{129,177},{193... | collective-permute-start | bytes 24584 | tf_op jit(solution)/shard_map/spread/ppermute | solution.py:314
  63.9 2.7 %collective-permute-start.18 = (bf16[32,128]{1,0:T(8,128)(2,1)S(1)}, bf16[32,128]{1,0:T(8,128)(2,1)S(1)}, u32[]{:S(2)}, u32[]{:S(2)}) collective-permute-start(bf16[32,128]{1,0:T(8,128)(2,1)S(1)} %get-tuple-element.52), channel_id=1, source_target_pairs={{0,32},{64,96},{128,160},{192,224},{1,33},{65,97},{129,161},{193,2... | collective-permute-start | bytes 24584 | tf_op jit(solution)/shard_map/spread/ppermute | solution.py:314
  64.6 12.1 %collective-permute-start.19 = (bf16[32,128]{1,0:T(8,128)(2,1)S(1)}, bf16[32,128]{1,0:T(8,128)(2,1)S(1)}, u32[]{:S(2)}, u32[]{:S(2)}) collective-permute-start(bf16[32,128]{1,0:T(8,128)(2,1)S(1)} %get-tuple-element.51), channel_id=1, source_target_pairs={{0,16},{64,80},{128,144},{192,208},{1,17},{65,81},{129,145},{193,2... | collective-permute-start | bytes 24584 | tf_op jit(solution)/shard_map/spread/ppermute | solution.py:314
